TPU v7x, 512 devices: a whole 4x8x8 slice. The times are simulated.
512 devices in a mesh: seq: 128 (over y, x, z_hi, core), dp: 4 (over z_lo).
Axes of the slice: x: 4, y: 8, z: 8 (z_hi: 2, z_lo: 4; z = z_hi * 4 + z_lo), core: 2. Of those that a mesh axis runs over, the one named last changes fastest.
Arguments:
- teacher_video: bfloat16 [4, 3, 16384, 1536], P('dp', None, 'seq'), may hold values from -150 to 150
- student_video: bfloat16 [4, 3, 16384, 1536], P('dp', None, 'seq'), may hold values from -150 to 150
- teacher_audio: bfloat16 [4, 2, 4096, 1536], P('dp', None, 'seq'), may hold values from -5 to 5
- student_audio: bfloat16 [4, 2, 4096, 1536], P('dp', None, 'seq'), may hold values from -5 to 5
- alignment: int32 [4, 128, 2], P('dp', 'seq'), may hold values from 0 to 127, as said below
- guidance_index: int32 [4], P('dp'), may hold values from 0 to 7
- step_index: int32 [4], P('dp'), may hold values from 0 to 999
- null_flag: int32 [4], P('dp'), may hold values from 0 to 1, as said below
- gamma: float32 [8, 12], replicated, may hold values from -0.5 to 0.5
Outputs:
- grad_video: bfloat16 [4, 3, 16384, 1536], P('dp', None, 'seq')
- grad_audio: bfloat16 [4, 2, 4096, 1536], P('dp', None, 'seq')
- gamma_grad: float32 [8, 12], replicated
Inputs may be any that keep to these rules, and one draw needn't show every extreme that they name: For video block i, alignment[b, i] holds the first audio block s and the number c >= 1 of consecutive audio blocks that intersect it in time; blocks s to s + c - 1 lie inside the clip and within 3 blocks of audio block i. `null_flag`: at least one clip is dropped and at least one is kept.
All inputs are finite; a program needn't handle non-finite values.
Results may differ from a plain program's by a relative error of at most 0.013.
Values may be sent and summed in bfloat16 or wider, within the bound.
No kernel may reach another device: no remote copies, remote signals or barrier semaphores. Data moves between devices by JAX's collectives and lax.ppermute only.
A program may use at most 64 MiB of HBM per device.

v0:
```python
import functools

import jax
import jax.numpy as jnp
from jax import lax
from jax.sharding import Mesh
from jax.sharding import PartitionSpec as P

VB = 128
REACH = 3
SEQ = ("seq_0", "seq_1", "seq_2", "seq_3")
SEQ_DP = ("seq_0", "seq_1", "seq_2", "seq_3", "dp")


def from_behind(x, axis, by):
    peers = lax.axis_size(axis)
    pairs = [(i, i + by) for i in range(peers) if 0 <= i + by < peers]
    return lax.ppermute(x, axis, pairs)


def one_axis_at_a_time(x, axes):
    return functools.reduce(lax.psum, axes, x)


def joint_probs(scores, usable):
    masked = jnp.where(usable, scores, -jnp.inf)
    highest = jnp.max(masked, axis=-1, keepdims=True)
    exponent = jnp.exp(masked - highest)
    return exponent / jnp.sum(exponent, axis=-1, keepdims=True)


def body(
    teacher_video,
    student_video,
    teacher_audio,
    student_audio,
    alignment,
    guidance_index,
    step_index,
    null_flag,
    gamma,
):
    reach_blocks = REACH
    head_count = gamma.shape[1]
    feature_width = teacher_video.shape[-1]
    head_dim = feature_width // head_count
    tokens = teacher_video.shape[2]
    audio_tokens = teacher_audio.shape[2]
    blocks = tokens // VB
    window = (2 * reach_blocks + 1) * audio_tokens
    score_scale = head_dim ** (-0.5)
    position = lax.axis_index(SEQ)
    level_index = guidance_index[0]
    weight = 1.0 + 0.75 * level_index.astype(jnp.float32)
    loss_weight = 1.0 / (1.0 + step_index[0].astype(jnp.float32) / 250.0)
    keep_audio = null_flag[0] == 0
    levels = jnp.arange(gamma.shape[0], dtype=jnp.int32)
    factor = jnp.sum(
        jnp.where(levels[:, None] == level_index, gamma, jnp.zeros_like(gamma)), axis=0
    )
    own_audio = (teacher_audio[0], student_audio[0])
    above = []
    carried = own_audio
    for hop in range(reach_blocks):
        carried = from_behind((carried[0], carried[1]), SEQ, -1)
        above.append(carried)
    below = []
    carried = own_audio
    for hop in range(reach_blocks):
        carried = from_behind((carried[0], carried[1]), SEQ, 1)
        below.append(carried)
    pieces = below[::-1] + [own_audio] + above
    teach_window = jnp.concatenate([piece[0] for piece in pieces], axis=1).reshape(
        2, window, head_count, head_dim
    )
    pupil_window = jnp.concatenate([piece[1] for piece in pieces], axis=1).reshape(
        2, window, head_count, head_dim
    )
    owners = position - reach_blocks + jnp.arange(window, dtype=jnp.int32) // audio_tokens
    teach_vid = teacher_video[0].reshape(3, blocks, VB, head_count, head_dim)
    pupil_vid = student_video[0].reshape(3, blocks, VB, head_count, head_dim)
    audio_sums = jnp.zeros((2, window, feature_width), jnp.float32)
    first_block = alignment[0, 0, 0]
    block_count = alignment[0, 0, 1]
    audio_ok = (owners >= first_block) & (owners < first_block + block_count) & keep_audio
    usable = jnp.concatenate([jnp.ones((VB,), bool), audio_ok])[None, None, :]
    teach_keys = jnp.concatenate([teach_vid[1, 0], teach_window[0]], axis=0)
    teach_values = jnp.concatenate([teach_vid[2, 0], teach_window[1]], axis=0)
    teach_scores = (
        jnp.einsum("qhe,khe->hqk", teach_vid[0, 0], teach_keys, preferred_element_type=jnp.float32)
        * score_scale
    )
    cond_probs = joint_probs(teach_scores, usable).astype(jnp.bfloat16)
    conditional = jnp.einsum(
        "hqk,khe->qhe", cond_probs, teach_values, preferred_element_type=jnp.float32
    )
    plain_probs = joint_probs(teach_scores[..., :VB], jnp.ones((1, 1, VB), bool)).astype(
        jnp.bfloat16
    )
    unconditional = jnp.einsum(
        "hqk,khe->qhe", plain_probs, teach_vid[2, 0], preferred_element_type=jnp.float32
    )
    target = unconditional + weight * (conditional - unconditional)
    pupil_query = pupil_vid[0, 0]
    pupil_keys = jnp.concatenate([pupil_vid[1, 0], pupil_window[0]], axis=0)
    pupil_values = jnp.concatenate([pupil_vid[2, 0], pupil_window[1]], axis=0)
    pupil_scores = (
        jnp.einsum("qhe,khe->hqk", pupil_query, pupil_keys, preferred_element_type=jnp.float32)
        * score_scale
    )
    probs = joint_probs(pupil_scores, usable)
    probs_round = probs.astype(jnp.bfloat16)
    student_out = jnp.einsum(
        "hqk,khe->qhe", probs_round, pupil_values, preferred_element_type=jnp.float32
    )
    residual = loss_weight * (student_out * factor[None, :, None] - target)
    head_totals = jnp.sum(residual * student_out, axis=(0, 2))
    out_grad = (residual * factor[None, :, None]).astype(jnp.bfloat16)
    prob_grad = jnp.einsum(
        "qhe,khe->hqk", out_grad, pupil_values, preferred_element_type=jnp.float32
    )
    row_delta = jnp.sum(out_grad.astype(jnp.float32) * student_out, axis=-1)
    score_grad = (score_scale * probs * (prob_grad - jnp.transpose(row_delta)[:, :, None])).astype(
        jnp.bfloat16
    )
    query_grad = jnp.einsum(
        "hqk,khe->qhe", score_grad, pupil_keys, preferred_element_type=jnp.float32
    )
    key_grad = jnp.einsum(
        "hqk,qhe->khe", score_grad, pupil_query, preferred_element_type=jnp.float32
    )
    value_grad = jnp.einsum(
        "hqk,qhe->khe", probs_round, out_grad, preferred_element_type=jnp.float32
    )
    video_blocks = [
        jnp.stack([query_grad, key_grad[:VB], value_grad[:VB]])
        .reshape(3, VB, feature_width)
        .astype(jnp.bfloat16)
    ]
    audio_sums = jnp.stack([key_grad[VB:], value_grad[VB:]]).reshape(2, window, feature_width)

    def slot_piece(offset):
        begin = (offset + reach_blocks) * audio_tokens
        return audio_sums[:, begin : begin + audio_tokens]

    own_total = slot_piece(0)
    collected = jnp.zeros_like(own_total)
    for offset in range(reach_blocks, 0, -1):
        collected = from_behind(collected + slot_piece(offset), SEQ, 1)
    gathered_low = jnp.zeros_like(own_total)
    for offset in range(-reach_blocks, 0):
        gathered_low = from_behind(gathered_low + slot_piece(offset), SEQ, -1)
    own_total = own_total + collected + gathered_low
    grad_audio = own_total.astype(jnp.bfloat16)[None]
    grad_video = jnp.stack(video_blocks, axis=1).reshape(3, tokens, feature_width)[None]
    total_tokens = tokens * lax.axis_size(SEQ)
    contribution = jnp.where(
        levels[:, None] == level_index, head_totals[None, :], jnp.zeros_like(gamma)
    ) / (total_tokens * head_dim)
    gamma_grad = one_axis_at_a_time(contribution, SEQ_DP)
    return (grad_video, grad_audio, gamma_grad)


def solution(mesh):
    finer = Mesh(
        mesh.devices.reshape(8, 4, 2, 2, mesh.shape["dp"]),
        ("seq_0", "seq_1", "seq_2", "seq_3", "dp"),
    )
    in_specs = (
        P("dp", None, SEQ, None),
        P("dp", None, SEQ, None),
        P("dp", None, SEQ, None),
        P("dp", None, SEQ, None),
        P("dp", SEQ, None),
        P("dp"),
        P("dp"),
        P("dp"),
        P(),
    )
    out_specs = (P("dp", None, SEQ, None), P("dp", None, SEQ, None), P())
    return jax.shard_map(body, mesh=finer, in_specs=in_specs, out_specs=out_specs, check_vma=False)
```

profile of v0, /device:TPU:1, one launch (start us, length us, event | category | flops | bytes accessed | tf_op | source)
XLA Modules:
  0.0 276.6 jit_solution(2017430031336949469)
XLA Ops:
  0.6 8.9 %collective-permute-start.9 = (bf16[2,32,1536]{2,1,0:T(8,128)(2,1)}, bf16[2,32,1536]{2,1,0:T(8,128)(2,1)S(1)}, u32[]{:S(2)}, u32[]{:S(2)}) collective-permute-start(bf16[2,32,1536]{2,1,0:T(8,128)(2,1)} %bitcast.107), channel_id=1, source_target_pairs={{4,0},{8,4},{12,8},{16,12},{20,16},{24,20},{28,24},{32,28},{36,32}... | collective-permute-start | bytes 589832 | tf_op jit(solution)/shard_map/ppermute | solution.py:18
  9.6 5.2 %collective-permute-start.6 = (bf16[2,32,1536]{2,1,0:T(8,128)(2,1)}, bf16[2,32,1536]{2,1,0:T(8,128)(2,1)S(1)}, u32[]{:S(2)}, u32[]{:S(2)}) collective-permute-start(bf16[2,32,1536]{2,1,0:T(8,128)(2,1)} %bitcast.108), channel_id=1, source_target_pairs={{0,4},{4,8},{8,12},{12,16},{16,20},{20,24},{24,28},{28,32},{32,36}... | collective-permute-start | bytes 589832 | tf_op jit(solution)/shard_map/ppermute | solution.py:18
  14.7 1.9 collective-permute-start.3
  16.7 7.6 %collective-permute-start = (bf16[2,32,1536]{2,1,0:T(8,128)(2,1)}, bf16[2,32,1536]{2,1,0:T(8,128)(2,1)}, u32[]{:S(2)}, u32[]{:S(2)}) collective-permute-start(bf16[2,32,1536]{2,1,0:T(8,128)(2,1)} %bitcast.106), channel_id=1, source_target_pairs={{0,4},{4,8},{8,12},{12,16},{16,20},{20,24},{24,28},{28,32},{32,36}... | collective-permute-start | bytes 589832 | tf_op jit(solution)/shard_map/ppermute | solution.py:18
  24.2 1.3 fusion.85
  27.9 0.9 copy.102
  29.0 0.9 copy.109
  29.9 0.9 copy.131
  31.1 0.9 copy.92
  32.5 1.0 copy.98
  33.5 3.5 %collective-permute-start.1 = (bf16[2,32,1536]{2,1,0:T(8,128)(2,1)}, bf16[2,32,1536]{2,1,0:T(8,128)(2,1)S(1)}, u32[]{:S(2)}, u32[]{:S(2)}) collective-permute-start(bf16[2,32,1536]{2,1,0:T(8,128)(2,1)} %collective-permute-done), channel_id=1, source_target_pairs={{0,4},{4,8},{8,12},{12,16},{16,20},{20,24},{24,28},{28,32},{32,36}... | collective-permute-start | bytes 589832 | tf_op jit(solution)/shard_map/ppermute | solution.py:18
  37.0 0.6 fusion.86
  38.9 0.7 and_and_fusion
  39.6 1.9 collective-permute-start.10
  41.5 7.5 %collective-permute-start.7 = (bf16[2,32,1536]{2,1,0:T(8,128)(2,1)S(1)}, bf16[2,32,1536]{2,1,0:T(8,128)(2,1)S(1)}, u32[]{:S(2)}, u32[]{:S(2)}) collective-permute-start(bf16[2,32,1536]{2,1,0:T(8,128)(2,1)S(1)} %collective-permute-done.6), channel_id=1, source_target_pairs={{0,4},{4,8},{8,12},{12,16},{16,20},{20,24},{24,28},{28,32},{32,36}... | collective-permute-start | bytes 589832 | tf_op jit(solution)/shard_map/ppermute | solution.py:18
  49.1 1.9 collective-permute-start.4
  51.0 7.5 %collective-permute-start.2 = (bf16[2,32,1536]{2,1,0:T(8,128)(2,1)S(1)}, bf16[2,32,1536]{2,1,0:T(8,128)(2,1)S(1)}, u32[]{:S(2)}, u32[]{:S(2)}) collective-permute-start(bf16[2,32,1536]{2,1,0:T(8,128)(2,1)S(1)} %collective-permute-done.1), channel_id=1, source_target_pairs={{0,4},{4,8},{8,12},{12,16},{16,20},{20,24},{24,28},{28,32},{32,36}... | collective-permute-start | bytes 589832 | tf_op jit(solution)/shard_map/ppermute | solution.py:18
  58.7 1.9 collective-permute-start.11
  60.6 7.6 %collective-permute-start.8 = (bf16[2,32,1536]{2,1,0:T(8,128)(2,1)S(1)}, bf16[2,32,1536]{2,1,0:T(8,128)(2,1)}, u32[]{:S(2)}, u32[]{:S(2)}) collective-permute-start(bf16[2,32,1536]{2,1,0:T(8,128)(2,1)S(1)} %collective-permute-done.7), channel_id=1, source_target_pairs={{0,4},{4,8},{8,12},{12,16},{16,20},{20,24},{24,28},{28,32},{32,36}... | collective-permute-start | bytes 589832 | tf_op jit(solution)/shard_map/ppermute | solution.py:18
  68.2 2.1 collective-permute-start.5
  70.4 0.9 constant_dynamic-update-slice_fusion.4
  71.3 0.9 constant_dynamic-update-slice_fusion.2
  72.3 8.5 %collective-permute-done.5 = bf16[2,32,1536]{2,1,0:T(8,128)(2,1)S(1)} collective-permute-done((bf16[2,32,1536]{2,1,0:T(8,128)(2,1)S(1)}, bf16[2,32,1536]{2,1,0:T(8,128)(2,1)S(1)}, u32[]{:S(2)}, u32[]{:S(2)}) %collective-permute-start.5) | collective-permute-done | bytes 196640 | tf_op jit(solution)/shard_map/ppermute | solution.py:18
  81.8 1.1 copy.99
  82.9 0.9 constant_dynamic-update-slice_fusion.13
  84.4 1.1 copy.110
  86.7 1.8 multiply_bitcast_fusion
  88.5 0.8 fusion.88
  89.3 1.3 fusion.87
  90.6 2.4 convolution_bitcast_fusion.2
  93.5 0.7 fusion.91
  94.7 1.5 convolution_bitcast_fusion.4
  96.1 3.7 %multiply_reduce_fusion = (f32[12]{0:T(128)S(1)}, f32[128,12]{0,1:T(8,128)S(1)}, bf16[128,12,128]{0,2,1:T(8,128)(2,1)}) fusion(f32[128,12,128]{0,2,1:T(8,128)} %convolution_bitcast_fusion.4, f32[12]{0:T(128)S(1)} %select_reduce_fusion.1, f32[128,12,128]{0,2,1:T(8,128)} %convolution_bitcast_fusion.2, f32[12,128]{1,0:T(8,128)S(1)} %fusion.88, ...), kind=kOutput, calls=%fused_computation.57 | convolution fusion | flops 286409056 | bytes 4534728 | tf_op jit(solution)/shard_map/hqk,khe->qhe/dot_general | solution.py:94
  99.8 2.3 convolution_bitcast_fusion
  102.4 1.6 multiply_convert_fusion
  105.0 1.7 convolution_bitcast_fusion.1
  106.7 1.3 copy-done
  108.1 1.7 copy.116
  109.7 1.9 copy.118
  111.6 4.9 %collective-permute-start.12 = (f32[2,32,1536]{2,1,0:T(8,128)S(1)}, f32[2,32,1536]{2,1,0:T(8,128)S(1)}, u32[]{:S(2)}, u32[]{:S(2)}) collective-permute-start(f32[2,32,1536]{2,1,0:T(8,128)S(1)} %fusion.35), channel_id=1, source_target_pairs={{0,4},{4,8},{8,12},{12,16},{16,20},{20,24},{24,28},{28,32},{32,36}... | collective-permute-start | bytes 1179656 | tf_op jit(solution)/shard_map/ppermute | solution.py:18
  116.5 4.7 %collective-permute-done.12 = f32[2,32,1536]{2,1,0:T(8,128)S(1)} collective-permute-done((f32[2,32,1536]{2,1,0:T(8,128)S(1)}, f32[2,32,1536]{2,1,0:T(8,128)S(1)}, u32[]{:S(2)}, u32[]{:S(2)}) %collective-permute-start.12) | collective-permute-done | bytes 393248 | tf_op jit(solution)/shard_map/ppermute | solution.py:18
  121.3 8.4 %collective-permute-start.13 = (f32[2,32,1536]{2,1,0:T(8,128)S(1)}, f32[2,32,1536]{2,1,0:T(8,128)S(1)}, u32[]{:S(2)}, u32[]{:S(2)}) collective-permute-start(f32[2,32,1536]{2,1,0:T(8,128)S(1)} %fusion.37), channel_id=1, source_target_pairs={{0,4},{4,8},{8,12},{12,16},{16,20},{20,24},{24,28},{28,32},{32,36}... | collective-permute-start | bytes 1179656 | tf_op jit(solution)/shard_map/ppermute | solution.py:18
  129.7 4.7 %collective-permute-done.13 = f32[2,32,1536]{2,1,0:T(8,128)S(1)} collective-permute-done((f32[2,32,1536]{2,1,0:T(8,128)S(1)}, f32[2,32,1536]{2,1,0:T(8,128)S(1)}, u32[]{:S(2)}, u32[]{:S(2)}) %collective-permute-start.13) | collective-permute-done | bytes 393248 | tf_op jit(solution)/shard_map/ppermute | solution.py:18
  134.4 0.8 fusion.39
  135.2 1.9 collective-permute-start.15
  137.2 15.9 %collective-permute-done.15 = f32[2,32,1536]{2,1,0:T(8,128)S(1)} collective-permute-done((f32[2,32,1536]{2,1,0:T(8,128)S(1)}, f32[2,32,1536]{2,1,0:T(8,128)S(1)}, u32[]{:S(2)}, u32[]{:S(2)}) %collective-permute-start.15) | collective-permute-done | bytes 393248 | tf_op jit(solution)/shard_map/ppermute | solution.py:18
  153.1 0.8 fusion.30
  153.9 1.9 collective-permute-start.16
  155.8 2.0 slice.191
  157.8 2.0 slice.192
  159.8 1.9 copy.115
  161.8 1.9 copy.113
  163.7 1.9 convolution_convert_fusion
  165.6 7.7 %collective-permute-start.14 = (f32[2,32,1536]{2,1,0:T(8,128)}, f32[2,32,1536]{2,1,0:T(8,128)S(1)}, u32[]{:S(2)}, u32[]{:S(2)}) collective-permute-start(f32[2,32,1536]{2,1,0:T(8,128)} %get-tuple-element.15), channel_id=1, source_target_pairs={{0,4},{4,8},{8,12},{12,16},{16,20},{20,24},{24,28},{28,32},{32,36}... | collective-permute-start | bytes 1179656 | tf_op jit(solution)/shard_map/ppermute | solution.py:18
  173.3 1.8 fusion.41
  175.1 1.9 collective-permute-start.17
  177.1 1.1 pad_maximum_fusion
  178.2 2.4 copy.120
  180.7 55.7 %psum.35 = f32[8,12]{1,0:T(8,128)S(1)} all-reduce(f32[8,12]{1,0:T(8,128)S(1)} %select_multiply_fusion), channel_id=1, replica_groups=mesh['seq_0'=8,'seq_1'=4,'seq_2'=2,'seq_3'=2,'dp'=4] {'seq_0'}, use_global_device_ids=true, to_apply=%region_9.10 | all-reduce | flops 96 | bytes 768 | tf_op jit(solution)/shard_map/psum | solution.py:22
  236.4 6.0 %psum.36 = f32[8,12]{1,0:T(8,128)S(1)} all-reduce(f32[8,12]{1,0:T(8,128)S(1)} %psum.35), channel_id=1, replica_groups=mesh['seq_0'=8,'seq_1'=4,'seq_2'=2,'seq_3'=2,'dp'=4] {'seq_1'}, use_global_device_ids=true, to_apply=%region_10.11 | all-reduce | flops 96 | bytes 768 | tf_op jit(solution)/shard_map/psum | solution.py:22
  242.4 12.4 %psum.37 = f32[8,12]{1,0:T(8,128)S(1)} all-reduce(f32[8,12]{1,0:T(8,128)S(1)} %psum.36), channel_id=1, replica_groups=mesh['seq_0'=8,'seq_1'=4,'seq_2'=2,'seq_3'=2,'dp'=4] {'seq_2'}, use_global_device_ids=true, to_apply=%region_11.12 | all-reduce | flops 96 | bytes 768 | tf_op jit(solution)/shard_map/psum | solution.py:22
  254.8 13.5 %psum.38 = f32[8,12]{1,0:T(8,128)S(1)} all-reduce(f32[8,12]{1,0:T(8,128)S(1)} %psum.37), channel_id=1, replica_groups=mesh['seq_0'=8,'seq_1'=4,'seq_2'=2,'seq_3'=2,'dp'=4] {'seq_3'}, use_global_device_ids=true, to_apply=%region_12.13 | all-reduce | flops 96 | bytes 768 | tf_op jit(solution)/shard_map/psum | solution.py:22
  268.3 7.6 %psum.39 = f32[8,12]{1,0:T(8,128)} all-reduce(f32[8,12]{1,0:T(8,128)S(1)} %psum.38), channel_id=1, replica_groups=mesh['seq_0'=8,'seq_1'=4,'seq_2'=2,'seq_3'=2,'dp'=4] {'dp'}, use_global_device_ids=true, to_apply=%region_13.14 | all-reduce | flops 96 | bytes 768 | tf_op jit(solution)/shard_map/psum | solution.py:22
  275.9 0.7 fusion.47
  (95 shorter events, 6.3 us)
Async XLA Ops:
  0.6 24.9 %copy-start.11 = (bf16[1,3,128,1536]{3,2,1,0:T(8,128)(2,1)S(1)}, bf16[1,3,128,1536]{3,2,1,0:T(8,128)(2,1)}, u32[]{:S(2)}) copy-start(bf16[1,3,128,1536]{3,2,1,0:T(8,128)(2,1)} %param.10) | copy-start | bytes 3538948
  0.6 38.9 %collective-permute-start.9 = (bf16[2,32,1536]{2,1,0:T(8,128)(2,1)}, bf16[2,32,1536]{2,1,0:T(8,128)(2,1)S(1)}, u32[]{:S(2)}, u32[]{:S(2)}) collective-permute-start(bf16[2,32,1536]{2,1,0:T(8,128)(2,1)} %bitcast.107), channel_id=1, source_target_pairs={{4,0},{8,4},{12,8},{16,12},{20,16},{24,20},{28,24},{32,28},{36,32}... | collective-permute-start | bytes 589832 | tf_op jit(solution)/shard_map/ppermute | solution.py:18
  9.6 32.0 %collective-permute-start.6 = (bf16[2,32,1536]{2,1,0:T(8,128)(2,1)}, bf16[2,32,1536]{2,1,0:T(8,128)(2,1)S(1)}, u32[]{:S(2)}, u32[]{:S(2)}) collective-permute-start(bf16[2,32,1536]{2,1,0:T(8,128)(2,1)} %bitcast.108), channel_id=1, source_target_pairs={{0,4},{4,8},{8,12},{12,16},{16,20},{20,24},{24,28},{28,32},{32,36}... | collective-permute-start | bytes 589832 | tf_op jit(solution)/shard_map/ppermute | solution.py:18
  14.7 34.3 %collective-permute-start.3 = (bf16[2,32,1536]{2,1,0:T(8,128)(2,1)}, bf16[2,32,1536]{2,1,0:T(8,128)(2,1)}, u32[]{:S(2)}, u32[]{:S(2)}) collective-permute-start(bf16[2,32,1536]{2,1,0:T(8,128)(2,1)} %bitcast.105), channel_id=1, source_target_pairs={{4,0},{8,4},{12,8},{16,12},{20,16},{24,20},{28,24},{32,28},{36,32}... | collective-permute-start | bytes 589832 | tf_op jit(solution)/shard_map/ppermute | solution.py:18
  16.7 16.8 %collective-permute-start = (bf16[2,32,1536]{2,1,0:T(8,128)(2,1)}, bf16[2,32,1536]{2,1,0:T(8,128)(2,1)}, u32[]{:S(2)}, u32[]{:S(2)}) collective-permute-start(bf16[2,32,1536]{2,1,0:T(8,128)(2,1)} %bitcast.106), channel_id=1, source_target_pairs={{0,4},{4,8},{8,12},{12,16},{16,20},{20,24},{24,28},{28,32},{32,36}... | collective-permute-start | bytes 589832 | tf_op jit(solution)/shard_map/ppermute | solution.py:18
  29.0 3.0 %copy-start.6 = (bf16[1,1,128,1536]{2,3,1,0:T(8,128)(2,1)}, bf16[1,1,128,1536]{2,3,1,0:T(8,128)(2,1)S(1)}, u32[]{:S(2)}) copy-start(bf16[1,1,128,1536]{2,3,1,0:T(8,128)(2,1)S(1)} %copy.106) | copy-start | bytes 1179652
  32.0 5.0 %copy-start.19 = (s32[1,1,2]{2,1,0:T(1,128)S(1)}, s32[1,1,2]{2,1,0:T(1,128)}, u32[]{:S(2)}) copy-start(s32[1,1,2]{2,1,0:T(1,128)} %param.13) | copy-start | bytes 28
  32.0 26.6 %copy-start.18 = (f32[8,12]{1,0:T(8,128)S(1)}, f32[8,12]{1,0:T(8,128)}, u32[]{:S(2)}) copy-start(f32[8,12]{1,0:T(8,128)} %param.17) | copy-start | bytes 1156
  32.3 39.1 %copy-start.16 = (bf16[1,2,32,1536]{3,2,1,0:T(8,128)(2,1)S(1)}, bf16[1,2,32,1536]{3,2,1,0:T(8,128)(2,1)}, u32[]{:S(2)}) copy-start(bf16[1,2,32,1536]{3,2,1,0:T(8,128)(2,1)} %param.12) | copy-start | bytes 589828
  33.5 17.6 %collective-permute-start.1 = (bf16[2,32,1536]{2,1,0:T(8,128)(2,1)}, bf16[2,32,1536]{2,1,0:T(8,128)(2,1)S(1)}, u32[]{:S(2)}, u32[]{:S(2)}) collective-permute-start(bf16[2,32,1536]{2,1,0:T(8,128)(2,1)} %collective-permute-done), channel_id=1, source_target_pairs={{0,4},{4,8},{8,12},{12,16},{16,20},{20,24},{24,28},{28,32},{32,36}... | collective-permute-start | bytes 589832 | tf_op jit(solution)/shard_map/ppermute | solution.py:18
  39.6 19.1 %collective-permute-start.10 = (bf16[2,32,1536]{2,1,0:T(8,128)(2,1)S(1)}, bf16[2,32,1536]{2,1,0:T(8,128)(2,1)S(1)}, u32[]{:S(2)}, u32[]{:S(2)}) collective-permute-start(bf16[2,32,1536]{2,1,0:T(8,128)(2,1)S(1)} %collective-permute-done.9), channel_id=1, source_target_pairs={{4,0},{8,4},{12,8},{16,12},{20,16},{24,20},{28,24},{32,28},{36,32}... | collective-permute-start | bytes 589832 | tf_op jit(solution)/shard_map/ppermute | solution.py:18
  41.5 19.1 %collective-permute-start.7 = (bf16[2,32,1536]{2,1,0:T(8,128)(2,1)S(1)}, bf16[2,32,1536]{2,1,0:T(8,128)(2,1)S(1)}, u32[]{:S(2)}, u32[]{:S(2)}) collective-permute-start(bf16[2,32,1536]{2,1,0:T(8,128)(2,1)S(1)} %collective-permute-done.6), channel_id=1, source_target_pairs={{0,4},{4,8},{8,12},{12,16},{16,20},{20,24},{24,28},{28,32},{32,36}... | collective-permute-start | bytes 589832 | tf_op jit(solution)/shard_map/ppermute | solution.py:18
  49.1 19.1 %collective-permute-start.4 = (bf16[2,32,1536]{2,1,0:T(8,128)(2,1)}, bf16[2,32,1536]{2,1,0:T(8,128)(2,1)S(1)}, u32[]{:S(2)}, u32[]{:S(2)}) collective-permute-start(bf16[2,32,1536]{2,1,0:T(8,128)(2,1)} %collective-permute-done.3), channel_id=1, source_target_pairs={{4,0},{8,4},{12,8},{16,12},{20,16},{24,20},{28,24},{32,28},{36,32}... | collective-permute-start | bytes 589832 | tf_op jit(solution)/shard_map/ppermute | solution.py:18
  51.0 19.3 %collective-permute-start.2 = (bf16[2,32,1536]{2,1,0:T(8,128)(2,1)S(1)}, bf16[2,32,1536]{2,1,0:T(8,128)(2,1)S(1)}, u32[]{:S(2)}, u32[]{:S(2)}) collective-permute-start(bf16[2,32,1536]{2,1,0:T(8,128)(2,1)S(1)} %collective-permute-done.1), channel_id=1, source_target_pairs={{0,4},{4,8},{8,12},{12,16},{16,20},{20,24},{24,28},{28,32},{32,36}... | collective-permute-start | bytes 589832 | tf_op jit(solution)/shard_map/ppermute | solution.py:18
  58.7 25.3 %collective-permute-start.11 = (bf16[2,32,1536]{2,1,0:T(8,128)(2,1)S(1)}, bf16[2,32,1536]{2,1,0:T(8,128)(2,1)S(1)}, u32[]{:S(2)}, u32[]{:S(2)}) collective-permute-start(bf16[2,32,1536]{2,1,0:T(8,128)(2,1)S(1)} %collective-permute-done.10), channel_id=1, source_target_pairs={{4,0},{8,4},{12,8},{16,12},{20,16},{24,20},{28,24},{32,28},{36,32}... | collective-permute-start | bytes 589832 | tf_op jit(solution)/shard_map/ppermute | solution.py:18
  60.6 22.3 %collective-permute-start.8 = (bf16[2,32,1536]{2,1,0:T(8,128)(2,1)S(1)}, bf16[2,32,1536]{2,1,0:T(8,128)(2,1)}, u32[]{:S(2)}, u32[]{:S(2)}) collective-permute-start(bf16[2,32,1536]{2,1,0:T(8,128)(2,1)S(1)} %collective-permute-done.7), channel_id=1, source_target_pairs={{0,4},{4,8},{8,12},{12,16},{16,20},{20,24},{24,28},{28,32},{32,36}... | collective-permute-start | bytes 589832 | tf_op jit(solution)/shard_map/ppermute | solution.py:18
  68.2 12.6 %collective-permute-start.5 = (bf16[2,32,1536]{2,1,0:T(8,128)(2,1)S(1)}, bf16[2,32,1536]{2,1,0:T(8,128)(2,1)S(1)}, u32[]{:S(2)}, u32[]{:S(2)}) collective-permute-start(bf16[2,32,1536]{2,1,0:T(8,128)(2,1)S(1)} %collective-permute-done.4), channel_id=1, source_target_pairs={{4,0},{8,4},{12,8},{16,12},{20,16},{24,20},{28,24},{32,28},{36,32}... | collective-permute-start | bytes 589832 | tf_op jit(solution)/shard_map/ppermute | solution.py:18
  81.5 11.5 %copy-start.1 = (bf16[224,12,128]{2,0,1:T(8,128)(2,1)}, bf16[224,12,128]{2,0,1:T(8,128)(2,1)S(1)}, u32[]{:S(2)}) copy-start(bf16[224,12,128]{2,0,1:T(8,128)(2,1)S(1)} %copy.93) | copy-start | bytes 2064388
  81.8 2.1 copy-start.17
  85.6 1.0 copy-start.4
  85.6 1.1 copy-start.5
  88.5 2.1 copy-start.7
  90.6 2.4 copy-start.3
  93.5 1.1 copy-start.12
  93.5 1.2 copy-start.14
  94.2 1.9 copy-start.20
  94.7 1.5 copy-start.13
  99.8 2.3 copy-start.15
  99.8 2.5 copy-start.21
  99.8 2.5 copy-start.22
  102.2 1.8 copy-start.10
  106.6 1.3 copy-start
  111.6 9.6 %collective-permute-start.12 = (f32[2,32,1536]{2,1,0:T(8,128)S(1)}, f32[2,32,1536]{2,1,0:T(8,128)S(1)}, u32[]{:S(2)}, u32[]{:S(2)}) collective-permute-start(f32[2,32,1536]{2,1,0:T(8,128)S(1)} %fusion.35), channel_id=1, source_target_pairs={{0,4},{4,8},{8,12},{12,16},{16,20},{20,24},{24,28},{28,32},{32,36}... | collective-permute-start | bytes 1179656 | tf_op jit(solution)/shard_map/ppermute | solution.py:18
  121.3 13.1 %collective-permute-start.13 = (f32[2,32,1536]{2,1,0:T(8,128)S(1)}, f32[2,32,1536]{2,1,0:T(8,128)S(1)}, u32[]{:S(2)}, u32[]{:S(2)}) collective-permute-start(f32[2,32,1536]{2,1,0:T(8,128)S(1)} %fusion.37), channel_id=1, source_target_pairs={{0,4},{4,8},{8,12},{12,16},{16,20},{20,24},{24,28},{28,32},{32,36}... | collective-permute-start | bytes 1179656 | tf_op jit(solution)/shard_map/ppermute | solution.py:18
  135.2 17.9 %collective-permute-start.15 = (f32[2,32,1536]{2,1,0:T(8,128)S(1)}, f32[2,32,1536]{2,1,0:T(8,128)S(1)}, u32[]{:S(2)}, u32[]{:S(2)}) collective-permute-start(f32[2,32,1536]{2,1,0:T(8,128)S(1)} %get-tuple-element.16), channel_id=1, source_target_pairs={{4,0},{8,4},{12,8},{16,12},{20,16},{24,20},{28,24},{32,28},{36,32}... | collective-permute-start | bytes 1179656 | tf_op jit(solution)/shard_map/ppermute | solution.py:18
  153.9 19.4 %collective-permute-start.16 = (f32[2,32,1536]{2,1,0:T(8,128)}, f32[2,32,1536]{2,1,0:T(8,128)}, u32[]{:S(2)}, u32[]{:S(2)}) collective-permute-start(f32[2,32,1536]{2,1,0:T(8,128)} %fusion.30), channel_id=1, source_target_pairs={{4,0},{8,4},{12,8},{16,12},{20,16},{24,20},{28,24},{32,28},{36,32}... | collective-permute-start | bytes 1179656 | tf_op jit(solution)/shard_map/ppermute | solution.py:18
  157.8 5.9 %copy-start.2 = (bf16[224,12,128]{2,0,1:T(8,128)(2,1)S(1)}, bf16[224,12,128]{2,0,1:T(8,128)(2,1)}, u32[]{:S(2)}) copy-start(bf16[224,12,128]{2,0,1:T(8,128)(2,1)} %copy-done.1) | copy-start | bytes 2064388
  165.6 11.4 %copy-start.8 = (bf16[128,12,128]{0,2,1:T(8,128)(2,1)S(1)}, bf16[128,12,128]{0,2,1:T(8,128)(2,1)}, u32[]{:S(2)}) copy-start(bf16[128,12,128]{0,2,1:T(8,128)(2,1)} %copy.115) | copy-start | bytes 1179652
  165.6 11.4 %copy-start.9 = (bf16[128,12,128]{0,2,1:T(8,128)(2,1)S(1)}, bf16[128,12,128]{0,2,1:T(8,128)(2,1)}, u32[]{:S(2)}) copy-start(bf16[128,12,128]{0,2,1:T(8,128)(2,1)} %copy.113) | copy-start | bytes 1179652
  165.6 110.3 %collective-permute-start.14 = (f32[2,32,1536]{2,1,0:T(8,128)}, f32[2,32,1536]{2,1,0:T(8,128)S(1)}, u32[]{:S(2)}, u32[]{:S(2)}) collective-permute-start(f32[2,32,1536]{2,1,0:T(8,128)} %get-tuple-element.15), channel_id=1, source_target_pairs={{0,4},{4,8},{8,12},{12,16},{16,20},{20,24},{24,28},{28,32},{32,36}... | collective-permute-start | bytes 1179656 | tf_op jit(solution)/shard_map/ppermute | solution.py:18
  175.1 100.8 %collective-permute-start.17 = (f32[2,32,1536]{2,1,0:T(8,128)}, f32[2,32,1536]{2,1,0:T(8,128)S(1)}, u32[]{:S(2)}, u32[]{:S(2)}) collective-permute-start(f32[2,32,1536]{2,1,0:T(8,128)} %fusion.41), channel_id=1, source_target_pairs={{4,0},{8,4},{12,8},{16,12},{20,16},{24,20},{28,24},{32,28},{36,32}... | collective-permute-start | bytes 1179656 | tf_op jit(solution)/shard_map/ppermute | solution.py:18
where the time goes:
time: 280 us; the launch traced here: 277 us
  blocking collectives  95.2 us (34%)
  starting transfers between devices  84.3 us (30%)
  waiting for transfers between devices  33.8 us (12%)
  local copies, waits for them, and re-layouts  32.3 us (12%)
  matrix products  18 us (6%)
  other arithmetic  8.29 us (3%)
  between operations  4.61 us (2%)
    psum x5, blocking collectives, one_axis_at_a_time(): return functools.reduce(lax.psum, axes, x)  95.2 us
    ppermute x18, starting transfers between devices, from_behind(): return lax.ppermute(x, axis, pairs)  84.3 us
    ppermute x18, waiting for transfers between devices, from_behind(): return lax.ppermute(x, axis, pairs)  33.8 us
    unnamed x64, local copies, waits for them, and re-layouts  9.62 us
  transfers between devices with their start and end apart: 18, of which 4 were waited for; matrix products, arithmetic and copies ran while one was open for 10% of the time, Pallas kernels for 0%

commit v1 on v0

v1 whole, which is shorter than its diff:
```python
import functools

import jax
import jax.numpy as jnp
from jax import lax
from jax.experimental import pallas as pl
from jax.experimental.pallas import tpu as pltpu
from jax.sharding import Mesh
from jax.sharding import PartitionSpec as P

SEQ = ("seq_0", "seq_1", "seq_2", "seq_3")
PLANE = ("seq_0", "seq_1")
COLUMN = ("seq_2", "seq_3", "dp")
HALF = "seq_2"
CORE = "seq_3"
SLOTS = 8
STEP_HEADS = 2
VMEM = 28 * 1024 * 1024


def dot(a, b, contract_a, contract_b):
    return lax.dot_general(
        a, b, (((contract_a,), (contract_b,)), ((), ())), preferred_element_type=jnp.float32
    )


def by_block(f, *pairs):
    return jnp.concatenate([f(*args) for args in zip(*pairs)], axis=1)


def halves(x):
    n = x.shape[1] // 2
    return x[:, :n], x[:, n:]


def with_bias(scores, bias, rows):
    out = []
    for slot in range(SLOTS):
        piece = halves(scores[slot * rows : (slot + 1) * rows])
        out.append(jnp.concatenate([piece[b] + bias[2 * slot + b] for b in range(2)], axis=1))
    return jnp.concatenate(out, axis=0)


def load_head(lanes, mine, other, audio):
    q = (mine[0, 0, :, lanes], other[0, :, lanes])
    k = (mine[0, 1, :, lanes], other[1, :, lanes])
    v = (mine[0, 2, :, lanes], other[2, :, lanes])
    ka = jnp.concatenate([ref[b, 0, :, lanes] for ref in audio for b in range(2)], axis=0)
    va = jnp.concatenate([ref[b, 1, :, lanes] for ref in audio for b in range(2)], axis=0)
    return q, k, v, ka, va


def scores_of(q, k, ka, scale, bias, rows):
    local = by_block(lambda kb, qb: dot(kb, qb, 1, 1), k, q) * scale
    audio = dot(ka, jnp.concatenate(q, axis=0), 1, 1) * scale
    return local, with_bias(audio, bias, rows)


def column_max(x):
    return jnp.max(x, axis=0, keepdims=True)


def column_sum(x):
    return jnp.sum(x, axis=0, keepdims=True)


def times_values(v, va, local, audio):
    return by_block(lambda vb, pb: dot(vb, pb, 0, 0), v, halves(local)) + dot(va, audio, 0, 0)


def teacher_kernel(dim, core, bias, scal, mine, other, own, zed, far, nat, target):
    rows = own.shape[2]
    for i in range(target.shape[0]):
        lanes = slice(i * dim, (i + 1) * dim)
        q, k, v, ka, va = load_head(lanes, mine, other, (own, zed, far, nat))
        local, audio = scores_of(q, k, ka, dim**-0.5, bias, rows)
        plain_max = column_max(local)
        plain = jnp.exp(local - plain_max)
        plain = (plain * (1.0 / column_sum(plain))).astype(jnp.bfloat16)
        highest = jnp.maximum(plain_max, column_max(audio))
        local = jnp.exp(local - highest)
        audio = jnp.exp(audio - highest)
        norm = 1.0 / (column_sum(local) + column_sum(audio))
        local = (local * norm).astype(jnp.bfloat16)
        audio = (audio * norm).astype(jnp.bfloat16)
        conditional = times_values(v, va, local, audio)
        unconditional = by_block(lambda vb, pb: dot(vb, pb, 0, 0), v, halves(plain))
        target[i] = unconditional + scal[0] * (conditional - unconditional)


def student_kernel(
    dim,
    core,
    bias,
    scal,
    mine,
    other,
    own,
    zed,
    far,
    nat,
    target,
    grad_mine,
    grad_other,
    own_out,
    zed_out,
    far_out,
    nat_out,
    totals,
):
    rows = own.shape[2]
    scale = dim**-0.5
    heads = target.shape[0]
    for i in range(heads):
        lanes = slice(i * dim, (i + 1) * dim)
        q, k, v, ka, va = load_head(lanes, mine, other, (own, zed, far, nat))
        local, audio = scores_of(q, k, ka, scale, bias, rows)
        highest = jnp.maximum(column_max(local), column_max(audio))
        local = jnp.exp(local - highest)
        audio = jnp.exp(audio - highest)
        norm = 1.0 / (column_sum(local) + column_sum(audio))
        local = local * norm
        audio = audio * norm
        local_round = local.astype(jnp.bfloat16)
        audio_round = audio.astype(jnp.bfloat16)
        out = times_values(v, va, local_round, audio_round)
        factor = scal[2 + pl.program_id(0) * heads + i]
        residual = scal[1] * (out * factor - target[i])
        product = residual * out
        n = product.shape[1] // 2
        product = product[:, :n] + product[:, n:]
        totals[i] = jnp.sum(product.reshape(dim // 8, 8, n), axis=0)
        out_grad = (residual * factor).astype(jnp.bfloat16)
        row_delta = column_sum(out_grad.astype(jnp.float32) * out)
        grads = halves(out_grad)
        local_grad = by_block(lambda vb, gb: dot(vb, gb, 1, 0), v, grads)
        audio_grad = dot(va, out_grad, 1, 0)
        local_grad = (scale * local * (local_grad - row_delta)).astype(jnp.bfloat16)
        audio_grad = (scale * audio * (audio_grad - row_delta)).astype(jnp.bfloat16)
        query_grad = times_values(k, ka, local_grad, audio_grad).T.astype(jnp.bfloat16)
        vb = query_grad.shape[0] // 2
        score_halves = halves(local_grad)
        prob_halves = halves(local_round)
        for b, ref in enumerate((grad_mine, grad_other)):
            ref[0, :, lanes] = query_grad[b * vb : (b + 1) * vb]
            ref[1, :, lanes] = dot(score_halves[b], q[b], 1, 0).astype(jnp.bfloat16)
            ref[2, :, lanes] = dot(prob_halves[b], grads[b], 1, 1).astype(jnp.bfloat16)
        audio_keys = dot(audio_grad, jnp.concatenate(q, axis=0), 1, 0)
        audio_values = dot(audio_round, out_grad, 1, 1)
        for slot in range(SLOTS):
            ref = (own_out, zed_out, far_out, nat_out)[slot // 2]
            at = slice(slot * rows, (slot + 1) * rows)
            ref[slot % 2, 0, :, lanes] = audio_keys[at].astype(ref.dtype)
            ref[slot % 2, 1, :, lanes] = audio_values[at].astype(ref.dtype)


def specs(steps, width, vb, rows):
    smem = pl.BlockSpec(memory_space=pltpu.SMEM)
    mine = pl.BlockSpec((1, 3, vb, width), lambda h, c: (0, 0, 0, c[0] * steps + h))
    video = pl.BlockSpec((3, vb, width), lambda h, c: (0, 0, h))
    window = pl.BlockSpec((2, 2, rows, width), lambda h, c: (0, 0, 0, c[0] * steps + h))
    piece = pl.BlockSpec((2, 2, rows, width), lambda h, c: (0, 0, 0, h))
    return smem, mine, video, window, piece


def teacher_call(core, bias, scal, mine, other, audio, head_dim):
    vb, half_width = mine.shape[2], other.shape[2]
    rows = audio[0].shape[2]
    width = STEP_HEADS * head_dim
    steps = half_width // width
    smem, own_video, video, window, _ = specs(steps, width, vb, rows)
    heads = half_width // head_dim
    return pl.pallas_call(
        functools.partial(teacher_kernel, head_dim),
        grid_spec=pltpu.PrefetchScalarGridSpec(
            num_scalar_prefetch=1,
            grid=(steps,),
            in_specs=[smem, smem, own_video, video] + [window] * 4,
            out_specs=pl.BlockSpec((STEP_HEADS, head_dim, 2 * vb), lambda h, c: (h, 0, 0)),
        ),
        out_shape=jax.ShapeDtypeStruct((heads, head_dim, 2 * vb), jnp.float32),
        compiler_params=pltpu.CompilerParams(vmem_limit_bytes=VMEM),
        cost_estimate=pl.CostEstimate(
            flops=600_000_000, bytes_accessed=4_000_000, transcendentals=900_000
        ),
        name="teacher",
    )(core, bias, scal, mine, other, *audio)


def student_call(core, bias, scal, mine, other, audio, target, head_dim):
    vb, half_width = mine.shape[2], other.shape[2]
    rows = audio[0].shape[2]
    width = STEP_HEADS * head_dim
    steps = half_width // width
    smem, own_video, video, window, piece = specs(steps, width, vb, rows)
    heads = half_width // head_dim
    video_shape = jax.ShapeDtypeStruct((3, vb, half_width), jnp.bfloat16)
    wide = jax.ShapeDtypeStruct((2, 2, rows, half_width), jnp.float32)
    narrow = jax.ShapeDtypeStruct((2, 2, rows, half_width), jnp.bfloat16)
    return pl.pallas_call(
        functools.partial(student_kernel, head_dim),
        grid_spec=pltpu.PrefetchScalarGridSpec(
            num_scalar_prefetch=1,
            grid=(steps,),
            in_specs=[smem, smem, own_video, video]
            + [window] * 4
            + [pl.BlockSpec((STEP_HEADS, head_dim, 2 * vb), lambda h, c: (h, 0, 0))],
            out_specs=[video, video, piece, piece, piece, piece]
            + [pl.BlockSpec((STEP_HEADS, 8, vb), lambda h, c: (h, 0, 0))],
        ),
        out_shape=[video_shape, video_shape, wide, wide, narrow, narrow]
        + [jax.ShapeDtypeStruct((heads, 8, vb), jnp.float32)],
        compiler_params=pltpu.CompilerParams(vmem_limit_bytes=VMEM),
        cost_estimate=pl.CostEstimate(
            flops=900_000_000, bytes_accessed=8_000_000, transcendentals=600_000
        ),
        name="student",
    )(core, bias, scal, mine, other, *audio, target)


def swap(x, axis):
    return lax.ppermute(x, axis, [(0, 1), (1, 0)])


def everywhere(x, axes):
    n = lax.axis_size(axes)
    copies = jnp.broadcast_to(x[None], (n,) + x.shape)
    return jnp.sum(lax.all_to_all(copies, axes, 0, 0), axis=0)


def body(
    teacher_video,
    student_video,
    teacher_audio,
    student_audio,
    alignment,
    guidance_index,
    step_index,
    null_flag,
    gamma,
):
    heads = gamma.shape[1]
    width = teacher_video.shape[3]
    half_width = width // 2
    head_dim = width // heads
    half_heads = heads // 2
    tokens = teacher_video.shape[2]
    core = lax.axis_index(CORE)
    half = lax.axis_index(HALF)
    position = lax.axis_index(SEQ)
    base = position - core

    group = lax.axis_size(HALF) * lax.axis_size(CORE)
    count = lax.axis_size(SEQ)
    places = range(count)

    def inside(pairs):
        return [(a, b) for a, b in pairs if 0 <= b < count]

    near_pairs = inside((i, i + group if i % 2 else i - group) for i in places)
    far_out = inside((i, i - group if (i // 2) % 2 else i + group) for i in places)
    far_back = [(b, a) for a, b in far_out]

    teach, pupil = teacher_audio[0], student_audio[0]
    teach_zed = swap(teach, HALF)
    pupil_zed = swap(pupil, HALF)
    teach_nat = lax.ppermute(teach, SEQ, near_pairs)
    pupil_nat = lax.ppermute(pupil, SEQ, near_pairs)
    teach_far = lax.ppermute(teach_zed, SEQ, far_out)
    pupil_far = lax.ppermute(pupil_zed, SEQ, far_out)

    def sibling(video):
        return swap(lax.dynamic_slice_in_dim(video[0], (1 - core) * half_width, half_width, 2), CORE)

    teach_other = sibling(teacher_video)
    pupil_other = sibling(student_video)
    spans = lax.all_gather(alignment[0, 0], CORE)

    def both(pieces):
        return [lax.all_gather(piece, CORE) for piece in pieces]

    teach_window = both((teach, teach_zed, teach_far, teach_nat))
    pupil_window = both((pupil, pupil_zed, pupil_far, pupil_nat))

    side = 2 - 4 * half
    owners = base + jnp.stack(
        [jnp.int32(0), jnp.int32(1), side, side + 1, -side, 1 - side, jnp.int32(4), jnp.int32(-3)]
    )
    order = jnp.stack([core, 1 - core])
    first = jnp.take(spans[:, 0], order)[None, :]
    length = jnp.take(spans[:, 1], order)[None, :]
    used = (owners[:, None] >= first) & (owners[:, None] < first + length) & (null_flag[0] == 0)
    bias = jnp.where(used, 0.0, -jnp.inf).astype(jnp.float32).reshape(2 * SLOTS)

    level_index = guidance_index[0]
    levels = jnp.arange(gamma.shape[0], dtype=jnp.int32)
    weight = 1.0 + 0.75 * level_index.astype(jnp.float32)
    loss_weight = 1.0 / (1.0 + step_index[0].astype(jnp.float32) / 250.0)
    factor = jnp.sum(
        jnp.where(levels[:, None] == level_index, gamma, jnp.zeros_like(gamma)), axis=0
    )
    factor = lax.dynamic_slice_in_dim(factor, core * half_heads, half_heads)
    scal = jnp.concatenate([jnp.stack([weight, loss_weight]), factor])
    which = core.astype(jnp.int32)[None]

    target = teacher_call(which, bias, scal, teacher_video, teach_other, teach_window, head_dim)
    grad_mine, grad_other, own, zed, far, nat, totals = student_call(
        which, bias, scal, student_video, pupil_other, pupil_window, target, head_dim
    )

    far_in = lax.ppermute(far, SEQ, far_back)
    next_in = lax.ppermute(nat[0], SEQ, inside((i, i + group) for i in places))
    prev_in = lax.ppermute(nat[1], SEQ, inside((i, i - group) for i in places))
    zed_in = swap((zed + far_in.astype(jnp.float32)).astype(jnp.bfloat16), HALF)
    own = own + zed_in.astype(jnp.float32)
    own = own + jnp.stack([next_in, prev_in]).astype(jnp.float32)
    leave = lax.dynamic_index_in_dim(own, 1 - core, 0, keepdims=False).astype(jnp.bfloat16)
    keep = lax.dynamic_index_in_dim(own, core, 0, keepdims=False).astype(jnp.bfloat16)

    def joined(mine, other):
        return jnp.where(
            core == 0,
            jnp.concatenate([mine, other], axis=-1),
            jnp.concatenate([other, mine], axis=-1),
        )[None]

    grad_audio = joined(keep, swap(leave, CORE))
    grad_video = joined(grad_mine, swap(grad_other, CORE))

    sums = jnp.sum(totals, axis=(1, 2))
    head_totals = lax.dynamic_update_slice_in_dim(
        jnp.zeros((heads,), jnp.float32), sums, core * half_heads, 0
    )
    contribution = jnp.where(
        levels[:, None] == level_index, head_totals[None, :], jnp.zeros_like(gamma)
    )
    gamma_grad = everywhere(everywhere(contribution, COLUMN), PLANE) / (tokens * count * head_dim)
    return (grad_video, grad_audio, gamma_grad)


def solution(mesh):
    finer = Mesh(
        mesh.devices.reshape(8, 4, 2, 2, mesh.shape["dp"]),
        ("seq_0", "seq_1", "seq_2", "seq_3", "dp"),
    )
    in_specs = (
        P("dp", None, SEQ, None),
        P("dp", None, SEQ, None),
        P("dp", None, SEQ, None),
        P("dp", None, SEQ, None),
        P("dp", SEQ, None),
        P("dp"),
        P("dp"),
        P("dp"),
        P(),
    )
    out_specs = (P("dp", None, SEQ, None), P("dp", None, SEQ, None), P())
    return jax.shard_map(body, mesh=finer, in_specs=in_specs, out_specs=out_specs, check_vma=False)
```

time: 280 us -> 129 us (0.46)
  blocking collectives: 95.2 us -> 34.6 us
  local copies, waits for them, and re-layouts: 32.3 us -> 4.68 us
  waiting for transfers between devices: 33.8 us -> 8.04 us
  starting transfers between devices: 84.3 us -> 64.2 us
  matrix products: 18 us -> 0 us
  Pallas kernels: 0 us -> 10.3 us
  other arithmetic: 8.29 us -> 3.69 us
    psum x5 -> x0, blocking collectives: 95.2 us -> none  [one_axis_at_a_time(): return functools.reduce(lax.psum, axes, x)]
    ppermute x18 -> x14, starting transfers between devices: 84.3 us -> 49.2 us  [the longest x7 28.3 us: swap(): return lax.ppermute(x, axis, [(0, 1), (1, 0)])]
    ppermute x18 -> x14, waiting for transfers between devices: 33.8 us -> 1.3 us  [the longest x1 1.03 us: body(): far_in = lax.ppermute(far, SEQ, far_back)]
    all_gather x0 -> x9, blocking collectives: none -> 19.9 us  [the longest x8 18 us: both(): return [lax.all_gather(piece, CORE) for piece in pieces]]
    dot_general x9 -> x0, matrix products: 17.3 us -> none  [the longest x1 3.69 us: body(): jnp.einsum('hqk,khe->qhe', cond_probs, teach_values, preferred_element_ty...]
    all_to_all x0 -> x1, starting transfers between devices: none -> 15 us  [everywhere(): return jnp.sum(lax.all_to_all(copies, axes, 0, 0), axis=0)]
    all_to_all x0 -> x1, blocking collectives: none -> 14.6 us  [everywhere(): return jnp.sum(lax.all_to_all(copies, axes, 0, 0), axis=0)]
    slice x18 -> x1, local copies, waits for them, and re-layouts: 13.6 us -> 0.17 us  [body(): first = jnp.take(spans[:, 0], order)[None, :]]
  transfers between devices with their start and end apart: 18 -> 15, of which waited for: 4 -> 3; matrix products, arithmetic and copies ran while one was open for 10% -> 5% of each run, Pallas kernels for 0% -> 3%
where the time goes in v1:
time: 129 us; the launch traced here: 128 us
  starting transfers between devices  64.2 us (50%)
  blocking collectives  34.6 us (27%)
  Pallas kernels  10.3 us (8%)
  waiting for transfers between devices  8.04 us (6%)
  local copies, waits for them, and re-layouts  4.68 us (4%)
  other arithmetic  3.69 us (3%)
  between operations  2.89 us (2%)
    ppermute x7, starting transfers between devices, swap(): return lax.ppermute(x, axis, [(0, 1), (1, 0)])  28.3 us
    all_gather x8, blocking collectives, both(): return [lax.all_gather(piece, CORE) for piece in pieces]  18 us
    all_to_all x1, starting transfers between devices, everywhere(): return jnp.sum(lax.all_to_all(copies, axes, 0, 0), axis=0)  15 us
    all_to_all x1, blocking collectives, everywhere(): return jnp.sum(lax.all_to_all(copies, axes, 0, 0), axis=0)  14.6 us
    all_to_all x1, waiting for transfers between devices, everywhere(): return jnp.sum(lax.all_to_all(copies, axes, 0, 0), axis=0)  6.74 us
    pallas_call x1, Pallas kernels, student_call(): pl.pallas_call(functools.partial(student_kernel, head_dim), grid_spec=plt...  6.6 us
    ppermute x1, starting transfers between devices, body(): lax.ppermute(nat[0], SEQ, inside(((i, i + group) for i in places)))  3.99 us
    ppermute x1, starting transfers between devices, body(): teach_nat = lax.ppermute(teach, SEQ, near_pairs)  3.8 us
  transfers between devices with their start and end apart: 15, of which 3 were waited for; matrix products, arithmetic and copies ran while one was open for 5% of the time, Pallas kernels for 3%

profile of v1, /device:TPU:1, one launch (start us, length us, event | category | flops | bytes accessed | tf_op | source)
XLA Modules:
  0.0 128.3 jit_solution(6653985182767307738)
XLA Ops:
  0.6 11.5 %collective-permute-start.5 = (bf16[2,32,1536]{2,1,0:T(8,128)(2,1)}, bf16[2,32,1536]{2,1,0:T(8,128)(2,1)}, u32[]{:S(2)}, u32[]{:S(2)}) collective-permute-start(bf16[2,32,1536]{2,1,0:T(8,128)(2,1)} %bitcast.43), channel_id=1, source_target_pairs={{0,8},{8,0},{1,9},{9,1},{2,10},{10,2},{3,11},{11,3},{4,12},{12,4},... | collective-permute-start | bytes 589832 | tf_op jit(solution)/shard_map/ppermute | solution.py:222
  12.1 3.8 %collective-permute-start.7 = (bf16[2,32,1536]{2,1,0:T(8,128)(2,1)}, bf16[2,32,1536]{2,1,0:T(8,128)(2,1)}, u32[]{:S(2)}, u32[]{:S(2)}) collective-permute-start(bf16[2,32,1536]{2,1,0:T(8,128)(2,1)} %bitcast.44), channel_id=1, source_target_pairs={{4,20},{12,28},{16,0},{20,36},{24,8},{28,44},{32,16},{36,52},{40,2... | collective-permute-start | bytes 589832 | tf_op jit(solution)/shard_map/ppermute | solution.py:267
  15.9 1.9 %collective-permute-start.1 = (bf16[2,32,1536]{2,1,0:T(8,128)(2,1)}, bf16[2,32,1536]{2,1,0:T(8,128)(2,1)}, u32[]{:S(2)}, u32[]{:S(2)}) collective-permute-start(bf16[2,32,1536]{2,1,0:T(8,128)(2,1)} %bitcast.45), channel_id=1, source_target_pairs={{0,8},{8,0},{1,9},{9,1},{2,10},{10,2},{3,11},{11,3},{4,12},{12,4},... | collective-permute-start | bytes 589832 | tf_op jit(solution)/shard_map/ppermute | solution.py:222
  17.8 3.2 %collective-permute-start.3 = (bf16[2,32,1536]{2,1,0:T(8,128)(2,1)}, bf16[2,32,1536]{2,1,0:T(8,128)(2,1)}, u32[]{:S(2)}, u32[]{:S(2)}) collective-permute-start(bf16[2,32,1536]{2,1,0:T(8,128)(2,1)} %bitcast.46), channel_id=1, source_target_pairs={{4,20},{12,28},{16,0},{20,36},{24,8},{28,44},{32,16},{36,52},{40,2... | collective-permute-start | bytes 589832 | tf_op jit(solution)/shard_map/ppermute | solution.py:268
  21.0 1.2 dynamic-slice_bitcast_fusion
  22.2 0.0 copy-start.4
  22.2 1.9 %collective-permute-start.4 = (bf16[3,128,768]{2,1,0:T(8,128)(2,1)S(1)}, bf16[3,128,768]{2,1,0:T(8,128)(2,1)S(1)}, u32[]{:S(2)}, u32[]{:S(2)}) collective-permute-start(bf16[3,128,768]{2,1,0:T(8,128)(2,1)S(1)} %dynamic-slice_bitcast_fusion), channel_id=1, source_target_pairs={{0,4},{4,0},{1,5},{5,1},{2,6},{6,2},{3,7},{7,3},{8,12},{12,8},{9,1... | collective-permute-start | bytes 1769480 | tf_op jit(solution)/shard_map/ppermute | solution.py:222
  24.1 0.0 copy-start.2
  24.1 0.1 compare_select_fusion
  24.2 2.0 %all-gather = s32[2,1,2]{2,1,0:T(1,128)S(1)} all-gather(s32[1,1,2]{2,1,0:T(1,128)S(1)} %copy-done.5), channel_id=2, replica_groups=mesh['seq_0'=8,'seq_1'=4,'seq_2'=2,'seq_3'=2,'dp'=4] {'seq_3'}, dimensions={0}, use_global_device_ids=true | all-gather | bytes 24 | tf_op jit(solution)/shard_map/all_gather | solution.py:277
  26.2 0.2 slice_reduce_fusion.1
  26.4 0.6 gather_fusion.1
  27.0 0.6 gather_fusion
  28.3 0.1 broadcast_select_fusion.1
  28.4 0.1 stack.39
  28.5 0.1 and_select_fusion
  28.6 0.1 select_n.74.bias
  30.1 0.1 select_reduce_fusion
  30.2 0.1 dynamic_slice.20
  30.3 0.1 pad_maximum_fusion.scal
  30.3 2.1 %all_gather.53.own = bf16[2,2,32,1536]{3,2,1,0:T(8,128)(2,1)S(1)} all-gather(bf16[1,2,32,1536]{3,2,1,0:T(8,128)(2,1)S(1)} %copy-done.2), channel_id=1, replica_groups=mesh['seq_0'=8,'seq_1'=4,'seq_2'=2,'seq_3'=2,'dp'=4] {'seq_3'}, dimensions={0}, use_global_device_ids=true | all-gather | bytes 589824 | tf_op jit(solution)/shard_map/all_gather | solution.py:280
  32.4 2.1 %all_gather.46.own = bf16[2,2,32,1536]{3,2,1,0:T(8,128)(2,1)S(1)} all-gather(bf16[1,2,32,1536]{3,2,1,0:T(8,128)(2,1)S(1)} %copy-done.3), channel_id=1, replica_groups=mesh['seq_0'=8,'seq_1'=4,'seq_2'=2,'seq_3'=2,'dp'=4] {'seq_3'}, dimensions={0}, use_global_device_ids=true | all-gather | bytes 589824 | tf_op jit(solution)/shard_map/all_gather | solution.py:280
  34.5 0.0 collective-permute-done.5
  34.5 2.2 %collective-permute-start = (bf16[3,128,768]{2,1,0:T(8,128)(2,1)S(1)}, bf16[3,128,768]{2,1,0:T(8,128)(2,1)S(1)}, u32[]{:S(2)}, u32[]{:S(2)}) collective-permute-start(bf16[3,128,768]{2,1,0:T(8,128)(2,1)S(1)} %dynamic-slice_bitcast_fusion.1), channel_id=1, source_target_pairs={{0,4},{4,0},{1,5},{5,1},{2,6},{6,2},{3,7},{7,3},{8,12},{12,8},{9,1... | collective-permute-start | bytes 1769480 | tf_op jit(solution)/shard_map/ppermute | solution.py:222
  36.7 2.3 %all-gather.4 = bf16[4,32,1536]{2,1,0:T(8,128)(2,1)S(1)} all-gather(bf16[2,32,1536]{2,1,0:T(8,128)(2,1)} %collective-permute-done.5), channel_id=6, replica_groups=mesh['seq_0'=8,'seq_1'=4,'seq_2'=2,'seq_3'=2,'dp'=4] {'seq_3'}, dimensions={0}, use_global_device_ids=true | all-gather | bytes 589824 | tf_op jit(solution)/shard_map/all_gather | solution.py:280
  39.0 0.0 collective-permute-done.1
  39.0 3.5 %collective-permute-start.6 = (bf16[2,32,1536]{2,1,0:T(8,128)(2,1)}, bf16[2,32,1536]{2,1,0:T(8,128)(2,1)S(1)}, u32[]{:S(2)}, u32[]{:S(2)}) collective-permute-start(bf16[2,32,1536]{2,1,0:T(8,128)(2,1)} %collective-permute-done.5), channel_id=1, source_target_pairs={{0,16},{4,20},{16,32},{20,36},{24,8},{28,12},{32,48},{36,52},{40,2... | collective-permute-start | bytes 589832 | tf_op jit(solution)/shard_map/ppermute | solution.py:269
  42.5 2.5 %all-gather.1 = bf16[4,32,1536]{2,1,0:T(8,128)(2,1)S(1)} all-gather(bf16[2,32,1536]{2,1,0:T(8,128)(2,1)} %collective-permute-done.1), channel_id=3, replica_groups=mesh['seq_0'=8,'seq_1'=4,'seq_2'=2,'seq_3'=2,'dp'=4] {'seq_3'}, dimensions={0}, use_global_device_ids=true | all-gather | bytes 589824 | tf_op jit(solution)/shard_map/all_gather | solution.py:280
  45.1 0.0 collective-permute-done.7
  45.1 3.8 %collective-permute-start.2 = (bf16[2,32,1536]{2,1,0:T(8,128)(2,1)}, bf16[2,32,1536]{2,1,0:T(8,128)(2,1)S(1)}, u32[]{:S(2)}, u32[]{:S(2)}) collective-permute-start(bf16[2,32,1536]{2,1,0:T(8,128)(2,1)} %collective-permute-done.1), channel_id=1, source_target_pairs={{0,16},{4,20},{16,32},{20,36},{24,8},{28,12},{32,48},{36,52},{40,2... | collective-permute-start | bytes 589832 | tf_op jit(solution)/shard_map/ppermute | solution.py:270
  48.8 2.6 %all-gather.6 = bf16[4,32,1536]{2,1,0:T(8,128)(2,1)S(1)} all-gather(bf16[2,32,1536]{2,1,0:T(8,128)(2,1)} %collective-permute-done.7), channel_id=8, replica_groups=mesh['seq_0'=8,'seq_1'=4,'seq_2'=2,'seq_3'=2,'dp'=4] {'seq_3'}, dimensions={0}, use_global_device_ids=true | all-gather | bytes 589824 | tf_op jit(solution)/shard_map/all_gather | solution.py:280
  51.4 0.0 collective-permute-done.3
  51.4 2.3 %all-gather.3 = bf16[4,32,1536]{2,1,0:T(8,128)(2,1)S(1)} all-gather(bf16[2,32,1536]{2,1,0:T(8,128)(2,1)} %collective-permute-done.3), channel_id=5, replica_groups=mesh['seq_0'=8,'seq_1'=4,'seq_2'=2,'seq_3'=2,'dp'=4] {'seq_3'}, dimensions={0}, use_global_device_ids=true | all-gather | bytes 589824 | tf_op jit(solution)/shard_map/all_gather | solution.py:280
  53.7 0.0 collective-permute-done.6
  53.7 2.1 %all-gather.5 = bf16[4,32,1536]{2,1,0:T(8,128)(2,1)S(1)} all-gather(bf16[2,32,1536]{2,1,0:T(8,128)(2,1)S(1)} %collective-permute-done.6), channel_id=7, replica_groups=mesh['seq_0'=8,'seq_1'=4,'seq_2'=2,'seq_3'=2,'dp'=4] {'seq_3'}, dimensions={0}, use_global_device_ids=true | all-gather | bytes 589824 | tf_op jit(solution)/shard_map/all_gather | solution.py:280
  55.8 0.0 collective-permute-done.2
  55.8 2.1 %all-gather.2 = bf16[4,32,1536]{2,1,0:T(8,128)(2,1)S(1)} all-gather(bf16[2,32,1536]{2,1,0:T(8,128)(2,1)S(1)} %collective-permute-done.2), channel_id=4, replica_groups=mesh['seq_0'=8,'seq_1'=4,'seq_2'=2,'seq_3'=2,'dp'=4] {'seq_3'}, dimensions={0}, use_global_device_ids=true | all-gather | bytes 589824 | tf_op jit(solution)/shard_map/all_gather | solution.py:280
  57.9 0.0 collective-permute-done.4.other
  57.9 3.7 %teacher.1.target = f32[6,128,256]{2,1,0:T(8,128)S(1)} custom-call(s32[1]{0:T(128)} %bitcast.core, f32[16]{0:T(128)S(1)} %select_n.74.bias, f32[8]{0:T(128)S(1)} %pad_maximum_fusion.scal, bf16[1,3,128,1536]{3,2,1,0:T(8,128)(2,1)S(1)} %copy-done, bf16[3,128,768]{2,1,0:T(8,128)(2,1)S(1)} %collective-permute-done.4.other, ...), custom_call_target="tpu_custom_call" | custom-call | flops 600000000 | bytes 4000000 | tf_op jit(solution)/shard_map/teacher/pallas_call | solution.py:173
  61.6 6.6 %student.1 = (bf16[3,128,768]{2,1,0:T(8,128)(2,1)S(1)}, bf16[3,128,768]{2,1,0:T(8,128)(2,1)S(1)}, f32[2,2,32,768]{3,2,1,0:T(8,128)S(1)}, f32[2,2,32,768]{3,2,1,0...) custom-call(s32[1]{0:T(128)} %bitcast.core, ...), custom_call_target="tpu_custom_call" | custom-call | flops 900000000 | bytes 8000000 | tf_op jit(solution)/shard_map/student/pallas_call | solution.py:200
  68.2 1.3 %collective-permute-start.9 = (bf16[2,2,32,768]{3,2,1,0:T(8,128)(2,1)S(1)}, bf16[2,2,32,768]{3,2,1,0:T(8,128)(2,1)S(1)}, u32[]{:S(2)}, u32[]{:S(2)}) collective-permute-start(bf16[2,2,32,768]{3,2,1,0:T(8,128)(2,1)S(1)} %get-tuple-element.15), channel_id=1, source_target_pairs={{16,0},{20,4},{32,16},{36,20},{8,24},{12,28},{48,32},{52,36},{24,4... | collective-permute-start | bytes 589832 | tf_op jit(solution)/shard_map/ppermute | solution.py:311
  69.5 4.0 %collective-permute-start.11 = (bf16[2,32,768]{2,1,0:T(8,128)(2,1)S(1)}, bf16[2,32,768]{2,1,0:T(8,128)(2,1)S(1)}, u32[]{:S(2)}, u32[]{:S(2)}) collective-permute-start(bf16[2,32,768]{2,1,0:T(8,128)(2,1)S(1)} %get-tuple-element.31), channel_id=1, source_target_pairs={{0,16},{4,20},{8,24},{12,28},{16,32},{20,36},{24,40},{28,44},{32,4... | collective-permute-start | bytes 294920 | tf_op jit(solution)/shard_map/ppermute | solution.py:312
  73.5 1.3 %collective-permute-start.12 = (bf16[2,32,768]{2,1,0:T(8,128)(2,1)S(1)}, bf16[2,32,768]{2,1,0:T(8,128)(2,1)}, u32[]{:S(2)}, u32[]{:S(2)}) collective-permute-start(bf16[2,32,768]{2,1,0:T(8,128)(2,1)S(1)} %get-tuple-element.32), channel_id=1, source_target_pairs={{16,0},{20,4},{24,8},{28,12},{32,16},{36,20},{40,24},{44,28},{48,3... | collective-permute-start | bytes 294920 | tf_op jit(solution)/shard_map/ppermute | solution.py:313
  74.8 0.1 reduce_sum.37
  74.9 0.2 dynamic_update_slice.14
  75.2 1.0 collective-permute-done.9
  76.2 4.3 %collective-permute-start.10 = (bf16[2,2,32,768]{3,2,1,0:T(8,128)(2,1)S(1)}, bf16[2,2,32,768]{3,2,1,0:T(8,128)(2,1)S(1)}, u32[]{:S(2)}, u32[]{:S(2)}) collective-permute-start(bf16[2,2,32,768]{3,2,1,0:T(8,128)(2,1)S(1)} %add_convert_fusion), channel_id=1, source_target_pairs={{0,8},{8,0},{1,9},{9,1},{2,10},{10,2},{3,11},{11,3},{4,12},{12,4},... | collective-permute-start | bytes 589832 | tf_op jit(solution)/shard_map/ppermute | solution.py:222
  80.5 0.1 broadcast_select_fusion
  80.6 14.6 %all_to_all.10 = f32[16,8,12]{2,1,0:T(8,128)S(1)} all-to-all(f32[16,8,12]{2,1,0:T(8,128)S(1)} %broadcast_in_dim.62), channel_id=1, replica_groups=mesh['seq_0'=8,'seq_1'=4,'seq_2'=2,'seq_3'=2,'dp'=4] {'seq_2','seq_3','dp'}, dimensions={0} | all-to-all | bytes 12288 | tf_op jit(solution)/shard_map/all_to_all | solution.py:228
  95.2 0.7 broadcast_in_dim.63
  95.9 15.0 %all-to-all-start.1 = ((f32[32,8,12]{2,1,0:T(8,128)}), f32[32,8,12]{2,1,0:T(8,128)S(1)}, u32[]{:S(2)}, u32[]{:S(2)}) async-start(f32[32,8,12]{2,1,0:T(8,128)} %broadcast_in_dim.63), calls=%async_computation.1 | async-start | bytes 262144 | tf_op jit(solution)/shard_map/all_to_all | solution.py:228
  110.9 2.6 %collective-permute-start.8 = (bf16[3,128,768]{2,1,0:T(8,128)(2,1)S(1)}, bf16[3,128,768]{2,1,0:T(8,128)(2,1)S(1)}, u32[]{:S(2)}, u32[]{:S(2)}) collective-permute-start(bf16[3,128,768]{2,1,0:T(8,128)(2,1)S(1)} %get-tuple-element.12), channel_id=1, source_target_pairs={{0,4},{4,0},{1,5},{5,1},{2,6},{6,2},{3,7},{7,3},{8,12},{12,8},{9,1... | collective-permute-start | bytes 1769480 | tf_op jit(solution)/shard_map/ppermute | solution.py:222
  113.5 6.7 %all-to-all-done.1 = f32[32,8,12]{2,1,0:T(8,128)S(1)} async-done(((f32[32,8,12]{2,1,0:T(8,128)}), f32[32,8,12]{2,1,0:T(8,128)S(1)}, u32[]{:S(2)}, u32[]{:S(2)}) %all-to-all-start.1) | async-done | bytes 12320 | tf_op jit(solution)/shard_map/all_to_all | solution.py:228
  120.3 0.1 copy.23
  120.4 0.0 collective-permute-done.11
  120.4 0.0 collective-permute-done.12
  120.4 0.0 collective-permute-done.10
  120.4 1.0 convert_add_fusion
  121.4 4.0 %collective-permute-start.13 = (bf16[2,32,768]{2,1,0:T(8,128)(2,1)S(1)}, bf16[2,32,768]{2,1,0:T(8,128)(2,1)S(1)}, u32[]{:S(2)}, u32[]{:S(2)}) collective-permute-start(bf16[2,32,768]{2,1,0:T(8,128)(2,1)S(1)} %get-tuple-element.30), channel_id=1, source_target_pairs={{0,4},{4,0},{1,5},{5,1},{2,6},{6,2},{3,7},{7,3},{8,12},{12,8},{9,1... | collective-permute-start | bytes 294920 | tf_op jit(solution)/shard_map/ppermute | solution.py:222
  125.4 0.7 copy.21
  126.1 0.2 collective-permute-done.13
  126.3 0.7 maximum_select_fusion.1
  127.1 0.0 collective-permute-done.8
  127.1 1.3 maximum_select_fusion
  (23 shorter events, 0.2 us)
Async XLA Ops:
  0.6 23.6 %copy-start.5 = (s32[1,1,2]{2,1,0:T(1,128)S(1)}, s32[1,1,2]{2,1,0:T(1,128)}, u32[]{:S(2)}) copy-start(s32[1,1,2]{2,1,0:T(1,128)} %param.15) | copy-start | bytes 28
  0.6 33.9 %collective-permute-start.5 = (bf16[2,32,1536]{2,1,0:T(8,128)(2,1)}, bf16[2,32,1536]{2,1,0:T(8,128)(2,1)}, u32[]{:S(2)}, u32[]{:S(2)}) collective-permute-start(bf16[2,32,1536]{2,1,0:T(8,128)(2,1)} %bitcast.43), channel_id=1, source_target_pairs={{0,8},{8,0},{1,9},{9,1},{2,10},{10,2},{3,11},{11,3},{4,12},{12,4},... | collective-permute-start | bytes 589832 | tf_op jit(solution)/shard_map/ppermute | solution.py:222
  12.1 32.9 %collective-permute-start.7 = (bf16[2,32,1536]{2,1,0:T(8,128)(2,1)}, bf16[2,32,1536]{2,1,0:T(8,128)(2,1)}, u32[]{:S(2)}, u32[]{:S(2)}) collective-permute-start(bf16[2,32,1536]{2,1,0:T(8,128)(2,1)} %bitcast.44), channel_id=1, source_target_pairs={{4,20},{12,28},{16,0},{20,36},{24,8},{28,44},{32,16},{36,52},{40,2... | collective-permute-start | bytes 589832 | tf_op jit(solution)/shard_map/ppermute | solution.py:267
  15.9 23.1 %collective-permute-start.1 = (bf16[2,32,1536]{2,1,0:T(8,128)(2,1)}, bf16[2,32,1536]{2,1,0:T(8,128)(2,1)}, u32[]{:S(2)}, u32[]{:S(2)}) collective-permute-start(bf16[2,32,1536]{2,1,0:T(8,128)(2,1)} %bitcast.45), channel_id=1, source_target_pairs={{0,8},{8,0},{1,9},{9,1},{2,10},{10,2},{3,11},{11,3},{4,12},{12,4},... | collective-permute-start | bytes 589832 | tf_op jit(solution)/shard_map/ppermute | solution.py:222
  17.8 33.6 %collective-permute-start.3 = (bf16[2,32,1536]{2,1,0:T(8,128)(2,1)}, bf16[2,32,1536]{2,1,0:T(8,128)(2,1)}, u32[]{:S(2)}, u32[]{:S(2)}) collective-permute-start(bf16[2,32,1536]{2,1,0:T(8,128)(2,1)} %bitcast.46), channel_id=1, source_target_pairs={{4,20},{12,28},{16,0},{20,36},{24,8},{28,44},{32,16},{36,52},{40,2... | collective-permute-start | bytes 589832 | tf_op jit(solution)/shard_map/ppermute | solution.py:268
  21.0 9.0 %copy-start.1 = (bf16[1,3,128,1536]{3,2,1,0:T(8,128)(2,1)S(1)}, bf16[1,3,128,1536]{3,2,1,0:T(8,128)(2,1)}, u32[]{:S(2)}) copy-start(bf16[1,3,128,1536]{3,2,1,0:T(8,128)(2,1)} %mine.3) | copy-start | bytes 3538948
  22.2 7.9 %copy-start.4 = (f32[8,12]{1,0:T(8,128)S(1)}, f32[8,12]{1,0:T(8,128)}, u32[]{:S(2)}) copy-start(f32[8,12]{1,0:T(8,128)} %param.19) | copy-start | bytes 1156
  22.2 35.7 %collective-permute-start.4 = (bf16[3,128,768]{2,1,0:T(8,128)(2,1)S(1)}, bf16[3,128,768]{2,1,0:T(8,128)(2,1)S(1)}, u32[]{:S(2)}, u32[]{:S(2)}) collective-permute-start(bf16[3,128,768]{2,1,0:T(8,128)(2,1)S(1)} %dynamic-slice_bitcast_fusion), channel_id=1, source_target_pairs={{0,4},{4,0},{1,5},{5,1},{2,6},{6,2},{3,7},{7,3},{8,12},{12,8},{9,1... | collective-permute-start | bytes 1769480 | tf_op jit(solution)/shard_map/ppermute | solution.py:222
  24.1 6.2 %copy-start.2 = (bf16[1,2,32,1536]{3,2,1,0:T(8,128)(2,1)S(1)}, bf16[1,2,32,1536]{3,2,1,0:T(8,128)(2,1)}, u32[]{:S(2)}) copy-start(bf16[1,2,32,1536]{3,2,1,0:T(8,128)(2,1)} %param.13) | copy-start | bytes 589828
  27.0 5.4 %copy-start.3 = (bf16[1,2,32,1536]{3,2,1,0:T(8,128)(2,1)S(1)}, bf16[1,2,32,1536]{3,2,1,0:T(8,128)(2,1)}, u32[]{:S(2)}) copy-start(bf16[1,2,32,1536]{3,2,1,0:T(8,128)(2,1)} %param.14) | copy-start | bytes 589828
  34.5 27.1 %collective-permute-start = (bf16[3,128,768]{2,1,0:T(8,128)(2,1)S(1)}, bf16[3,128,768]{2,1,0:T(8,128)(2,1)S(1)}, u32[]{:S(2)}, u32[]{:S(2)}) collective-permute-start(bf16[3,128,768]{2,1,0:T(8,128)(2,1)S(1)} %dynamic-slice_bitcast_fusion.1), channel_id=1, source_target_pairs={{0,4},{4,0},{1,5},{5,1},{2,6},{6,2},{3,7},{7,3},{8,12},{12,8},{9,1... | collective-permute-start | bytes 1769480 | tf_op jit(solution)/shard_map/ppermute | solution.py:222
  39.0 14.7 %collective-permute-start.6 = (bf16[2,32,1536]{2,1,0:T(8,128)(2,1)}, bf16[2,32,1536]{2,1,0:T(8,128)(2,1)S(1)}, u32[]{:S(2)}, u32[]{:S(2)}) collective-permute-start(bf16[2,32,1536]{2,1,0:T(8,128)(2,1)} %collective-permute-done.5), channel_id=1, source_target_pairs={{0,16},{4,20},{16,32},{20,36},{24,8},{28,12},{32,48},{36,52},{40,2... | collective-permute-start | bytes 589832 | tf_op jit(solution)/shard_map/ppermute | solution.py:269
  45.1 12.8 %copy-start = (bf16[1,3,128,1536]{3,2,1,0:T(8,128)(2,1)S(1)}, bf16[1,3,128,1536]{3,2,1,0:T(8,128)(2,1)}, u32[]{:S(2)}) copy-start(bf16[1,3,128,1536]{3,2,1,0:T(8,128)(2,1)} %mine.2) | copy-start | bytes 3538948
  45.1 10.7 %collective-permute-start.2 = (bf16[2,32,1536]{2,1,0:T(8,128)(2,1)}, bf16[2,32,1536]{2,1,0:T(8,128)(2,1)S(1)}, u32[]{:S(2)}, u32[]{:S(2)}) collective-permute-start(bf16[2,32,1536]{2,1,0:T(8,128)(2,1)} %collective-permute-done.1), channel_id=1, source_target_pairs={{0,16},{4,20},{16,32},{20,36},{24,8},{28,12},{32,48},{36,52},{40,2... | collective-permute-start | bytes 589832 | tf_op jit(solution)/shard_map/ppermute | solution.py:270
  68.2 8.0 %collective-permute-start.9 = (bf16[2,2,32,768]{3,2,1,0:T(8,128)(2,1)S(1)}, bf16[2,2,32,768]{3,2,1,0:T(8,128)(2,1)S(1)}, u32[]{:S(2)}, u32[]{:S(2)}) collective-permute-start(bf16[2,2,32,768]{3,2,1,0:T(8,128)(2,1)S(1)} %get-tuple-element.15), channel_id=1, source_target_pairs={{16,0},{20,4},{32,16},{36,20},{8,24},{12,28},{48,32},{52,36},{24,4... | collective-permute-start | bytes 589832 | tf_op jit(solution)/shard_map/ppermute | solution.py:311
  69.5 50.9 %collective-permute-start.11 = (bf16[2,32,768]{2,1,0:T(8,128)(2,1)S(1)}, bf16[2,32,768]{2,1,0:T(8,128)(2,1)S(1)}, u32[]{:S(2)}, u32[]{:S(2)}) collective-permute-start(bf16[2,32,768]{2,1,0:T(8,128)(2,1)S(1)} %get-tuple-element.31), channel_id=1, source_target_pairs={{0,16},{4,20},{8,24},{12,28},{16,32},{20,36},{24,40},{28,44},{32,4... | collective-permute-start | bytes 294920 | tf_op jit(solution)/shard_map/ppermute | solution.py:312
  73.5 46.9 %collective-permute-start.12 = (bf16[2,32,768]{2,1,0:T(8,128)(2,1)S(1)}, bf16[2,32,768]{2,1,0:T(8,128)(2,1)}, u32[]{:S(2)}, u32[]{:S(2)}) collective-permute-start(bf16[2,32,768]{2,1,0:T(8,128)(2,1)S(1)} %get-tuple-element.32), channel_id=1, source_target_pairs={{16,0},{20,4},{24,8},{28,12},{32,16},{36,20},{40,24},{44,28},{48,3... | collective-permute-start | bytes 294920 | tf_op jit(solution)/shard_map/ppermute | solution.py:313
  76.2 44.2 %collective-permute-start.10 = (bf16[2,2,32,768]{3,2,1,0:T(8,128)(2,1)S(1)}, bf16[2,2,32,768]{3,2,1,0:T(8,128)(2,1)S(1)}, u32[]{:S(2)}, u32[]{:S(2)}) collective-permute-start(bf16[2,2,32,768]{3,2,1,0:T(8,128)(2,1)S(1)} %add_convert_fusion), channel_id=1, source_target_pairs={{0,8},{8,0},{1,9},{9,1},{2,10},{10,2},{3,11},{11,3},{4,12},{12,4},... | collective-permute-start | bytes 589832 | tf_op jit(solution)/shard_map/ppermute | solution.py:222
  95.9 24.4 %all-to-all-start.1 = ((f32[32,8,12]{2,1,0:T(8,128)}), f32[32,8,12]{2,1,0:T(8,128)S(1)}, u32[]{:S(2)}, u32[]{:S(2)}) async-start(f32[32,8,12]{2,1,0:T(8,128)} %broadcast_in_dim.63), calls=%async_computation.1 | async-start | bytes 262144 | tf_op jit(solution)/shard_map/all_to_all | solution.py:228
  110.9 16.1 %collective-permute-start.8 = (bf16[3,128,768]{2,1,0:T(8,128)(2,1)S(1)}, bf16[3,128,768]{2,1,0:T(8,128)(2,1)S(1)}, u32[]{:S(2)}, u32[]{:S(2)}) collective-permute-start(bf16[3,128,768]{2,1,0:T(8,128)(2,1)S(1)} %get-tuple-element.12), channel_id=1, source_target_pairs={{0,4},{4,0},{1,5},{5,1},{2,6},{6,2},{3,7},{7,3},{8,12},{12,8},{9,1... | collective-permute-start | bytes 1769480 | tf_op jit(solution)/shard_map/ppermute | solution.py:222
  121.4 4.9 %collective-permute-start.13 = (bf16[2,32,768]{2,1,0:T(8,128)(2,1)S(1)}, bf16[2,32,768]{2,1,0:T(8,128)(2,1)S(1)}, u32[]{:S(2)}, u32[]{:S(2)}) collective-permute-start(bf16[2,32,768]{2,1,0:T(8,128)(2,1)S(1)} %get-tuple-element.30), channel_id=1, source_target_pairs={{0,4},{4,0},{1,5},{5,1},{2,6},{6,2},{3,7},{7,3},{8,12},{12,8},{9,1... | collective-permute-start | bytes 294920 | tf_op jit(solution)/shard_map/ppermute | solution.py:222

commit v2 on v1

--- a/solution.py
+++ b/solution.py
@@ -45,9 +45,13 @@
     q = (mine[0, 0, :, lanes], other[0, :, lanes])
     k = (mine[0, 1, :, lanes], other[1, :, lanes])
     v = (mine[0, 2, :, lanes], other[2, :, lanes])
-    ka = jnp.concatenate([ref[b, 0, :, lanes] for ref in audio for b in range(2)], axis=0)
-    va = jnp.concatenate([ref[b, 1, :, lanes] for ref in audio for b in range(2)], axis=0)
-    return q, k, v, ka, va
+    own, zed, far, same, opposite = audio
+
+    def window(i):
+        pieces = [ref[b, i, :, lanes] for ref in (own, zed, far) for b in range(2)]
+        return jnp.concatenate(pieces + [same[i, :, lanes], opposite[i, :, lanes]], axis=0)
+
+    return q, k, v, window(0), window(1)
 
 
 def scores_of(q, k, ka, scale, bias, rows):
@@ -68,11 +72,11 @@
     return by_block(lambda vb, pb: dot(vb, pb, 0, 0), v, halves(local)) + dot(va, audio, 0, 0)
 
 
-def teacher_kernel(dim, core, bias, scal, mine, other, own, zed, far, nat, target):
+def teacher_kernel(dim, core, bias, scal, mine, other, own, zed, far, same, opposite, target):
     rows = own.shape[2]
     for i in range(target.shape[0]):
         lanes = slice(i * dim, (i + 1) * dim)
-        q, k, v, ka, va = load_head(lanes, mine, other, (own, zed, far, nat))
+        q, k, v, ka, va = load_head(lanes, mine, other, (own, zed, far, same, opposite))
         local, audio = scores_of(q, k, ka, dim**-0.5, bias, rows)
         plain_max = column_max(local)
         plain = jnp.exp(local - plain_max)
@@ -98,14 +102,15 @@
     own,
     zed,
     far,
-    nat,
+    same,
+    opposite,
     target,
     grad_mine,
     grad_other,
     own_out,
     zed_out,
     far_out,
-    nat_out,
+    opposite_out,
     totals,
 ):
     rows = own.shape[2]
@@ -113,7 +118,7 @@
     heads = target.shape[0]
     for i in range(heads):
         lanes = slice(i * dim, (i + 1) * dim)
-        q, k, v, ka, va = load_head(lanes, mine, other, (own, zed, far, nat))
+        q, k, v, ka, va = load_head(lanes, mine, other, (own, zed, far, same, opposite))
         local, audio = scores_of(q, k, ka, scale, bias, rows)
         highest = jnp.maximum(column_max(local), column_max(audio))
         local = jnp.exp(local - highest)
@@ -141,26 +146,29 @@
         vb = query_grad.shape[0] // 2
         score_halves = halves(local_grad)
         prob_halves = halves(local_round)
-        for b, ref in enumerate((grad_mine, grad_other)):
-            ref[0, :, lanes] = query_grad[b * vb : (b + 1) * vb]
-            ref[1, :, lanes] = dot(score_halves[b], q[b], 1, 0).astype(jnp.bfloat16)
-            ref[2, :, lanes] = dot(prob_halves[b], grads[b], 1, 1).astype(jnp.bfloat16)
+        for b, (ref, first) in enumerate(((grad_mine, (0,)), (grad_other, ()))):
+            ref[(*first, 0, slice(None), lanes)] = query_grad[b * vb : (b + 1) * vb]
+            key_grad = dot(score_halves[b], q[b], 1, 0)
+            ref[(*first, 1, slice(None), lanes)] = key_grad.astype(jnp.bfloat16)
+            value_grad = dot(prob_halves[b], grads[b], 1, 1)
+            ref[(*first, 2, slice(None), lanes)] = value_grad.astype(jnp.bfloat16)
         audio_keys = dot(audio_grad, jnp.concatenate(q, axis=0), 1, 0)
         audio_values = dot(audio_round, out_grad, 1, 1)
-        for slot in range(SLOTS):
-            ref = (own_out, zed_out, far_out, nat_out)[slot // 2]
+        places = [(own_out, 0), (own_out, 1), (zed_out, 0), (zed_out, 1)]
+        places += [(far_out, 0), (far_out, 1), (far_out, 2), (opposite_out, 0)]
+        for slot, (ref, b) in enumerate(places):
             at = slice(slot * rows, (slot + 1) * rows)
-            ref[slot % 2, 0, :, lanes] = audio_keys[at].astype(ref.dtype)
-            ref[slot % 2, 1, :, lanes] = audio_values[at].astype(ref.dtype)
-
-
-def specs(steps, width, vb, rows):
+            ref[b, 0, :, lanes] = audio_keys[at].astype(ref.dtype)
+            ref[b, 1, :, lanes] = audio_values[at].astype(ref.dtype)
+
+
+def specs(steps, width, vb, rows, which):
     smem = pl.BlockSpec(memory_space=pltpu.SMEM)
     mine = pl.BlockSpec((1, 3, vb, width), lambda h, c: (0, 0, 0, c[0] * steps + h))
     video = pl.BlockSpec((3, vb, width), lambda h, c: (0, 0, h))
-    window = pl.BlockSpec((2, 2, rows, width), lambda h, c: (0, 0, 0, c[0] * steps + h))
-    piece = pl.BlockSpec((2, 2, rows, width), lambda h, c: (0, 0, 0, h))
-    return smem, mine, video, window, piece
+    pair = pl.BlockSpec((2, 2, rows, width), lambda h, c: (0, 0, 0, h))
+    single = pl.BlockSpec((2, rows, width), lambda h, c: (which, 0, h))
+    return smem, mine, video, pair, single
 
 
 def teacher_call(core, bias, scal, mine, other, audio, head_dim):
@@ -168,14 +176,14 @@
     rows = audio[0].shape[2]
     width = STEP_HEADS * head_dim
     steps = half_width // width
-    smem, own_video, video, window, _ = specs(steps, width, vb, rows)
+    smem, own_video, video, pair, single = specs(steps, width, vb, rows, 0)
     heads = half_width // head_dim
     return pl.pallas_call(
         functools.partial(teacher_kernel, head_dim),
         grid_spec=pltpu.PrefetchScalarGridSpec(
             num_scalar_prefetch=1,
             grid=(steps,),
-            in_specs=[smem, smem, own_video, video] + [window] * 4,
+            in_specs=[smem, smem, own_video, video] + [pair] * 3 + [single] * 2,
             out_specs=pl.BlockSpec((STEP_HEADS, head_dim, 2 * vb), lambda h, c: (h, 0, 0)),
         ),
         out_shape=jax.ShapeDtypeStruct((heads, head_dim, 2 * vb), jnp.float32),
@@ -192,24 +200,37 @@
     rows = audio[0].shape[2]
     width = STEP_HEADS * head_dim
     steps = half_width // width
-    smem, own_video, video, window, piece = specs(steps, width, vb, rows)
+    smem, own_video, video, pair, single = specs(steps, width, vb, rows, 1)
     heads = half_width // head_dim
-    video_shape = jax.ShapeDtypeStruct((3, vb, half_width), jnp.bfloat16)
-    wide = jax.ShapeDtypeStruct((2, 2, rows, half_width), jnp.float32)
-    narrow = jax.ShapeDtypeStruct((2, 2, rows, half_width), jnp.bfloat16)
+
+    def blocks(n, dtype):
+        shape = jax.ShapeDtypeStruct((n, 2, rows, half_width), dtype)
+        return shape, pl.BlockSpec((n, 2, rows, width), lambda h, c: (0, 0, 0, h))
+
+    outs = [
+        (jax.ShapeDtypeStruct(mine.shape, jnp.bfloat16), own_video),
+        (jax.ShapeDtypeStruct(other.shape, jnp.bfloat16), video),
+        blocks(2, jnp.float32),
+        blocks(2, jnp.float32),
+        blocks(3, jnp.bfloat16),
+        blocks(1, jnp.bfloat16),
+        (
+            jax.ShapeDtypeStruct((heads, 8, vb), jnp.float32),
+            pl.BlockSpec((STEP_HEADS, 8, vb), lambda h, c: (h, 0, 0)),
+        ),
+    ]
     return pl.pallas_call(
         functools.partial(student_kernel, head_dim),
         grid_spec=pltpu.PrefetchScalarGridSpec(
             num_scalar_prefetch=1,
             grid=(steps,),
             in_specs=[smem, smem, own_video, video]
-            + [window] * 4
+            + [pair] * 3
+            + [single] * 2
             + [pl.BlockSpec((STEP_HEADS, head_dim, 2 * vb), lambda h, c: (h, 0, 0))],
-            out_specs=[video, video, piece, piece, piece, piece]
-            + [pl.BlockSpec((STEP_HEADS, 8, vb), lambda h, c: (h, 0, 0))],
-        ),
-        out_shape=[video_shape, video_shape, wide, wide, narrow, narrow]
-        + [jax.ShapeDtypeStruct((heads, 8, vb), jnp.float32)],
+            out_specs=[spec for _, spec in outs],
+        ),
+        out_shape=[shape for shape, _ in outs],
         compiler_params=pltpu.CompilerParams(vmem_limit_bytes=VMEM),
         cost_estimate=pl.CostEstimate(
             flops=900_000_000, bytes_accessed=8_000_000, transcendentals=600_000
@@ -257,38 +278,45 @@
     def inside(pairs):
         return [(a, b) for a, b in pairs if 0 <= b < count]
 
-    near_pairs = inside((i, i + group if i % 2 else i - group) for i in places)
     far_out = inside((i, i - group if (i // 2) % 2 else i + group) for i in places)
     far_back = [(b, a) for a, b in far_out]
 
-    teach, pupil = teacher_audio[0], student_audio[0]
-    teach_zed = swap(teach, HALF)
-    pupil_zed = swap(pupil, HALF)
-    teach_nat = lax.ppermute(teach, SEQ, near_pairs)
-    pupil_nat = lax.ppermute(pupil, SEQ, near_pairs)
-    teach_far = lax.ppermute(teach_zed, SEQ, far_out)
-    pupil_far = lax.ppermute(pupil_zed, SEQ, far_out)
-
-    def sibling(video):
-        return swap(lax.dynamic_slice_in_dim(video[0], (1 - core) * half_width, half_width, 2), CORE)
-
-    teach_other = sibling(teacher_video)
-    pupil_other = sibling(student_video)
+    def part(x, which):
+        return lax.dynamic_slice_in_dim(x, which * half_width, half_width, x.ndim - 1)
+
+    audio = jnp.concatenate([teacher_audio[0], student_audio[0]], axis=0)
+    got = swap(part(audio, 1 - core), CORE)
+    kept = part(audio, core)
+    pairs = [jnp.stack([kept[i : i + 2], got[i : i + 2]]) for i in (0, 2)]
+    inner = core == half
+    zeds = [swap(pair, HALF) for pair in pairs]
+    zeds[0], teacher_video, student_video, alignment = lax.optimization_barrier(
+        (zeds[0], teacher_video, student_video, alignment)
+    )
+    same = lax.ppermute(jnp.where(inner, got, kept), SEQ, far_out)
+    opposite = lax.ppermute(jnp.where(inner, kept, got), SEQ, far_back)
+    fars = [lax.ppermute(zed, SEQ, far_out) for zed in zeds]
+
+    teach_other = swap(part(teacher_video[0], 1 - core), CORE)
+    pupil_other = swap(part(student_video[0], 1 - core), CORE)
     spans = lax.all_gather(alignment[0, 0], CORE)
 
-    def both(pieces):
-        return [lax.all_gather(piece, CORE) for piece in pieces]
-
-    teach_window = both((teach, teach_zed, teach_far, teach_nat))
-    pupil_window = both((pupil, pupil_zed, pupil_far, pupil_nat))
-
     side = 2 - 4 * half
-    owners = base + jnp.stack(
-        [jnp.int32(0), jnp.int32(1), side, side + 1, -side, 1 - side, jnp.int32(4), jnp.int32(-3)]
-    )
-    order = jnp.stack([core, 1 - core])
-    first = jnp.take(spans[:, 0], order)[None, :]
-    length = jnp.take(spans[:, 1], order)[None, :]
+    near = 7 * half
+    owners = jnp.stack(
+        [
+            base + core,
+            base + 1 - core,
+            base + side + core,
+            base + side + 1 - core,
+            base - side + core,
+            base - side + 1 - core,
+            base - 3 + near,
+            base + 4 - near,
+        ]
+    )
+    span = jnp.where(core == 0, spans, spans[::-1])
+    first, length = span[None, :, 0], span[None, :, 1]
     used = (owners[:, None] >= first) & (owners[:, None] < first + length) & (null_flag[0] == 0)
     bias = jnp.where(used, 0.0, -jnp.inf).astype(jnp.float32).reshape(2 * SLOTS)
 
@@ -303,29 +331,11 @@
     scal = jnp.concatenate([jnp.stack([weight, loss_weight]), factor])
     which = core.astype(jnp.int32)[None]
 
-    target = teacher_call(which, bias, scal, teacher_video, teach_other, teach_window, head_dim)
-    grad_mine, grad_other, own, zed, far, nat, totals = student_call(
-        which, bias, scal, student_video, pupil_other, pupil_window, target, head_dim
-    )
-
-    far_in = lax.ppermute(far, SEQ, far_back)
-    next_in = lax.ppermute(nat[0], SEQ, inside((i, i + group) for i in places))
-    prev_in = lax.ppermute(nat[1], SEQ, inside((i, i - group) for i in places))
-    zed_in = swap((zed + far_in.astype(jnp.float32)).astype(jnp.bfloat16), HALF)
-    own = own + zed_in.astype(jnp.float32)
-    own = own + jnp.stack([next_in, prev_in]).astype(jnp.float32)
-    leave = lax.dynamic_index_in_dim(own, 1 - core, 0, keepdims=False).astype(jnp.bfloat16)
-    keep = lax.dynamic_index_in_dim(own, core, 0, keepdims=False).astype(jnp.bfloat16)
-
-    def joined(mine, other):
-        return jnp.where(
-            core == 0,
-            jnp.concatenate([mine, other], axis=-1),
-            jnp.concatenate([other, mine], axis=-1),
-        )[None]
-
-    grad_audio = joined(keep, swap(leave, CORE))
-    grad_video = joined(grad_mine, swap(grad_other, CORE))
+    windows = [(pair, zed, far, same, opposite) for pair, zed, far in zip(pairs, zeds, fars)]
+    target = teacher_call(which, bias, scal, teacher_video, teach_other, windows[0], head_dim)
+    grad_video, grad_other, own, zed, far, opposite, totals = student_call(
+        which, bias, scal, student_video, pupil_other, windows[1], target, head_dim
+    )
 
     sums = jnp.sum(totals, axis=(1, 2))
     head_totals = lax.dynamic_update_slice_in_dim(
@@ -334,7 +344,28 @@
     contribution = jnp.where(
         levels[:, None] == level_index, head_totals[None, :], jnp.zeros_like(gamma)
     )
-    gamma_grad = everywhere(everywhere(contribution, COLUMN), PLANE) / (tokens * count * head_dim)
+    far_in = lax.ppermute(far, SEQ, far_back)
+    far_in, contribution = lax.optimization_barrier((far_in, everywhere(contribution, COLUMN)))
+    far_in = far_in.astype(jnp.float32)
+    opposite_in = lax.ppermute(opposite[0], SEQ, far_out).astype(jnp.float32)
+    zed_in = swap((zed + far_in[:2]).astype(jnp.bfloat16), HALF)
+    zed_in, gamma_grad = lax.optimization_barrier((zed_in, everywhere(contribution, PLANE)))
+    zed_in = zed_in.astype(jnp.float32)
+    near_in = (far_in[2], opposite_in)
+    keep = own[0] + jnp.where(inner, near_in[1], near_in[0])
+    leave = own[1] + jnp.where(inner, near_in[0], near_in[1])
+    keep = (keep + zed_in[0]).astype(jnp.bfloat16)
+    arrived = swap((leave + zed_in[1]).astype(jnp.bfloat16), CORE)
+    grad_audio = jnp.where(
+        core == 0,
+        jnp.concatenate([keep, arrived], axis=-1),
+        jnp.concatenate([arrived, keep], axis=-1),
+    )[None]
+    grad_video = lax.dynamic_update_slice_in_dim(
+        grad_video, swap(grad_other, CORE)[None], (1 - core) * half_width, 3
+    )
+
+    gamma_grad = gamma_grad / (tokens * count * head_dim)
     return (grad_video, grad_audio, gamma_grad)
 
 

time: 129 us -> 116 us (0.90)
  blocking collectives: 34.6 us -> 25 us
  starting transfers between devices: 64.2 us -> 57.1 us
  other arithmetic: 3.69 us -> 6.1 us
  local copies, waits for them, and re-layouts: 4.68 us -> 6.28 us
  waiting for transfers between devices: 8.04 us -> 6.64 us
    all_gather x8 -> x0, blocking collectives: 18 us -> none  [both(): return [lax.all_gather(piece, CORE) for piece in pieces]]
    all_to_all x1, blocking collectives: 14.6 us -> 23.3 us  [everywhere(): return jnp.sum(lax.all_to_all(copies, axes, 0, 0), axis=0)]
    ppermute x6 -> x5, starting transfers between devices: 19.5 us -> 12.7 us  [the longest x2 4.64 us: body(): fars = [lax.ppermute(zed, SEQ, far_out) for zed in zeds]]
    all_to_all x1, starting transfers between devices: 15 us -> 8.5 us  [everywhere(): return jnp.sum(lax.all_to_all(copies, axes, 0, 0), axis=0)]
    ppermute x7 -> x8, starting transfers between devices: 28.3 us -> 34.6 us  [swap(): return lax.ppermute(x, axis, [(0, 1), (1, 0)])]
  transfers between devices with their start and end apart: 15 -> 15, of which waited for: 3 -> 4; matrix products, arithmetic and copies ran while one was open for 5% -> 7% of each run, Pallas kernels for 3% -> 3%
where the time goes in v2:
time: 116 us; the launch traced here: 115 us
  starting transfers between devices  57.1 us (49%)
  blocking collectives  25 us (22%)
  Pallas kernels  11.4 us (10%)
  waiting for transfers between devices  6.64 us (6%)
  local copies, waits for them, and re-layouts  6.28 us (5%)
  other arithmetic  6.1 us (5%)
  between operations  2.93 us (3%)
    ppermute x8, starting transfers between devices, swap(): return lax.ppermute(x, axis, [(0, 1), (1, 0)])  34.6 us
    all_to_all x1, blocking collectives, everywhere(): return jnp.sum(lax.all_to_all(copies, axes, 0, 0), axis=0)  23.3 us
    all_to_all x1, starting transfers between devices, everywhere(): return jnp.sum(lax.all_to_all(copies, axes, 0, 0), axis=0)  8.5 us
    pallas_call x1, Pallas kernels, student_call(): pl.pallas_call(functools.partial(student_kernel, head_dim), grid_spec=plt...  7.47 us
    all_to_all x1, waiting for transfers between devices, everywhere(): return jnp.sum(lax.all_to_all(copies, axes, 0, 0), axis=0)  5.9 us
    ppermute x2, starting transfers between devices, body(): fars = [lax.ppermute(zed, SEQ, far_out) for zed in zeds]  4.64 us
    pallas_call x1, Pallas kernels, teacher_call(): pl.pallas_call(functools.partial(teacher_kernel, head_dim), grid_spec=plt...  3.91 us
    ppermute x1, starting transfers between devices, body(): opposite_in = lax.ppermute(opposite[0], SEQ, far_out).astype(jnp.float32)  3.68 us
  transfers between devices with their start and end apart: 15, of which 4 were waited for; matrix products, arithmetic and copies ran while one was open for 7% of the time, Pallas kernels for 3%

profile of v2, /device:TPU:1, one launch (start us, length us, event | category | flops | bytes accessed | tf_op | source)
XLA Modules:
  0.0 115.5 jit_solution(4239795489885942391)
XLA Ops:
  0.6 1.0 fusion.7
  1.6 8.8 %collective-permute-start = (bf16[4,32,768]{2,1,0:T(8,128)(2,1)S(1)}, bf16[4,32,768]{2,1,0:T(8,128)(2,1)S(1)}, u32[]{:S(2)}, u32[]{:S(2)}) collective-permute-start(bf16[4,32,768]{2,1,0:T(8,128)(2,1)S(1)} %fusion.7), channel_id=1, source_target_pairs={{0,4},{4,0},{1,5},{5,1},{2,6},{6,2},{3,7},{7,3},{8,12},{12,8},{9,1... | collective-permute-start | bytes 589832 | tf_op jit(solution)/shard_map/ppermute | solution.py:243
  12.4 0.8 select_reduce_fusion
  13.2 0.1 dynamic_slice.21
  13.3 0.6 stack.57
  13.9 0.1 pad_maximum_fusion.2.scal
  14.0 0.0 collective-permute-done
  14.0 1.7 %broadcast_select_fusion = (bf16[4,32,768]{2,1,0:T(8,128)(2,1)}, bf16[4,32,768]{2,1,0:T(8,128)(2,1)S(1)}) fusion(bf16[4,32,768]{2,1,0:T(8,128)(2,1)S(1)} %collective-permute-done, pred[]{:T(512)S(6)} %eq.31, s32[]{:T(128)S(6)} %select_n.81, bf16[2,32,1536]{2,1,0:T(8,128)(2,1)} %bitcast.63, bf16[2,32,1536]{2,1,0:T(8,128)(2,1)} %bitcast.61), kind=kLoop, calls=%fused_computation.25 | loop fusion | flops 491520 | bytes 983045 | tf_op jit(solution)/shard_map/jit(_where)/select_n | solution.py:297
  15.7 0.0 copy-start.1
  15.7 5.4 %collective-permute-start.1 = (bf16[2,2,32,768]{3,2,1,0:T(8,128)(2,1)S(1)}, bf16[2,2,32,768]{3,2,1,0:T(8,128)(2,1)S(1)}, u32[]{:S(2)}, u32[]{:S(2)}) collective-permute-start(bf16[2,2,32,768]{3,2,1,0:T(8,128)(2,1)S(1)} %pad_maximum_fusion.own), channel_id=1, source_target_pairs={{0,8},{8,0},{1,9},{9,1},{2,10},{10,2},{3,11},{11,3},{4,12},{12,4},... | collective-permute-start | bytes 589832 | tf_op jit(solution)/shard_map/ppermute | solution.py:243
  21.1 0.7 broadcast_select_fusion.1
  21.8 3.1 %collective-permute-start.5 = (bf16[4,32,768]{2,1,0:T(8,128)(2,1)}, bf16[4,32,768]{2,1,0:T(8,128)(2,1)S(1)}, u32[]{:S(2)}, u32[]{:S(2)}) collective-permute-start(bf16[4,32,768]{2,1,0:T(8,128)(2,1)} %broadcast_select_fusion.1), channel_id=1, source_target_pairs={{0,16},{4,20},{16,32},{20,36},{24,8},{28,12},{32,48},{36,52},{40,2... | collective-permute-start | bytes 589832 | tf_op jit(solution)/shard_map/ppermute | solution.py:296
  25.0 1.3 %collective-permute-start.6 = (bf16[4,32,768]{2,1,0:T(8,128)(2,1)}, bf16[4,32,768]{2,1,0:T(8,128)(2,1)S(1)}, u32[]{:S(2)}, u32[]{:S(2)}) collective-permute-start(bf16[4,32,768]{2,1,0:T(8,128)(2,1)} %get-tuple-element.44), channel_id=1, source_target_pairs={{16,0},{20,4},{32,16},{36,20},{8,24},{12,28},{48,32},{52,36},{24,4... | collective-permute-start | bytes 589832 | tf_op jit(solution)/shard_map/ppermute | solution.py:297
  26.3 0.0 copy-start.4
  26.3 4.8 %collective-permute-start.3 = (bf16[2,2,32,768]{3,2,1,0:T(8,128)(2,1)S(1)}, bf16[2,2,32,768]{3,2,1,0:T(8,128)(2,1)S(1)}, u32[]{:S(2)}, u32[]{:S(2)}) collective-permute-start(bf16[2,2,32,768]{3,2,1,0:T(8,128)(2,1)S(1)} %pad_maximum_fusion.1.own), channel_id=1, source_target_pairs={{0,8},{8,0},{1,9},{9,1},{2,10},{10,2},{3,11},{11,3},{4,12},{12,4},... | collective-permute-start | bytes 589832 | tf_op jit(solution)/shard_map/ppermute | solution.py:243
  31.1 0.0 collective-permute-done.1.zed
  31.1 0.0 copy-done
  31.1 0.9 dynamic-slice_bitcast_fusion
  32.0 3.0 %collective-permute-start.7 = (bf16[3,128,768]{2,1,0:T(8,128)(2,1)}, bf16[3,128,768]{2,1,0:T(8,128)(2,1)}, u32[]{:S(2)}, u32[]{:S(2)}) collective-permute-start(bf16[3,128,768]{2,1,0:T(8,128)(2,1)} %dynamic-slice_bitcast_fusion), channel_id=1, source_target_pairs={{0,4},{4,0},{1,5},{5,1},{2,6},{6,2},{3,7},{7,3},{8,12},{12,8},{9,1... | collective-permute-start | bytes 1769480 | tf_op jit(solution)/shard_map/ppermute | solution.py:243
  35.0 0.0 copy-done.1
  35.0 0.9 dynamic-slice_bitcast_fusion.1
  35.9 0.0 copy-done.4
  35.9 1.8 %all-gather = s32[2,1,2]{2,1,0:T(1,128)S(1)} all-gather(s32[1,1,2]{2,1,0:T(1,128)S(1)} %copy-done.4), channel_id=2, replica_groups=mesh['seq_0'=8,'seq_1'=4,'seq_2'=2,'seq_3'=2,'dp'=4] {'seq_3'}, dimensions={0}, use_global_device_ids=true | all-gather | bytes 24 | tf_op jit(solution)/shard_map/all_gather | solution.py:302
  37.7 2.1 %collective-permute-start.2 = (bf16[3,128,768]{2,1,0:T(8,128)(2,1)}, bf16[3,128,768]{2,1,0:T(8,128)(2,1)}, u32[]{:S(2)}, u32[]{:S(2)}) collective-permute-start(bf16[3,128,768]{2,1,0:T(8,128)(2,1)} %dynamic-slice_bitcast_fusion.1), channel_id=1, source_target_pairs={{0,4},{4,0},{1,5},{5,1},{2,6},{6,2},{3,7},{7,3},{8,12},{12,8},{9,1... | collective-permute-start | bytes 1769480 | tf_op jit(solution)/shard_map/ppermute | solution.py:243
  39.8 0.2 slice_reduce_fusion
  40.0 0.0 collective-permute-done.5.same
  40.0 2.3 %collective-permute-start.8 = (bf16[2,2,32,768]{3,2,1,0:T(8,128)(2,1)S(1)}, bf16[2,2,32,768]{3,2,1,0:T(8,128)(2,1)}, u32[]{:S(2)}, u32[]{:S(2)}) collective-permute-start(bf16[2,2,32,768]{3,2,1,0:T(8,128)(2,1)S(1)} %collective-permute-done.1.zed), channel_id=1, source_target_pairs={{0,16},{4,20},{16,32},{20,36},{24,8},{28,12},{32,48},{36,52},{40,2... | collective-permute-start | bytes 589832 | tf_op jit(solution)/shard_map/ppermute | solution.py:298
  42.4 0.0 collective-permute-done.3.zed
  42.4 2.3 %collective-permute-start.4 = (bf16[2,2,32,768]{3,2,1,0:T(8,128)(2,1)S(1)}, bf16[2,2,32,768]{3,2,1,0:T(8,128)(2,1)}, u32[]{:S(2)}, u32[]{:S(2)}) collective-permute-start(bf16[2,2,32,768]{3,2,1,0:T(8,128)(2,1)S(1)} %collective-permute-done.3.zed), channel_id=1, source_target_pairs={{0,16},{4,20},{16,32},{20,36},{24,8},{28,12},{32,48},{36,52},{40,2... | collective-permute-start | bytes 589832 | tf_op jit(solution)/shard_map/ppermute | solution.py:298
  44.7 0.7 and_select_fusion
  45.4 0.1 select_n.85.bias
  45.4 0.0 collective-permute-done.6.opposite
  45.4 0.2 collective-permute-done.8.far
  45.6 0.0 collective-permute-done.7.other
  45.6 3.9 %teacher.1.target = f32[6,128,256]{2,1,0:T(8,128)S(1)} custom-call(s32[1]{0:T(128)} %bitcast.core, f32[16]{0:T(128)S(1)} %select_n.85.bias, f32[8]{0:T(128)S(1)} %pad_maximum_fusion.2.scal, bf16[1,3,128,1536]{3,2,1,0:T(8,128)(2,1)S(1)} %copy-done, bf16[3,128,768]{2,1,0:T(8,128)(2,1)} %collective-permute-done.7.other, ...), custom_call_target="tpu_custom_call" | custom-call | flops 600000000 | bytes 4000000 | tf_op jit(solution)/shard_map/teacher/pallas_call | solution.py:181
  49.6 0.3 collective-permute-done.4.far
  49.8 0.0 collective-permute-done.2.other
  49.8 7.5 %student.1 = (bf16[1,3,128,1536]{3,2,1,0:T(8,128)(2,1)}, bf16[3,128,768]{2,1,0:T(8,128)(2,1)S(1)}, f32[2,2,32,768]{3,2,1,0:T(8,128)S(1)}, f32[2,2,32,768]{3,2,1,...) custom-call(s32[1]{0:T(128)} %bitcast.core, ...), custom_call_target="tpu_custom_call" | custom-call | flops 900000000 | bytes 8000000 | tf_op jit(solution)/shard_map/student/pallas_call | solution.py:222
  57.3 0.8 copy-done.2
  58.1 1.3 %collective-permute-start.11 = (bf16[3,2,32,768]{3,2,1,0:T(8,128)(2,1)}, bf16[3,2,32,768]{3,2,1,0:T(8,128)(2,1)S(1)}, u32[]{:S(2)}, u32[]{:S(2)}) collective-permute-start(bf16[3,2,32,768]{3,2,1,0:T(8,128)(2,1)} %get-tuple-element.26), channel_id=1, source_target_pairs={{16,0},{20,4},{32,16},{36,20},{8,24},{12,28},{48,32},{52,36},{24,4... | collective-permute-start | bytes 884744 | tf_op jit(solution)/shard_map/ppermute | solution.py:347
  59.4 0.1 reduce_sum.37
  59.6 0.2 dynamic_update_slice.18
  59.8 0.1 broadcast_select_fusion.2
  59.9 23.3 %all_to_all.10 = f32[16,8,12]{2,1,0:T(8,128)S(1)} all-to-all(f32[16,8,12]{2,1,0:T(8,128)S(1)} %broadcast_in_dim.60), channel_id=1, replica_groups=mesh['seq_0'=8,'seq_1'=4,'seq_2'=2,'seq_3'=2,'dp'=4] {'seq_2','seq_3','dp'}, dimensions={0} | all-to-all | bytes 12288 | tf_op jit(solution)/shard_map/all_to_all | solution.py:249
  83.2 0.1 copy.22
  83.3 0.0 collective-permute-done.11
  83.4 2.5 %collective-permute-start.12 = (bf16[2,2,32,768]{3,2,1,0:T(8,128)(2,1)S(1)}, bf16[2,2,32,768]{3,2,1,0:T(8,128)(2,1)S(1)}, u32[]{:S(2)}, u32[]{:S(2)}) collective-permute-start(bf16[2,2,32,768]{3,2,1,0:T(8,128)(2,1)S(1)} %fusion), channel_id=1, source_target_pairs={{0,8},{8,0},{1,9},{9,1},{2,10},{10,2},{3,11},{11,3},{4,12},{12,4},... | collective-permute-start | bytes 589832 | tf_op jit(solution)/shard_map/ppermute | solution.py:243
  85.8 3.7 %collective-permute-start.10 = (bf16[2,32,768]{2,1,0:T(8,128)(2,1)S(1)}, bf16[2,32,768]{2,1,0:T(8,128)(2,1)S(1)}, u32[]{:S(2)}, u32[]{:S(2)}) collective-permute-start(bf16[2,32,768]{2,1,0:T(8,128)(2,1)S(1)} %bitcast.59), channel_id=1, source_target_pairs={{0,16},{4,20},{16,32},{20,36},{24,8},{28,12},{32,48},{36,52},{40,2... | collective-permute-start | bytes 294920 | tf_op jit(solution)/shard_map/ppermute | solution.py:350
  89.5 0.1 copy.19
  89.6 0.7 broadcast_in_dim.61
  90.3 8.5 %all-to-all-start.1 = ((f32[32,8,12]{2,1,0:T(8,128)}), f32[32,8,12]{2,1,0:T(8,128)S(1)}, u32[]{:S(2)}, u32[]{:S(2)}) async-start(f32[32,8,12]{2,1,0:T(8,128)} %broadcast_in_dim.61), calls=%async_computation.1 | async-start | bytes 262144 | tf_op jit(solution)/shard_map/all_to_all | solution.py:249
  98.8 0.0 copy-done.3
  98.8 3.4 %collective-permute-start.9 = (bf16[3,128,768]{2,1,0:T(8,128)(2,1)S(1)}, bf16[3,128,768]{2,1,0:T(8,128)(2,1)S(1)}, u32[]{:S(2)}, u32[]{:S(2)}) collective-permute-start(bf16[3,128,768]{2,1,0:T(8,128)(2,1)S(1)} %copy-done.3), channel_id=1, source_target_pairs={{0,4},{4,0},{1,5},{5,1},{2,6},{6,2},{3,7},{7,3},{8,12},{12,8},{9,1... | collective-permute-start | bytes 1769480 | tf_op jit(solution)/shard_map/ppermute | solution.py:243
  102.2 5.9 %all-to-all-done.1 = f32[32,8,12]{2,1,0:T(8,128)S(1)} async-done(((f32[32,8,12]{2,1,0:T(8,128)}), f32[32,8,12]{2,1,0:T(8,128)S(1)}, u32[]{:S(2)}, u32[]{:S(2)}) %all-to-all-start.1) | async-done | bytes 12320 | tf_op jit(solution)/shard_map/all_to_all | solution.py:249
  108.2 0.1 copy.23
  108.3 0.0 collective-permute-done.12
  108.3 0.0 collective-permute-done.10
  108.3 0.1 fusion.9
  108.4 4.6 %collective-permute-start.13 = (bf16[2,32,768]{2,1,0:T(8,128)(2,1)S(1)}, bf16[2,32,768]{2,1,0:T(8,128)(2,1)S(1)}, u32[]{:S(2)}, u32[]{:S(2)}) collective-permute-start(bf16[2,32,768]{2,1,0:T(8,128)(2,1)S(1)} %get-tuple-element.47), channel_id=1, source_target_pairs={{0,4},{4,0},{1,5},{5,1},{2,6},{6,2},{3,7},{7,3},{8,12},{12,8},{9,1... | collective-permute-start | bytes 294920 | tf_op jit(solution)/shard_map/ppermute | solution.py:243
  113.0 0.7 copy.21
  113.7 0.2 collective-permute-done.13
  113.9 0.7 maximum_select_fusion
  114.6 0.0 collective-permute-done.9
  114.6 0.9 bitcast_dynamic-update-slice_fusion
  (18 shorter events, 0.3 us)
Async XLA Ops:
  1.6 12.4 %collective-permute-start = (bf16[4,32,768]{2,1,0:T(8,128)(2,1)S(1)}, bf16[4,32,768]{2,1,0:T(8,128)(2,1)S(1)}, u32[]{:S(2)}, u32[]{:S(2)}) collective-permute-start(bf16[4,32,768]{2,1,0:T(8,128)(2,1)S(1)} %fusion.7), channel_id=1, source_target_pairs={{0,4},{4,0},{1,5},{5,1},{2,6},{6,2},{3,7},{7,3},{8,12},{12,8},{9,1... | collective-permute-start | bytes 589832 | tf_op jit(solution)/shard_map/ppermute | solution.py:243
  15.7 15.5 %copy-start = (bf16[1,3,128,1536]{3,2,1,0:T(8,128)(2,1)S(1)}, bf16[1,3,128,1536]{3,2,1,0:T(8,128)(2,1)}, u32[]{:S(2)}) copy-start(bf16[1,3,128,1536]{3,2,1,0:T(8,128)(2,1)} %mine) | copy-start | bytes 3538948
  15.7 19.3 %copy-start.1 = (bf16[1,3,128,1536]{3,2,1,0:T(8,128)(2,1)S(1)}, bf16[1,3,128,1536]{3,2,1,0:T(8,128)(2,1)}, u32[]{:S(2)}) copy-start(bf16[1,3,128,1536]{3,2,1,0:T(8,128)(2,1)} %mine.1) | copy-start | bytes 3538948
  15.7 15.4 %collective-permute-start.1 = (bf16[2,2,32,768]{3,2,1,0:T(8,128)(2,1)S(1)}, bf16[2,2,32,768]{3,2,1,0:T(8,128)(2,1)S(1)}, u32[]{:S(2)}, u32[]{:S(2)}) collective-permute-start(bf16[2,2,32,768]{3,2,1,0:T(8,128)(2,1)S(1)} %pad_maximum_fusion.own), channel_id=1, source_target_pairs={{0,8},{8,0},{1,9},{9,1},{2,10},{10,2},{3,11},{11,3},{4,12},{12,4},... | collective-permute-start | bytes 589832 | tf_op jit(solution)/shard_map/ppermute | solution.py:243
  21.8 18.2 %collective-permute-start.5 = (bf16[4,32,768]{2,1,0:T(8,128)(2,1)}, bf16[4,32,768]{2,1,0:T(8,128)(2,1)S(1)}, u32[]{:S(2)}, u32[]{:S(2)}) collective-permute-start(bf16[4,32,768]{2,1,0:T(8,128)(2,1)} %broadcast_select_fusion.1), channel_id=1, source_target_pairs={{0,16},{4,20},{16,32},{20,36},{24,8},{28,12},{32,48},{36,52},{40,2... | collective-permute-start | bytes 589832 | tf_op jit(solution)/shard_map/ppermute | solution.py:296
  25.0 20.5 %collective-permute-start.6 = (bf16[4,32,768]{2,1,0:T(8,128)(2,1)}, bf16[4,32,768]{2,1,0:T(8,128)(2,1)S(1)}, u32[]{:S(2)}, u32[]{:S(2)}) collective-permute-start(bf16[4,32,768]{2,1,0:T(8,128)(2,1)} %get-tuple-element.44), channel_id=1, source_target_pairs={{16,0},{20,4},{32,16},{36,20},{8,24},{12,28},{48,32},{52,36},{24,4... | collective-permute-start | bytes 589832 | tf_op jit(solution)/shard_map/ppermute | solution.py:297
  26.3 9.6 %copy-start.4 = (s32[1,1,2]{2,1,0:T(1,128)S(1)}, s32[1,1,2]{2,1,0:T(1,128)}, u32[]{:S(2)}) copy-start(s32[1,1,2]{2,1,0:T(1,128)} %param.13) | copy-start | bytes 28
  26.3 16.1 %collective-permute-start.3 = (bf16[2,2,32,768]{3,2,1,0:T(8,128)(2,1)S(1)}, bf16[2,2,32,768]{3,2,1,0:T(8,128)(2,1)S(1)}, u32[]{:S(2)}, u32[]{:S(2)}) collective-permute-start(bf16[2,2,32,768]{3,2,1,0:T(8,128)(2,1)S(1)} %pad_maximum_fusion.1.own), channel_id=1, source_target_pairs={{0,8},{8,0},{1,9},{9,1},{2,10},{10,2},{3,11},{11,3},{4,12},{12,4},... | collective-permute-start | bytes 589832 | tf_op jit(solution)/shard_map/ppermute | solution.py:243
  32.0 13.6 %collective-permute-start.7 = (bf16[3,128,768]{2,1,0:T(8,128)(2,1)}, bf16[3,128,768]{2,1,0:T(8,128)(2,1)}, u32[]{:S(2)}, u32[]{:S(2)}) collective-permute-start(bf16[3,128,768]{2,1,0:T(8,128)(2,1)} %dynamic-slice_bitcast_fusion), channel_id=1, source_target_pairs={{0,4},{4,0},{1,5},{5,1},{2,6},{6,2},{3,7},{7,3},{8,12},{12,8},{9,1... | collective-permute-start | bytes 1769480 | tf_op jit(solution)/shard_map/ppermute | solution.py:243
  37.7 12.1 %collective-permute-start.2 = (bf16[3,128,768]{2,1,0:T(8,128)(2,1)}, bf16[3,128,768]{2,1,0:T(8,128)(2,1)}, u32[]{:S(2)}, u32[]{:S(2)}) collective-permute-start(bf16[3,128,768]{2,1,0:T(8,128)(2,1)} %dynamic-slice_bitcast_fusion.1), channel_id=1, source_target_pairs={{0,4},{4,0},{1,5},{5,1},{2,6},{6,2},{3,7},{7,3},{8,12},{12,8},{9,1... | collective-permute-start | bytes 1769480 | tf_op jit(solution)/shard_map/ppermute | solution.py:243
  40.0 5.6 %collective-permute-start.8 = (bf16[2,2,32,768]{3,2,1,0:T(8,128)(2,1)S(1)}, bf16[2,2,32,768]{3,2,1,0:T(8,128)(2,1)}, u32[]{:S(2)}, u32[]{:S(2)}) collective-permute-start(bf16[2,2,32,768]{3,2,1,0:T(8,128)(2,1)S(1)} %collective-permute-done.1.zed), channel_id=1, source_target_pairs={{0,16},{4,20},{16,32},{20,36},{24,8},{28,12},{32,48},{36,52},{40,2... | collective-permute-start | bytes 589832 | tf_op jit(solution)/shard_map/ppermute | solution.py:298
  42.4 7.5 %collective-permute-start.4 = (bf16[2,2,32,768]{3,2,1,0:T(8,128)(2,1)S(1)}, bf16[2,2,32,768]{3,2,1,0:T(8,128)(2,1)}, u32[]{:S(2)}, u32[]{:S(2)}) collective-permute-start(bf16[2,2,32,768]{3,2,1,0:T(8,128)(2,1)S(1)} %collective-permute-done.3.zed), channel_id=1, source_target_pairs={{0,16},{4,20},{16,32},{20,36},{24,8},{28,12},{32,48},{36,52},{40,2... | collective-permute-start | bytes 589832 | tf_op jit(solution)/shard_map/ppermute | solution.py:298
  57.3 0.8 copy-start.2
  58.1 25.1 %collective-permute-start.11 = (bf16[3,2,32,768]{3,2,1,0:T(8,128)(2,1)}, bf16[3,2,32,768]{3,2,1,0:T(8,128)(2,1)S(1)}, u32[]{:S(2)}, u32[]{:S(2)}) collective-permute-start(bf16[3,2,32,768]{3,2,1,0:T(8,128)(2,1)} %get-tuple-element.26), channel_id=1, source_target_pairs={{16,0},{20,4},{32,16},{36,20},{8,24},{12,28},{48,32},{52,36},{24,4... | collective-permute-start | bytes 884744 | tf_op jit(solution)/shard_map/ppermute | solution.py:347
  83.2 15.6 %copy-start.3 = (bf16[3,128,768]{2,1,0:T(8,128)(2,1)S(1)}, bf16[3,128,768]{2,1,0:T(8,128)(2,1)}, u32[]{:S(2)}) copy-start(bf16[3,128,768]{2,1,0:T(8,128)(2,1)} %copy-done.2) | copy-start | bytes 1769476
  83.4 24.9 %collective-permute-start.12 = (bf16[2,2,32,768]{3,2,1,0:T(8,128)(2,1)S(1)}, bf16[2,2,32,768]{3,2,1,0:T(8,128)(2,1)S(1)}, u32[]{:S(2)}, u32[]{:S(2)}) collective-permute-start(bf16[2,2,32,768]{3,2,1,0:T(8,128)(2,1)S(1)} %fusion), channel_id=1, source_target_pairs={{0,8},{8,0},{1,9},{9,1},{2,10},{10,2},{3,11},{11,3},{4,12},{12,4},... | collective-permute-start | bytes 589832 | tf_op jit(solution)/shard_map/ppermute | solution.py:243
  85.8 22.5 %collective-permute-start.10 = (bf16[2,32,768]{2,1,0:T(8,128)(2,1)S(1)}, bf16[2,32,768]{2,1,0:T(8,128)(2,1)S(1)}, u32[]{:S(2)}, u32[]{:S(2)}) collective-permute-start(bf16[2,32,768]{2,1,0:T(8,128)(2,1)S(1)} %bitcast.59), channel_id=1, source_target_pairs={{0,16},{4,20},{16,32},{20,36},{24,8},{28,12},{32,48},{36,52},{40,2... | collective-permute-start | bytes 294920 | tf_op jit(solution)/shard_map/ppermute | solution.py:350
  90.3 17.9 %all-to-all-start.1 = ((f32[32,8,12]{2,1,0:T(8,128)}), f32[32,8,12]{2,1,0:T(8,128)S(1)}, u32[]{:S(2)}, u32[]{:S(2)}) async-start(f32[32,8,12]{2,1,0:T(8,128)} %broadcast_in_dim.61), calls=%async_computation.1 | async-start | bytes 262144 | tf_op jit(solution)/shard_map/all_to_all | solution.py:249
  98.8 15.9 %collective-permute-start.9 = (bf16[3,128,768]{2,1,0:T(8,128)(2,1)S(1)}, bf16[3,128,768]{2,1,0:T(8,128)(2,1)S(1)}, u32[]{:S(2)}, u32[]{:S(2)}) collective-permute-start(bf16[3,128,768]{2,1,0:T(8,128)(2,1)S(1)} %copy-done.3), channel_id=1, source_target_pairs={{0,4},{4,0},{1,5},{5,1},{2,6},{6,2},{3,7},{7,3},{8,12},{12,8},{9,1... | collective-permute-start | bytes 1769480 | tf_op jit(solution)/shard_map/ppermute | solution.py:243
  108.4 5.5 %collective-permute-start.13 = (bf16[2,32,768]{2,1,0:T(8,128)(2,1)S(1)}, bf16[2,32,768]{2,1,0:T(8,128)(2,1)S(1)}, u32[]{:S(2)}, u32[]{:S(2)}) collective-permute-start(bf16[2,32,768]{2,1,0:T(8,128)(2,1)S(1)} %get-tuple-element.47), channel_id=1, source_target_pairs={{0,4},{4,0},{1,5},{5,1},{2,6},{6,2},{3,7},{7,3},{8,12},{12,8},{9,1... | collective-permute-start | bytes 294920 | tf_op jit(solution)/shard_map/ppermute | solution.py:243

commit v3 on v2

--- a/solution.py
+++ b/solution.py
@@ -9,12 +9,12 @@
 from jax.sharding import PartitionSpec as P
 
 SEQ = ("seq_0", "seq_1", "seq_2", "seq_3")
-PLANE = ("seq_0", "seq_1")
-COLUMN = ("seq_2", "seq_3", "dp")
+FIRST = ("seq_0", "seq_2")
+SECOND = ("seq_1", "dp")
 HALF = "seq_2"
 CORE = "seq_3"
 SLOTS = 8
-STEP_HEADS = 2
+STEP_HEADS = 3
 VMEM = 28 * 1024 * 1024
 
 
@@ -45,13 +45,9 @@
     q = (mine[0, 0, :, lanes], other[0, :, lanes])
     k = (mine[0, 1, :, lanes], other[1, :, lanes])
     v = (mine[0, 2, :, lanes], other[2, :, lanes])
-    own, zed, far, same, opposite = audio
-
-    def window(i):
-        pieces = [ref[b, i, :, lanes] for ref in (own, zed, far) for b in range(2)]
-        return jnp.concatenate(pieces + [same[i, :, lanes], opposite[i, :, lanes]], axis=0)
-
-    return q, k, v, window(0), window(1)
+    ka = jnp.concatenate([ref[0, :, lanes] for ref in audio], axis=0)
+    va = jnp.concatenate([ref[1, :, lanes] for ref in audio], axis=0)
+    return q, k, v, ka, va
 
 
 def scores_of(q, k, ka, scale, bias, rows):
@@ -72,11 +68,12 @@
     return by_block(lambda vb, pb: dot(vb, pb, 0, 0), v, halves(local)) + dot(va, audio, 0, 0)
 
 
-def teacher_kernel(dim, core, bias, scal, mine, other, own, zed, far, same, opposite, target):
-    rows = own.shape[2]
+def teacher_kernel(dim, core, bias, scal, mine, other, *refs):
+    *audio_refs, target = refs
+    rows = audio_refs[0].shape[1]
     for i in range(target.shape[0]):
         lanes = slice(i * dim, (i + 1) * dim)
-        q, k, v, ka, va = load_head(lanes, mine, other, (own, zed, far, same, opposite))
+        q, k, v, ka, va = load_head(lanes, mine, other, audio_refs)
         local, audio = scores_of(q, k, ka, dim**-0.5, bias, rows)
         plain_max = column_max(local)
         plain = jnp.exp(local - plain_max)
@@ -92,33 +89,15 @@
         target[i] = unconditional + scal[0] * (conditional - unconditional)
 
 
-def student_kernel(
-    dim,
-    core,
-    bias,
-    scal,
-    mine,
-    other,
-    own,
-    zed,
-    far,
-    same,
-    opposite,
-    target,
-    grad_mine,
-    grad_other,
-    own_out,
-    zed_out,
-    far_out,
-    opposite_out,
-    totals,
-):
-    rows = own.shape[2]
+def student_kernel(dim, core, bias, scal, mine, other, *refs):
+    audio_refs, target = refs[:SLOTS], refs[SLOTS]
+    grad_mine, grad_other, own_out, zed_out, far_out, opposite_out, totals = refs[SLOTS + 1 :]
+    rows = audio_refs[0].shape[1]
     scale = dim**-0.5
     heads = target.shape[0]
     for i in range(heads):
         lanes = slice(i * dim, (i + 1) * dim)
-        q, k, v, ka, va = load_head(lanes, mine, other, (own, zed, far, same, opposite))
+        q, k, v, ka, va = load_head(lanes, mine, other, audio_refs)
         local, audio = scores_of(q, k, ka, scale, bias, rows)
         highest = jnp.maximum(column_max(local), column_max(audio))
         local = jnp.exp(local - highest)
@@ -162,28 +141,29 @@
             ref[b, 1, :, lanes] = audio_values[at].astype(ref.dtype)
 
 
-def specs(steps, width, vb, rows, which):
+def specs(steps, width, vb, audio, which):
     smem = pl.BlockSpec(memory_space=pltpu.SMEM)
     mine = pl.BlockSpec((1, 3, vb, width), lambda h, c: (0, 0, 0, c[0] * steps + h))
     video = pl.BlockSpec((3, vb, width), lambda h, c: (0, 0, h))
-    pair = pl.BlockSpec((2, 2, rows, width), lambda h, c: (0, 0, 0, h))
-    single = pl.BlockSpec((2, rows, width), lambda h, c: (which, 0, h))
-    return smem, mine, video, pair, single
+
+    def piece(x):
+        at = which if x.shape[0] > 2 else 0
+        return pl.BlockSpec((2, x.shape[1], width), lambda h, c: (at, 0, h))
+
+    return [smem, smem, mine, video] + [piece(x) for x in audio]
 
 
 def teacher_call(core, bias, scal, mine, other, audio, head_dim):
     vb, half_width = mine.shape[2], other.shape[2]
-    rows = audio[0].shape[2]
     width = STEP_HEADS * head_dim
     steps = half_width // width
-    smem, own_video, video, pair, single = specs(steps, width, vb, rows, 0)
     heads = half_width // head_dim
     return pl.pallas_call(
         functools.partial(teacher_kernel, head_dim),
         grid_spec=pltpu.PrefetchScalarGridSpec(
             num_scalar_prefetch=1,
             grid=(steps,),
-            in_specs=[smem, smem, own_video, video] + [pair] * 3 + [single] * 2,
+            in_specs=specs(steps, width, vb, audio, 0),
             out_specs=pl.BlockSpec((STEP_HEADS, head_dim, 2 * vb), lambda h, c: (h, 0, 0)),
         ),
         out_shape=jax.ShapeDtypeStruct((heads, head_dim, 2 * vb), jnp.float32),
@@ -197,10 +177,10 @@
 
 def student_call(core, bias, scal, mine, other, audio, target, head_dim):
     vb, half_width = mine.shape[2], other.shape[2]
-    rows = audio[0].shape[2]
+    rows = audio[0].shape[1]
     width = STEP_HEADS * head_dim
     steps = half_width // width
-    smem, own_video, video, pair, single = specs(steps, width, vb, rows, 1)
+    in_specs = specs(steps, width, vb, audio, 1)
     heads = half_width // head_dim
 
     def blocks(n, dtype):
@@ -208,8 +188,8 @@
         return shape, pl.BlockSpec((n, 2, rows, width), lambda h, c: (0, 0, 0, h))
 
     outs = [
-        (jax.ShapeDtypeStruct(mine.shape, jnp.bfloat16), own_video),
-        (jax.ShapeDtypeStruct(other.shape, jnp.bfloat16), video),
+        (jax.ShapeDtypeStruct(mine.shape, jnp.bfloat16), in_specs[2]),
+        (jax.ShapeDtypeStruct(other.shape, jnp.bfloat16), in_specs[3]),
         blocks(2, jnp.float32),
         blocks(2, jnp.float32),
         blocks(3, jnp.bfloat16),
@@ -224,9 +204,7 @@
         grid_spec=pltpu.PrefetchScalarGridSpec(
             num_scalar_prefetch=1,
             grid=(steps,),
-            in_specs=[smem, smem, own_video, video]
-            + [pair] * 3
-            + [single] * 2
+            in_specs=in_specs
             + [pl.BlockSpec((STEP_HEADS, head_dim, 2 * vb), lambda h, c: (h, 0, 0))],
             out_specs=[spec for _, spec in outs],
         ),
@@ -285,21 +263,27 @@
         return lax.dynamic_slice_in_dim(x, which * half_width, half_width, x.ndim - 1)
 
     audio = jnp.concatenate([teacher_audio[0], student_audio[0]], axis=0)
+    kept = part(audio, core)
     got = swap(part(audio, 1 - core), CORE)
-    kept = part(audio, core)
-    pairs = [jnp.stack([kept[i : i + 2], got[i : i + 2]]) for i in (0, 2)]
     inner = core == half
-    zeds = [swap(pair, HALF) for pair in pairs]
-    zeds[0], teacher_video, student_video, alignment = lax.optimization_barrier(
-        (zeds[0], teacher_video, student_video, alignment)
-    )
-    same = lax.ppermute(jnp.where(inner, got, kept), SEQ, far_out)
-    opposite = lax.ppermute(jnp.where(inner, kept, got), SEQ, far_back)
-    fars = [lax.ppermute(zed, SEQ, far_out) for zed in zeds]
-
-    teach_other = swap(part(teacher_video[0], 1 - core), CORE)
+    zed_kept, got, teacher_video, alignment, guidance_index, step_index = (
+        lax.optimization_barrier(
+            (swap(kept, HALF), got, teacher_video, alignment, guidance_index, step_index)
+        )
+    )
+    zed_got, far_kept, same, opposite, teach_other, spans = lax.optimization_barrier(
+        (
+            swap(got, HALF),
+            lax.ppermute(zed_kept, SEQ, far_out),
+            lax.ppermute(jnp.where(inner, got, kept), SEQ, far_out),
+            lax.ppermute(jnp.where(inner, kept, got), SEQ, far_back),
+            swap(part(teacher_video[0], 1 - core), CORE),
+            lax.all_gather(alignment[0, 0], CORE),
+        )
+    )
+    far_got = [lax.ppermute(zed_got[i : i + 2], SEQ, far_out) for i in (0, 2)]
+    far_got[0], student_video = lax.optimization_barrier((far_got[0], student_video))
     pupil_other = swap(part(student_video[0], 1 - core), CORE)
-    spans = lax.all_gather(alignment[0, 0], CORE)
 
     side = 2 - 4 * half
     near = 7 * half
@@ -331,7 +315,10 @@
     scal = jnp.concatenate([jnp.stack([weight, loss_weight]), factor])
     which = core.astype(jnp.int32)[None]
 
-    windows = [(pair, zed, far, same, opposite) for pair, zed, far in zip(pairs, zeds, fars)]
+    windows = [
+        (kept, got, zed_kept, zed_got, far_kept, far_got[i], same, opposite)
+        for i in range(2)
+    ]
     target = teacher_call(which, bias, scal, teacher_video, teach_other, windows[0], head_dim)
     grad_video, grad_other, own, zed, far, opposite, totals = student_call(
         which, bias, scal, student_video, pupil_other, windows[1], target, head_dim
@@ -345,17 +332,18 @@
         levels[:, None] == level_index, head_totals[None, :], jnp.zeros_like(gamma)
     )
     far_in = lax.ppermute(far, SEQ, far_back)
-    far_in, contribution = lax.optimization_barrier((far_in, everywhere(contribution, COLUMN)))
+    far_in, contribution = lax.optimization_barrier((far_in, everywhere(contribution, FIRST)))
     far_in = far_in.astype(jnp.float32)
     opposite_in = lax.ppermute(opposite[0], SEQ, far_out).astype(jnp.float32)
     zed_in = swap((zed + far_in[:2]).astype(jnp.bfloat16), HALF)
-    zed_in, gamma_grad = lax.optimization_barrier((zed_in, everywhere(contribution, PLANE)))
+    zed_in, gamma_grad = lax.optimization_barrier((zed_in, everywhere(contribution, SECOND)))
     zed_in = zed_in.astype(jnp.float32)
     near_in = (far_in[2], opposite_in)
     keep = own[0] + jnp.where(inner, near_in[1], near_in[0])
     leave = own[1] + jnp.where(inner, near_in[0], near_in[1])
     keep = (keep + zed_in[0]).astype(jnp.bfloat16)
     arrived = swap((leave + zed_in[1]).astype(jnp.bfloat16), CORE)
+    gamma_grad, arrived = lax.optimization_barrier((lax.psum(gamma_grad, CORE), arrived))
     grad_audio = jnp.where(
         core == 0,
         jnp.concatenate([keep, arrived], axis=-1),

time: 116 us -> 136 us (1.17)
  starting transfers between devices: 57.1 us -> 68.2 us
  blocking collectives: 25 us -> 34.5 us
  other arithmetic: 6.1 us -> 3.27 us
  local copies, waits for them, and re-layouts: 6.28 us -> 8.65 us
    ppermute x8, starting transfers between devices: 34.6 us -> 42.9 us  [swap(): return lax.ppermute(x, axis, [(0, 1), (1, 0)])]
    ppermute x4 -> x5, starting transfers between devices: 9.05 us -> 16.2 us  [the longest x2 7.17 us: body(): far_got = [lax.ppermute(zed_got[i:i + 2], SEQ, far_out) for i in (0, 2)]]
    all_to_all x1, blocking collectives: 23.3 us -> 29.4 us  [everywhere(): return jnp.sum(lax.all_to_all(copies, axes, 0, 0), axis=0)]
    all_to_all x1, starting transfers between devices: 8.5 us -> 4.19 us  [everywhere(): return jnp.sum(lax.all_to_all(copies, axes, 0, 0), axis=0)]
    psum x0 -> x1, blocking collectives: none -> 2.51 us  [body(): lax.psum(gamma_grad, CORE)]
    select_n x2 -> x1, other arithmetic: 2.37 us -> 0.78 us  [body(): jnp.where(inner, kept, got)]
    ppermute x8, waiting for transfers between devices: 0.26 us -> 1.74 us  [swap(): return lax.ppermute(x, axis, [(0, 1), (1, 0)])]
  transfers between devices with their start and end apart: 15 -> 16, of which waited for: 4 -> 2; matrix products, arithmetic and copies ran while one was open for 7% -> 4% of each run, Pallas kernels for 3% -> 3%
where the time goes in v3:
time: 136 us; the launch traced here: 135 us
  starting transfers between devices  68.2 us (50%)
  blocking collectives  34.5 us (25%)
  Pallas kernels  10.9 us (8%)
  local copies, waits for them, and re-layouts  8.65 us (6%)
  waiting for transfers between devices  6.57 us (5%)
  other arithmetic  3.27 us (2%)
  between operations  2.93 us (2%)
    ppermute x8, starting transfers between devices, swap(): return lax.ppermute(x, axis, [(0, 1), (1, 0)])  42.9 us
    all_to_all x1, blocking collectives, everywhere(): return jnp.sum(lax.all_to_all(copies, axes, 0, 0), axis=0)  29.4 us
    pallas_call x1, Pallas kernels, student_call(): pl.pallas_call(functools.partial(student_kernel, head_dim), grid_spec=plt...  7.21 us
    ppermute x2, starting transfers between devices, body(): far_got = [lax.ppermute(zed_got[i:i + 2], SEQ, far_out) for i in (0, 2)]  7.17 us
    all_to_all x1, waiting for transfers between devices, everywhere(): return jnp.sum(lax.all_to_all(copies, axes, 0, 0), axis=0)  4.81 us
    ppermute x1, starting transfers between devices, body(): lax.ppermute(zed_kept, SEQ, far_out)  4.67 us
    all_to_all x1, starting transfers between devices, everywhere(): return jnp.sum(lax.all_to_all(copies, axes, 0, 0), axis=0)  4.19 us
    pallas_call x1, Pallas kernels, teacher_call(): pl.pallas_call(functools.partial(teacher_kernel, head_dim), grid_spec=plt...  3.68 us
  transfers between devices with their start and end apart: 16, of which 2 were waited for; matrix products, arithmetic and copies ran while one was open for 4% of the time, Pallas kernels for 3%

profile of v3, /device:TPU:1, one launch (start us, length us, event | category | flops | bytes accessed | tf_op | source)
XLA Modules:
  0.0 135.0 jit_solution(8860864951572915309)
XLA Ops:
  0.6 1.1 fusion.7
  1.7 0.0 copy-start.6
  1.7 0.0 copy-start.8
  1.7 11.5 %collective-permute-start = (bf16[4,32,768]{2,1,0:T(8,128)(2,1)S(1)}, bf16[4,32,768]{2,1,0:T(8,128)(2,1)S(1)}, u32[]{:S(2)}, u32[]{:S(2)}) collective-permute-start(bf16[4,32,768]{2,1,0:T(8,128)(2,1)S(1)} %get-tuple-element.73.refs_0_), channel_id=1, source_target_pairs={{0,8},{8,0},{1,9},{9,1},{2,10},{10,2},{3,11},{11,3},{4,12},{12,4},... | collective-permute-start | bytes 589832 | tf_op jit(solution)/shard_map/ppermute | solution.py:221
  13.2 0.0 copy-start.1
  13.2 3.0 %collective-permute-start.1 = (bf16[4,32,768]{2,1,0:T(8,128)(2,1)S(1)}, bf16[4,32,768]{2,1,0:T(8,128)(2,1)S(1)}, u32[]{:S(2)}, u32[]{:S(2)}) collective-permute-start(bf16[4,32,768]{2,1,0:T(8,128)(2,1)S(1)} %get-tuple-element.72), channel_id=1, source_target_pairs={{0,4},{4,0},{1,5},{5,1},{2,6},{6,2},{3,7},{7,3},{8,12},{12,8},{9,1... | collective-permute-start | bytes 589832 | tf_op jit(solution)/shard_map/ppermute | solution.py:221
  16.2 1.7 %collective-permute-done.refs_2_ = bf16[4,32,768]{2,1,0:T(8,128)(2,1)S(1)} collective-permute-done((bf16[4,32,768]{2,1,0:T(8,128)(2,1)S(1)}, bf16[4,32,768]{2,1,0:T(8,128)(2,1)S(1)}, u32[]{:S(2)}, u32[]{:S(2)}) %collective-permute-start) | collective-permute-done | bytes 196640 | tf_op jit(solution)/shard_map/ppermute | solution.py:221
  17.9 0.0 collective-permute-done.1.refs_1_
  18.0 1.9 %dynamic-slice_bitcast_fusion.1 = bf16[3,128,768]{2,1,0:T(8,128)(2,1)} fusion(bf16[1,3,128,1536]{3,2,1,0:T(8,128)(2,1)} %mine, s32[]{:T(128)S(6)} %select_n.82), kind=kLoop, calls=%fused_computation.2 | loop fusion | bytes 1179652 | tf_op jit(solution)/shard_map/dynamic_slice | solution.py:263
  19.9 6.5 %collective-permute-start.6 = (bf16[3,128,768]{2,1,0:T(8,128)(2,1)}, bf16[3,128,768]{2,1,0:T(8,128)(2,1)}, u32[]{:S(2)}, u32[]{:S(2)}) collective-permute-start(bf16[3,128,768]{2,1,0:T(8,128)(2,1)} %dynamic-slice_bitcast_fusion.1), channel_id=1, source_target_pairs={{0,4},{4,0},{1,5},{5,1},{2,6},{6,2},{3,7},{7,3},{8,12},{12,8},{9,1... | collective-permute-start | bytes 1769480 | tf_op jit(solution)/shard_map/ppermute | solution.py:221
  28.4 0.0 copy-start
  28.4 8.2 %collective-permute-start.2 = (bf16[4,32,768]{2,1,0:T(8,128)(2,1)S(1)}, bf16[4,32,768]{2,1,0:T(8,128)(2,1)S(1)}, u32[]{:S(2)}, u32[]{:S(2)}) collective-permute-start(bf16[4,32,768]{2,1,0:T(8,128)(2,1)S(1)} %collective-permute-done.1.refs_1_), channel_id=1, source_target_pairs={{0,8},{8,0},{1,9},{9,1},{2,10},{10,2},{3,11},{11,3},{4,12},{12,4},... | collective-permute-start | bytes 589832 | tf_op jit(solution)/shard_map/ppermute | solution.py:221
  36.6 0.8 broadcast_select_fusion
  37.3 3.1 %collective-permute-start.4 = (bf16[4,32,768]{2,1,0:T(8,128)(2,1)}, bf16[4,32,768]{2,1,0:T(8,128)(2,1)S(1)}, u32[]{:S(2)}, u32[]{:S(2)}) collective-permute-start(bf16[4,32,768]{2,1,0:T(8,128)(2,1)} %get-tuple-element.71), channel_id=1, source_target_pairs={{0,16},{4,20},{16,32},{20,36},{24,8},{28,12},{32,48},{36,52},{40,2... | collective-permute-start | bytes 589832 | tf_op jit(solution)/shard_map/ppermute | solution.py:278
  40.4 1.3 collective-permute-start.5
  41.7 4.7 %collective-permute-start.3 = (bf16[4,32,768]{2,1,0:T(8,128)(2,1)S(1)}, bf16[4,32,768]{2,1,0:T(8,128)(2,1)}, u32[]{:S(2)}, u32[]{:S(2)}) collective-permute-start(bf16[4,32,768]{2,1,0:T(8,128)(2,1)S(1)} %collective-permute-done.refs_2_), channel_id=1, source_target_pairs={{0,16},{4,20},{16,32},{20,36},{24,8},{28,12},{32,48},{36,52},{40,2... | collective-permute-start | bytes 589832 | tf_op jit(solution)/shard_map/ppermute | solution.py:277
  46.4 0.1 select_reduce_fusion
  46.5 0.1 dynamic_slice.23
  46.6 0.7 stack.39
  47.2 2.6 %all-gather = s32[2,1,2]{2,1,0:T(1,128)S(1)} all-gather(s32[1,1,2]{2,1,0:T(1,128)S(1)} %copy-done.8), channel_id=2, replica_groups=mesh['seq_0'=8,'seq_1'=4,'seq_2'=2,'seq_3'=2,'dp'=4] {'seq_3'}, dimensions={0}, use_global_device_ids=true | all-gather | bytes 24 | tf_op jit(solution)/shard_map/all_gather | solution.py:281
  49.8 0.0 collective-permute-done.4.refs_6_
  49.8 0.0 collective-permute-done.5.refs_7_
  49.8 0.0 collective-permute-done.2.refs_3_
  49.8 0.0 collective-permute-done.3.refs_4_
  49.9 0.0 collective-permute-done.6.other
  49.9 0.7 fusion.10
  50.5 4.0 %collective-permute-start.7 = (bf16[2,32,768]{2,1,0:T(8,128)(2,1)}, bf16[2,32,768]{2,1,0:T(8,128)(2,1)}, u32[]{:S(2)}, u32[]{:S(2)}) collective-permute-start(bf16[2,32,768]{2,1,0:T(8,128)(2,1)} %get-tuple-element.75), channel_id=1, source_target_pairs={{0,16},{4,20},{16,32},{20,36},{24,8},{28,12},{32,48},{36,52},{40,2... | collective-permute-start | bytes 294920 | tf_op jit(solution)/shard_map/ppermute | solution.py:284
  54.6 0.1 pad_maximum_fusion.scal
  54.7 3.1 %collective-permute-start.9 = (bf16[2,32,768]{2,1,0:T(8,128)(2,1)}, bf16[2,32,768]{2,1,0:T(8,128)(2,1)}, u32[]{:S(2)}, u32[]{:S(2)}) collective-permute-start(bf16[2,32,768]{2,1,0:T(8,128)(2,1)} %get-tuple-element.74), channel_id=1, source_target_pairs={{0,16},{4,20},{16,32},{20,36},{24,8},{28,12},{32,48},{36,52},{40,2... | collective-permute-start | bytes 294920 | tf_op jit(solution)/shard_map/ppermute | solution.py:284
  57.8 0.9 dynamic-slice_bitcast_fusion
  58.7 4.2 %collective-permute-start.8 = (bf16[3,128,768]{2,1,0:T(8,128)(2,1)}, bf16[3,128,768]{2,1,0:T(8,128)(2,1)}, u32[]{:S(2)}, u32[]{:S(2)}) collective-permute-start(bf16[3,128,768]{2,1,0:T(8,128)(2,1)} %dynamic-slice_bitcast_fusion), channel_id=1, source_target_pairs={{0,4},{4,0},{1,5},{5,1},{2,6},{6,2},{3,7},{7,3},{8,12},{12,8},{9,1... | collective-permute-start | bytes 1769480 | tf_op jit(solution)/shard_map/ppermute | solution.py:221
  62.9 0.2 slice_reduce_fusion
  63.1 0.1 and_select_fusion
  63.2 0.1 select_n.88.bias
  63.3 3.7 %teacher.1.refs_8_ = f32[6,128,256]{2,1,0:T(8,128)S(1)} custom-call(s32[1]{0:T(128)} %bitcast.core, f32[16]{0:T(128)S(1)} %select_n.88.bias, f32[8]{0:T(128)S(1)} %pad_maximum_fusion.scal, bf16[1,3,128,1536]{3,2,1,0:T(8,128)(2,1)S(1)} %copy-done, bf16[3,128,768]{2,1,0:T(8,128)(2,1)} %collective-permute-done.6.other, ...), custom_call_target="tpu_custom_call" | custom-call | flops 600000000 | bytes 4000000 | tf_op jit(solution)/shard_map/teacher/pallas_call | solution.py:161
  67.0 0.0 collective-permute-done.9.refs_5_
  67.0 0.0 collective-permute-done.8.other
  67.0 7.2 %student.1 = (bf16[1,3,128,1536]{3,2,1,0:T(8,128)(2,1)}, bf16[3,128,768]{2,1,0:T(8,128)(2,1)S(1)}, f32[2,2,32,768]{3,2,1,0:T(8,128)S(1)}, f32[2,2,32,768]{3,2,1,...) custom-call(s32[1]{0:T(128)} %bitcast.core, ...), custom_call_target="tpu_custom_call" | custom-call | flops 900000000 | bytes 8000000 | tf_op jit(solution)/shard_map/student/pallas_call | solution.py:202
  74.2 0.8 copy-done.2
  75.0 0.6 copy-done.4
  75.7 1.4 %collective-permute-start.12 = (bf16[3,2,32,768]{3,2,1,0:T(8,128)(2,1)}, bf16[3,2,32,768]{3,2,1,0:T(8,128)(2,1)S(1)}, u32[]{:S(2)}, u32[]{:S(2)}) collective-permute-start(bf16[3,2,32,768]{3,2,1,0:T(8,128)(2,1)} %get-tuple-element.48), channel_id=1, source_target_pairs={{16,0},{20,4},{32,16},{36,20},{8,24},{12,28},{48,32},{52,36},{24,4... | collective-permute-start | bytes 884744 | tf_op jit(solution)/shard_map/ppermute | solution.py:334
  77.1 0.1 reduce_sum.37
  77.2 0.2 dynamic_update_slice.18
  77.4 0.1 broadcast_select_fusion.2
  77.5 29.4 %all_to_all.10 = f32[16,8,12]{2,1,0:T(8,128)S(1)} all-to-all(f32[16,8,12]{2,1,0:T(8,128)S(1)} %broadcast_in_dim.60), channel_id=1, replica_groups=mesh['seq_0'=8,'seq_1'=4,'seq_2'=2,'seq_3'=2,'dp'=4] {'seq_0','seq_2'}, dimensions={0} | all-to-all | bytes 12288 | tf_op jit(solution)/shard_map/all_to_all | solution.py:227
  106.9 0.1 copy.22
  107.0 0.0 collective-permute-done.12
  107.1 2.2 %collective-permute-start.13 = (bf16[2,2,32,768]{3,2,1,0:T(8,128)(2,1)S(1)}, bf16[2,2,32,768]{3,2,1,0:T(8,128)(2,1)S(1)}, u32[]{:S(2)}, u32[]{:S(2)}) collective-permute-start(bf16[2,2,32,768]{3,2,1,0:T(8,128)(2,1)S(1)} %fusion), channel_id=1, source_target_pairs={{0,8},{8,0},{1,9},{9,1},{2,10},{10,2},{3,11},{11,3},{4,12},{12,4},... | collective-permute-start | bytes 589832 | tf_op jit(solution)/shard_map/ppermute | solution.py:221
  109.3 3.5 %collective-permute-start.11 = (bf16[2,32,768]{2,1,0:T(8,128)(2,1)S(1)}, bf16[2,32,768]{2,1,0:T(8,128)(2,1)S(1)}, u32[]{:S(2)}, u32[]{:S(2)}) collective-permute-start(bf16[2,32,768]{2,1,0:T(8,128)(2,1)S(1)} %bitcast.51), channel_id=1, source_target_pairs={{0,16},{4,20},{16,32},{20,36},{24,8},{28,12},{32,48},{36,52},{40,2... | collective-permute-start | bytes 294920 | tf_op jit(solution)/shard_map/ppermute | solution.py:337
  112.8 0.1 copy.19
  112.9 0.6 broadcast_in_dim.61
  113.5 4.2 %all-to-all-start.1 = ((f32[16,8,12]{2,1,0:T(8,128)}), f32[16,8,12]{2,1,0:T(8,128)S(1)}, u32[]{:S(2)}, u32[]{:S(2)}) async-start(f32[16,8,12]{2,1,0:T(8,128)} %broadcast_in_dim.61), calls=%async_computation.1 | async-start | bytes 131072 | tf_op jit(solution)/shard_map/all_to_all | solution.py:227
  117.7 4.1 %collective-permute-start.10 = (bf16[3,128,768]{2,1,0:T(8,128)(2,1)S(1)}, bf16[3,128,768]{2,1,0:T(8,128)(2,1)S(1)}, u32[]{:S(2)}, u32[]{:S(2)}) collective-permute-start(bf16[3,128,768]{2,1,0:T(8,128)(2,1)S(1)} %copy-done.3), channel_id=1, source_target_pairs={{0,4},{4,0},{1,5},{5,1},{2,6},{6,2},{3,7},{7,3},{8,12},{12,8},{9,1... | collective-permute-start | bytes 1769480 | tf_op jit(solution)/shard_map/ppermute | solution.py:221
  121.8 4.8 %all-to-all-done.1 = f32[16,8,12]{2,1,0:T(8,128)S(1)} async-done(((f32[16,8,12]{2,1,0:T(8,128)}), f32[16,8,12]{2,1,0:T(8,128)S(1)}, u32[]{:S(2)}, u32[]{:S(2)}) %all-to-all-start.1) | async-done | bytes 6176 | tf_op jit(solution)/shard_map/all_to_all | solution.py:227
  126.7 0.1 copy.23
  126.8 0.0 collective-permute-done.13
  126.8 0.0 collective-permute-done.11
  126.8 0.1 fusion.9
  126.9 3.3 %collective-permute-start.14 = (bf16[2,32,768]{2,1,0:T(8,128)(2,1)S(1)}, bf16[2,32,768]{2,1,0:T(8,128)(2,1)S(1)}, u32[]{:S(2)}, u32[]{:S(2)}) collective-permute-start(bf16[2,32,768]{2,1,0:T(8,128)(2,1)S(1)} %get-tuple-element.69), channel_id=1, source_target_pairs={{0,4},{4,0},{1,5},{5,1},{2,6},{6,2},{3,7},{7,3},{8,12},{12,8},{9,1... | collective-permute-start | bytes 294920 | tf_op jit(solution)/shard_map/ppermute | solution.py:221
  130.2 2.5 %psum.7 = f32[8,12]{0,1:T(8,128)S(1)} all-reduce(f32[8,12]{0,1:T(8,128)S(1)} %copy.23), channel_id=1, replica_groups=mesh['seq_0'=8,'seq_1'=4,'seq_2'=2,'seq_3'=2,'dp'=4] {'seq_3'}, use_global_device_ids=true, to_apply=%region_4.5 | all-reduce | flops 96 | bytes 768 | tf_op jit(solution)/shard_map/psum | solution.py:346
  132.7 0.7 copy.21
  133.4 0.7 maximum_select_fusion
  134.1 0.0 collective-permute-done.10
  134.1 0.9 bitcast_dynamic-update-slice_fusion
  (26 shorter events, 0.2 us)
Async XLA Ops:
  1.7 44.7 %copy-start.6 = (f32[8,12]{1,0:T(8,128)S(1)}, f32[8,12]{1,0:T(8,128)}, u32[]{:S(2)}) copy-start(f32[8,12]{1,0:T(8,128)} %param.17) | copy-start | bytes 1156
  1.7 45.5 %copy-start.8 = (s32[1,1,2]{2,1,0:T(1,128)S(1)}, s32[1,1,2]{2,1,0:T(1,128)}, u32[]{:S(2)}) copy-start(s32[1,1,2]{2,1,0:T(1,128)} %param.13) | copy-start | bytes 28
  1.7 16.2 %collective-permute-start = (bf16[4,32,768]{2,1,0:T(8,128)(2,1)S(1)}, bf16[4,32,768]{2,1,0:T(8,128)(2,1)S(1)}, u32[]{:S(2)}, u32[]{:S(2)}) collective-permute-start(bf16[4,32,768]{2,1,0:T(8,128)(2,1)S(1)} %get-tuple-element.73.refs_0_), channel_id=1, source_target_pairs={{0,8},{8,0},{1,9},{9,1},{2,10},{10,2},{3,11},{11,3},{4,12},{12,4},... | collective-permute-start | bytes 589832 | tf_op jit(solution)/shard_map/ppermute | solution.py:221
  13.2 44.6 %copy-start.1 = (bf16[1,3,128,1536]{3,2,1,0:T(8,128)(2,1)S(1)}, bf16[1,3,128,1536]{3,2,1,0:T(8,128)(2,1)}, u32[]{:S(2)}) copy-start(bf16[1,3,128,1536]{3,2,1,0:T(8,128)(2,1)} %mine.1) | copy-start | bytes 3538948
  13.2 4.7 %collective-permute-start.1 = (bf16[4,32,768]{2,1,0:T(8,128)(2,1)S(1)}, bf16[4,32,768]{2,1,0:T(8,128)(2,1)S(1)}, u32[]{:S(2)}, u32[]{:S(2)}) collective-permute-start(bf16[4,32,768]{2,1,0:T(8,128)(2,1)S(1)} %get-tuple-element.72), channel_id=1, source_target_pairs={{0,4},{4,0},{1,5},{5,1},{2,6},{6,2},{3,7},{7,3},{8,12},{12,8},{9,1... | collective-permute-start | bytes 589832 | tf_op jit(solution)/shard_map/ppermute | solution.py:221
  19.9 30.0 %collective-permute-start.6 = (bf16[3,128,768]{2,1,0:T(8,128)(2,1)}, bf16[3,128,768]{2,1,0:T(8,128)(2,1)}, u32[]{:S(2)}, u32[]{:S(2)}) collective-permute-start(bf16[3,128,768]{2,1,0:T(8,128)(2,1)} %dynamic-slice_bitcast_fusion.1), channel_id=1, source_target_pairs={{0,4},{4,0},{1,5},{5,1},{2,6},{6,2},{3,7},{7,3},{8,12},{12,8},{9,1... | collective-permute-start | bytes 1769480 | tf_op jit(solution)/shard_map/ppermute | solution.py:221
  28.4 34.9 %copy-start = (bf16[1,3,128,1536]{3,2,1,0:T(8,128)(2,1)S(1)}, bf16[1,3,128,1536]{3,2,1,0:T(8,128)(2,1)}, u32[]{:S(2)}) copy-start(bf16[1,3,128,1536]{3,2,1,0:T(8,128)(2,1)} %mine) | copy-start | bytes 3538948
  28.4 21.5 %collective-permute-start.2 = (bf16[4,32,768]{2,1,0:T(8,128)(2,1)S(1)}, bf16[4,32,768]{2,1,0:T(8,128)(2,1)S(1)}, u32[]{:S(2)}, u32[]{:S(2)}) collective-permute-start(bf16[4,32,768]{2,1,0:T(8,128)(2,1)S(1)} %collective-permute-done.1.refs_1_), channel_id=1, source_target_pairs={{0,8},{8,0},{1,9},{9,1},{2,10},{10,2},{3,11},{11,3},{4,12},{12,4},... | collective-permute-start | bytes 589832 | tf_op jit(solution)/shard_map/ppermute | solution.py:221
  37.3 12.5 %collective-permute-start.4 = (bf16[4,32,768]{2,1,0:T(8,128)(2,1)}, bf16[4,32,768]{2,1,0:T(8,128)(2,1)S(1)}, u32[]{:S(2)}, u32[]{:S(2)}) collective-permute-start(bf16[4,32,768]{2,1,0:T(8,128)(2,1)} %get-tuple-element.71), channel_id=1, source_target_pairs={{0,16},{4,20},{16,32},{20,36},{24,8},{28,12},{32,48},{36,52},{40,2... | collective-permute-start | bytes 589832 | tf_op jit(solution)/shard_map/ppermute | solution.py:278
  40.4 9.4 %collective-permute-start.5 = (bf16[4,32,768]{2,1,0:T(8,128)(2,1)}, bf16[4,32,768]{2,1,0:T(8,128)(2,1)S(1)}, u32[]{:S(2)}, u32[]{:S(2)}) collective-permute-start(bf16[4,32,768]{2,1,0:T(8,128)(2,1)} %get-tuple-element.70), channel_id=1, source_target_pairs={{16,0},{20,4},{32,16},{36,20},{8,24},{12,28},{48,32},{52,36},{24,4... | collective-permute-start | bytes 589832 | tf_op jit(solution)/shard_map/ppermute | solution.py:279
  41.7 8.1 %collective-permute-start.3 = (bf16[4,32,768]{2,1,0:T(8,128)(2,1)S(1)}, bf16[4,32,768]{2,1,0:T(8,128)(2,1)}, u32[]{:S(2)}, u32[]{:S(2)}) collective-permute-start(bf16[4,32,768]{2,1,0:T(8,128)(2,1)S(1)} %collective-permute-done.refs_2_), channel_id=1, source_target_pairs={{0,16},{4,20},{16,32},{20,36},{24,8},{28,12},{32,48},{36,52},{40,2... | collective-permute-start | bytes 589832 | tf_op jit(solution)/shard_map/ppermute | solution.py:277
  50.5 7.3 %collective-permute-start.7 = (bf16[2,32,768]{2,1,0:T(8,128)(2,1)}, bf16[2,32,768]{2,1,0:T(8,128)(2,1)}, u32[]{:S(2)}, u32[]{:S(2)}) collective-permute-start(bf16[2,32,768]{2,1,0:T(8,128)(2,1)} %get-tuple-element.75), channel_id=1, source_target_pairs={{0,16},{4,20},{16,32},{20,36},{24,8},{28,12},{32,48},{36,52},{40,2... | collective-permute-start | bytes 294920 | tf_op jit(solution)/shard_map/ppermute | solution.py:284
  54.7 8.4 %copy-start.7 = (s32[8]{0:T(128)S(1)}, s32[8]{0:T(128)}, u32[]{:S(2)}) copy-start(s32[8]{0:T(128)} %stack.39) | copy-start | bytes 100
  54.7 12.3 %collective-permute-start.9 = (bf16[2,32,768]{2,1,0:T(8,128)(2,1)}, bf16[2,32,768]{2,1,0:T(8,128)(2,1)}, u32[]{:S(2)}, u32[]{:S(2)}) collective-permute-start(bf16[2,32,768]{2,1,0:T(8,128)(2,1)} %get-tuple-element.74), channel_id=1, source_target_pairs={{0,16},{4,20},{16,32},{20,36},{24,8},{28,12},{32,48},{36,52},{40,2... | collective-permute-start | bytes 294920 | tf_op jit(solution)/shard_map/ppermute | solution.py:284
  58.7 8.3 %collective-permute-start.8 = (bf16[3,128,768]{2,1,0:T(8,128)(2,1)}, bf16[3,128,768]{2,1,0:T(8,128)(2,1)}, u32[]{:S(2)}, u32[]{:S(2)}) collective-permute-start(bf16[3,128,768]{2,1,0:T(8,128)(2,1)} %dynamic-slice_bitcast_fusion), channel_id=1, source_target_pairs={{0,4},{4,0},{1,5},{5,1},{2,6},{6,2},{3,7},{7,3},{8,12},{12,8},{9,1... | collective-permute-start | bytes 1769480 | tf_op jit(solution)/shard_map/ppermute | solution.py:221
  74.2 0.8 copy-start.2
  75.0 0.6 copy-start.4
  75.7 33.7 %copy-start.5 = (bf16[1,2,32,768]{3,2,1,0:T(8,128)(2,1)S(1)}, bf16[1,2,32,768]{3,2,1,0:T(8,128)(2,1)}, u32[]{:S(2)}) copy-start(bf16[1,2,32,768]{3,2,1,0:T(8,128)(2,1)} %copy-done.4) | copy-start | bytes 294916
  75.7 31.4 %collective-permute-start.12 = (bf16[3,2,32,768]{3,2,1,0:T(8,128)(2,1)}, bf16[3,2,32,768]{3,2,1,0:T(8,128)(2,1)S(1)}, u32[]{:S(2)}, u32[]{:S(2)}) collective-permute-start(bf16[3,2,32,768]{3,2,1,0:T(8,128)(2,1)} %get-tuple-element.48), channel_id=1, source_target_pairs={{16,0},{20,4},{32,16},{36,20},{8,24},{12,28},{48,32},{52,36},{24,4... | collective-permute-start | bytes 884744 | tf_op jit(solution)/shard_map/ppermute | solution.py:334
  77.5 40.2 %copy-start.3 = (bf16[3,128,768]{2,1,0:T(8,128)(2,1)S(1)}, bf16[3,128,768]{2,1,0:T(8,128)(2,1)}, u32[]{:S(2)}) copy-start(bf16[3,128,768]{2,1,0:T(8,128)(2,1)} %copy-done.2) | copy-start | bytes 1769476
  107.1 19.6 %collective-permute-start.13 = (bf16[2,2,32,768]{3,2,1,0:T(8,128)(2,1)S(1)}, bf16[2,2,32,768]{3,2,1,0:T(8,128)(2,1)S(1)}, u32[]{:S(2)}, u32[]{:S(2)}) collective-permute-start(bf16[2,2,32,768]{3,2,1,0:T(8,128)(2,1)S(1)} %fusion), channel_id=1, source_target_pairs={{0,8},{8,0},{1,9},{9,1},{2,10},{10,2},{3,11},{11,3},{4,12},{12,4},... | collective-permute-start | bytes 589832 | tf_op jit(solution)/shard_map/ppermute | solution.py:221
  109.3 17.5 %collective-permute-start.11 = (bf16[2,32,768]{2,1,0:T(8,128)(2,1)S(1)}, bf16[2,32,768]{2,1,0:T(8,128)(2,1)S(1)}, u32[]{:S(2)}, u32[]{:S(2)}) collective-permute-start(bf16[2,32,768]{2,1,0:T(8,128)(2,1)S(1)} %bitcast.51), channel_id=1, source_target_pairs={{0,16},{4,20},{16,32},{20,36},{24,8},{28,12},{32,48},{36,52},{40,2... | collective-permute-start | bytes 294920 | tf_op jit(solution)/shard_map/ppermute | solution.py:337
  113.5 13.1 %all-to-all-start.1 = ((f32[16,8,12]{2,1,0:T(8,128)}), f32[16,8,12]{2,1,0:T(8,128)S(1)}, u32[]{:S(2)}, u32[]{:S(2)}) async-start(f32[16,8,12]{2,1,0:T(8,128)} %broadcast_in_dim.61), calls=%async_computation.1 | async-start | bytes 131072 | tf_op jit(solution)/shard_map/all_to_all | solution.py:227
  117.7 16.4 %collective-permute-start.10 = (bf16[3,128,768]{2,1,0:T(8,128)(2,1)S(1)}, bf16[3,128,768]{2,1,0:T(8,128)(2,1)S(1)}, u32[]{:S(2)}, u32[]{:S(2)}) collective-permute-start(bf16[3,128,768]{2,1,0:T(8,128)(2,1)S(1)} %copy-done.3), channel_id=1, source_target_pairs={{0,4},{4,0},{1,5},{5,1},{2,6},{6,2},{3,7},{7,3},{8,12},{12,8},{9,1... | collective-permute-start | bytes 1769480 | tf_op jit(solution)/shard_map/ppermute | solution.py:221
  126.9 5.8 %collective-permute-start.14 = (bf16[2,32,768]{2,1,0:T(8,128)(2,1)S(1)}, bf16[2,32,768]{2,1,0:T(8,128)(2,1)S(1)}, u32[]{:S(2)}, u32[]{:S(2)}) collective-permute-start(bf16[2,32,768]{2,1,0:T(8,128)(2,1)S(1)} %get-tuple-element.69), channel_id=1, source_target_pairs={{0,4},{4,0},{1,5},{5,1},{2,6},{6,2},{3,7},{7,3},{8,12},{12,8},{9,1... | collective-permute-start | bytes 294920 | tf_op jit(solution)/shard_map/ppermute | solution.py:221

commit v4 on v3

--- a/solution.py
+++ b/solution.py
@@ -9,13 +9,13 @@
 from jax.sharding import PartitionSpec as P
 
 SEQ = ("seq_0", "seq_1", "seq_2", "seq_3")
-FIRST = ("seq_0", "seq_2")
-SECOND = ("seq_1", "dp")
+PLANE = ("seq_0", "seq_1")
+COLUMN = ("seq_2", "seq_3", "dp")
 HALF = "seq_2"
 CORE = "seq_3"
 SLOTS = 8
-STEP_HEADS = 3
-VMEM = 28 * 1024 * 1024
+STEP_HEADS = 6
+VMEM = 36 * 1024 * 1024
 
 
 def dot(a, b, contract_a, contract_b):
@@ -45,9 +45,13 @@
     q = (mine[0, 0, :, lanes], other[0, :, lanes])
     k = (mine[0, 1, :, lanes], other[1, :, lanes])
     v = (mine[0, 2, :, lanes], other[2, :, lanes])
-    ka = jnp.concatenate([ref[0, :, lanes] for ref in audio], axis=0)
-    va = jnp.concatenate([ref[1, :, lanes] for ref in audio], axis=0)
-    return q, k, v, ka, va
+    own, zed, far, same, opposite = audio
+
+    def window(i):
+        pieces = [ref[b, i, :, lanes] for ref in (own, zed, far) for b in range(2)]
+        return jnp.concatenate(pieces + [same[i, :, lanes], opposite[i, :, lanes]], axis=0)
+
+    return q, k, v, window(0), window(1)
 
 
 def scores_of(q, k, ka, scale, bias, rows):
@@ -70,7 +74,7 @@
 
 def teacher_kernel(dim, core, bias, scal, mine, other, *refs):
     *audio_refs, target = refs
-    rows = audio_refs[0].shape[1]
+    rows = audio_refs[0].shape[2]
     for i in range(target.shape[0]):
         lanes = slice(i * dim, (i + 1) * dim)
         q, k, v, ka, va = load_head(lanes, mine, other, audio_refs)
@@ -90,9 +94,9 @@
 
 
 def student_kernel(dim, core, bias, scal, mine, other, *refs):
-    audio_refs, target = refs[:SLOTS], refs[SLOTS]
-    grad_mine, grad_other, own_out, zed_out, far_out, opposite_out, totals = refs[SLOTS + 1 :]
-    rows = audio_refs[0].shape[1]
+    audio_refs, target = refs[:5], refs[5]
+    grad_mine, grad_other, own_out, zed_out, far_out, opposite_out, totals = refs[6:]
+    rows = audio_refs[0].shape[2]
     scale = dim**-0.5
     heads = target.shape[0]
     for i in range(heads):
@@ -146,11 +150,10 @@
     mine = pl.BlockSpec((1, 3, vb, width), lambda h, c: (0, 0, 0, c[0] * steps + h))
     video = pl.BlockSpec((3, vb, width), lambda h, c: (0, 0, h))
 
-    def piece(x):
-        at = which if x.shape[0] > 2 else 0
-        return pl.BlockSpec((2, x.shape[1], width), lambda h, c: (at, 0, h))
-
-    return [smem, smem, mine, video] + [piece(x) for x in audio]
+    rows = audio[0].shape[2]
+    pair = pl.BlockSpec((2, 2, rows, width), lambda h, c: (0, 0, 0, h))
+    single = pl.BlockSpec((2, rows, width), lambda h, c: (which, 0, h))
+    return [smem, smem, mine, video] + [pair] * 3 + [single] * 2
 
 
 def teacher_call(core, bias, scal, mine, other, audio, head_dim):
@@ -177,7 +180,7 @@
 
 def student_call(core, bias, scal, mine, other, audio, target, head_dim):
     vb, half_width = mine.shape[2], other.shape[2]
-    rows = audio[0].shape[1]
+    rows = audio[0].shape[2]
     width = STEP_HEADS * head_dim
     steps = half_width // width
     in_specs = specs(steps, width, vb, audio, 1)
@@ -189,7 +192,10 @@
 
     outs = [
         (jax.ShapeDtypeStruct(mine.shape, jnp.bfloat16), in_specs[2]),
-        (jax.ShapeDtypeStruct(other.shape, jnp.bfloat16), in_specs[3]),
+        (
+            jax.ShapeDtypeStruct((3, vb, half_width), jnp.bfloat16),
+            pl.BlockSpec((3, vb, width), lambda h, c: (0, 0, h)),
+        ),
         blocks(2, jnp.float32),
         blocks(2, jnp.float32),
         blocks(3, jnp.bfloat16),
@@ -262,28 +268,34 @@
     def part(x, which):
         return lax.dynamic_slice_in_dim(x, which * half_width, half_width, x.ndim - 1)
 
+    span = alignment[0, 0]
+    rows = teacher_audio.shape[2]
+    upper = lax.broadcasted_iota(jnp.int32, (1, rows, half_width), 1) < rows // 2
+    slab = jnp.where(upper, span[0], span[1]).astype(jnp.bfloat16)
     audio = jnp.concatenate([teacher_audio[0], student_audio[0]], axis=0)
     kept = part(audio, core)
-    got = swap(part(audio, 1 - core), CORE)
+    received = swap(jnp.concatenate([part(audio, 1 - core), slab], axis=0), CORE)
+    got = received[:4]
+    span_other = jnp.stack([received[4, 0, 0], received[4, rows // 2, 0]]).astype(jnp.int32)
     inner = core == half
-    zed_kept, got, teacher_video, alignment, guidance_index, step_index = (
+    pairs = [jnp.stack([kept[i : i + 2], got[i : i + 2]]) for i in (0, 2)]
+    zeds = [swap(pair, HALF) for pair in pairs]
+    zeds[0], teacher_video, student_video, guidance_index, step_index, span_other = (
         lax.optimization_barrier(
-            (swap(kept, HALF), got, teacher_video, alignment, guidance_index, step_index)
+            (zeds[0], teacher_video, student_video, guidance_index, step_index, span_other)
         )
     )
-    zed_got, far_kept, same, opposite, teach_other, spans = lax.optimization_barrier(
-        (
-            swap(got, HALF),
-            lax.ppermute(zed_kept, SEQ, far_out),
-            lax.ppermute(jnp.where(inner, got, kept), SEQ, far_out),
-            lax.ppermute(jnp.where(inner, kept, got), SEQ, far_back),
-            swap(part(teacher_video[0], 1 - core), CORE),
-            lax.all_gather(alignment[0, 0], CORE),
-        )
-    )
-    far_got = [lax.ppermute(zed_got[i : i + 2], SEQ, far_out) for i in (0, 2)]
-    far_got[0], student_video = lax.optimization_barrier((far_got[0], student_video))
+    teach_other = swap(part(teacher_video[0], 1 - core), CORE)
     pupil_other = swap(part(student_video[0], 1 - core), CORE)
+    same = lax.ppermute(jnp.where(inner, got, kept), SEQ, far_out)
+    opposite = lax.ppermute(jnp.where(inner, kept, got), SEQ, far_back)
+    zeds[1], same, opposite = lax.optimization_barrier(
+        (zeds[1], same, opposite)
+    )
+    zeds, teach_other = lax.optimization_barrier(
+        (zeds, teach_other)
+    )
+    fars = [lax.ppermute(zed, SEQ, far_out) for zed in zeds]
 
     side = 2 - 4 * half
     near = 7 * half
@@ -299,8 +311,8 @@
             base + 4 - near,
         ]
     )
-    span = jnp.where(core == 0, spans, spans[::-1])
-    first, length = span[None, :, 0], span[None, :, 1]
+    spans = jnp.stack([span, span_other])
+    first, length = spans[None, :, 0], spans[None, :, 1]
     used = (owners[:, None] >= first) & (owners[:, None] < first + length) & (null_flag[0] == 0)
     bias = jnp.where(used, 0.0, -jnp.inf).astype(jnp.float32).reshape(2 * SLOTS)
 
@@ -315,10 +327,7 @@
     scal = jnp.concatenate([jnp.stack([weight, loss_weight]), factor])
     which = core.astype(jnp.int32)[None]
 
-    windows = [
-        (kept, got, zed_kept, zed_got, far_kept, far_got[i], same, opposite)
-        for i in range(2)
-    ]
+    windows = [(pair, zed, far, same, opposite) for pair, zed, far in zip(pairs, zeds, fars)]
     target = teacher_call(which, bias, scal, teacher_video, teach_other, windows[0], head_dim)
     grad_video, grad_other, own, zed, far, opposite, totals = student_call(
         which, bias, scal, student_video, pupil_other, windows[1], target, head_dim
@@ -332,27 +341,31 @@
         levels[:, None] == level_index, head_totals[None, :], jnp.zeros_like(gamma)
     )
     far_in = lax.ppermute(far, SEQ, far_back)
-    far_in, contribution = lax.optimization_barrier((far_in, everywhere(contribution, FIRST)))
+    opposite_in = lax.ppermute(opposite[0], SEQ, far_out)
+    other_in = swap(grad_other, CORE)
+    far_in, opposite_in, other_in, contribution = lax.optimization_barrier(
+        (far_in, opposite_in, other_in, contribution)
+    )
+    grad_video = lax.dynamic_update_slice_in_dim(
+        grad_video, other_in[None], (1 - core) * half_width, 3
+    )
     far_in = far_in.astype(jnp.float32)
-    opposite_in = lax.ppermute(opposite[0], SEQ, far_out).astype(jnp.float32)
     zed_in = swap((zed + far_in[:2]).astype(jnp.bfloat16), HALF)
-    zed_in, gamma_grad = lax.optimization_barrier((zed_in, everywhere(contribution, SECOND)))
-    zed_in = zed_in.astype(jnp.float32)
-    near_in = (far_in[2], opposite_in)
+    near_in = (far_in[2], opposite_in.astype(jnp.float32))
     keep = own[0] + jnp.where(inner, near_in[1], near_in[0])
     leave = own[1] + jnp.where(inner, near_in[0], near_in[1])
+    zed_in, contribution, keep, leave, grad_video = lax.optimization_barrier(
+        (zed_in, everywhere(contribution, COLUMN), keep, leave, grad_video)
+    )
+    zed_in = zed_in.astype(jnp.float32)
     keep = (keep + zed_in[0]).astype(jnp.bfloat16)
     arrived = swap((leave + zed_in[1]).astype(jnp.bfloat16), CORE)
-    gamma_grad, arrived = lax.optimization_barrier((lax.psum(gamma_grad, CORE), arrived))
+    gamma_grad, arrived = lax.optimization_barrier((everywhere(contribution, PLANE), arrived))
     grad_audio = jnp.where(
         core == 0,
         jnp.concatenate([keep, arrived], axis=-1),
         jnp.concatenate([arrived, keep], axis=-1),
     )[None]
-    grad_video = lax.dynamic_update_slice_in_dim(
-        grad_video, swap(grad_other, CORE)[None], (1 - core) * half_width, 3
-    )
-
     gamma_grad = gamma_grad / (tokens * count * head_dim)
     return (grad_video, grad_audio, gamma_grad)
 

time: 136 us -> 133 us (0.978)
  blocking collectives: 34.5 us -> 0 us
  waiting for transfers between devices: 6.57 us -> 28.3 us
  starting transfers between devices: 68.2 us -> 77.1 us
  other arithmetic: 3.27 us -> 5.22 us
    all_to_all x1 -> x0, blocking collectives: 29.4 us -> none  [everywhere(): return jnp.sum(lax.all_to_all(copies, axes, 0, 0), axis=0)]
    all_to_all x1 -> x2, starting transfers between devices: 4.19 us -> 24.3 us  [everywhere(): return jnp.sum(lax.all_to_all(copies, axes, 0, 0), axis=0)]
    all_to_all x1 -> x2, waiting for transfers between devices: 4.81 us -> 16.5 us  [everywhere(): return jnp.sum(lax.all_to_all(copies, axes, 0, 0), axis=0)]
    ppermute x8, starting transfers between devices: 42.9 us -> 37.3 us  [swap(): return lax.ppermute(x, axis, [(0, 1), (1, 0)])]
    ppermute x6 -> x5, starting transfers between devices: 19.7 us -> 14.2 us  [the longest x2 6.62 us: body(): fars = [lax.ppermute(zed, SEQ, far_out) for zed in zeds]]
    ppermute x6 -> x5, waiting for transfers between devices: 0.02 us -> 5.41 us  [the longest x1 3.64 us: body(): opposite = lax.ppermute(jnp.where(inner, kept, got), SEQ, far_back)]
    ppermute x1, waiting for transfers between devices: 0.01 us -> 3.23 us  [body(): far_in = lax.ppermute(far, SEQ, far_back)]
    convert_element_type x0 -> x2, other arithmetic: none -> 2.66 us  [the longest x1 1.37 us: body(): jnp.stack([received[4, 0, 0], received[4, rows // 2, 0]]).astype(jnp.int32)]
  transfers between devices with their start and end apart: 16 -> 16, of which waited for: 2 -> 6; matrix products, arithmetic and copies ran while one was open for 4% -> 5% of each run, Pallas kernels for 3% -> 2%
where the time goes in v4:
time: 133 us
  starting transfers between devices  77.1 us (58%)
  waiting for transfers between devices  28.3 us (21%)
  Pallas kernels  10.6 us (8%)
  local copies, waits for them, and re-layouts  8.5 us (6%)
  other arithmetic  5.22 us (4%)
  between operations  3 us (2%)
    ppermute x8, starting transfers between devices, swap(): return lax.ppermute(x, axis, [(0, 1), (1, 0)])  37.3 us
    all_to_all x2, starting transfers between devices, everywhere(): return jnp.sum(lax.all_to_all(copies, axes, 0, 0), axis=0)  24.3 us
    all_to_all x2, waiting for transfers between devices, everywhere(): return jnp.sum(lax.all_to_all(copies, axes, 0, 0), axis=0)  16.5 us
    pallas_call x1, Pallas kernels, student_call(): pl.pallas_call(functools.partial(student_kernel, head_dim), grid_spec=plt...  7.26 us
    ppermute x2, starting transfers between devices, body(): fars = [lax.ppermute(zed, SEQ, far_out) for zed in zeds]  6.62 us
    ppermute x1, starting transfers between devices, body(): opposite_in = lax.ppermute(opposite[0], SEQ, far_out)  4.85 us
    ppermute x1, waiting for transfers between devices, body(): opposite = lax.ppermute(jnp.where(inner, kept, got), SEQ, far_back)  3.64 us
    pallas_call x1, Pallas kernels, teacher_call(): pl.pallas_call(functools.partial(teacher_kernel, head_dim), grid_spec=plt...  3.3 us
  transfers between devices with their start and end apart: 16, of which 6 were waited for; matrix products, arithmetic and copies ran while one was open for 5% of the time, Pallas kernels for 2%

profile of v4, /device:TPU:1, one launch (start us, length us, event | category | flops | bytes accessed | tf_op | source)
XLA Modules:
  0.0 132.7 jit_solution(3610411716815296659)
XLA Ops:
  0.6 0.0 copy-start.4
  0.6 0.0 copy-start.5
  0.7 1.3 fusion.13
  2.0 1.3 fusion.10
  3.3 1.0 fusion.3
  4.3 0.1 iota.12
  4.4 8.8 %collective-permute-start = (bf16[5,32,768]{2,1,0:T(8,128)(2,1)S(1)}, bf16[5,32,768]{2,1,0:T(8,128)(2,1)S(1)}, u32[]{:S(2)}, u32[]{:S(2)}) collective-permute-start(bf16[5,32,768]{2,1,0:T(8,128)(2,1)S(1)} %pad_maximum_fusion), channel_id=1, source_target_pairs={{0,4},{4,0},{1,5},{5,1},{2,6},{6,2},{3,7},{7,3},{8,12},{12,8},{9,1... | collective-permute-start | bytes 737288 | tf_op jit(solution)/shard_map/ppermute | solution.py:227
  15.2 0.1 select_reduce_fusion
  15.3 0.1 dynamic_slice.21
  15.4 0.1 stack.66
  15.4 0.0 collective-permute-done
  15.5 0.1 broadcast_select_fusion
  15.6 0.0 copy-start.1
  15.6 5.4 %collective-permute-start.1 = (bf16[2,2,32,768]{3,2,1,0:T(8,128)(2,1)S(1)}, bf16[2,2,32,768]{3,2,1,0:T(8,128)(2,1)S(1)}, u32[]{:S(2)}, u32[]{:S(2)}) collective-permute-start(bf16[2,2,32,768]{3,2,1,0:T(8,128)(2,1)S(1)} %pad_maximum_fusion.1.refs_0_), channel_id=1, source_target_pairs={{0,8},{8,0},{1,9},{9,1},{2,10},{10,2},{3,11},{11,3},{4,12},{12,4},... | collective-permute-start | bytes 589832 | tf_op jit(solution)/shard_map/ppermute | solution.py:227
  21.0 3.9 %collective-permute-start.3 = (bf16[2,2,32,768]{3,2,1,0:T(8,128)(2,1)S(1)}, bf16[2,2,32,768]{3,2,1,0:T(8,128)(2,1)S(1)}, u32[]{:S(2)}, u32[]{:S(2)}) collective-permute-start(bf16[2,2,32,768]{3,2,1,0:T(8,128)(2,1)S(1)} %pad_maximum_fusion.2.refs_0_), channel_id=1, source_target_pairs={{0,8},{8,0},{1,9},{9,1},{2,10},{10,2},{3,11},{11,3},{4,12},{12,4},... | collective-permute-start | bytes 589832 | tf_op jit(solution)/shard_map/ppermute | solution.py:227
  25.0 0.5 fusion.12
  25.5 1.4 %maximum_convert_fusion = s32[2]{0:T(128)S(1)} fusion(bf16[1]{0:T(256)(128)(2,1)} %bitcast.17, bf16[1]{0:T(256)(128)(2,1)} %bitcast.16), kind=kLoop, calls=%fused_computation.42 | loop fusion | flops 8 | bytes 12 | tf_op jit(solution)/shard_map/convert_element_type | solution.py:279
  26.9 3.1 %collective-permute-done.1.refs_1_ = bf16[2,2,32,768]{3,2,1,0:T(8,128)(2,1)S(1)} collective-permute-done((bf16[2,2,32,768]{3,2,1,0:T(8,128)(2,1)S(1)}, bf16[2,2,32,768]{3,2,1,0:T(8,128)(2,1)S(1)}, u32[]{:S(2)}, u32[]{:S(2)}) %collective-permute-start.1) | collective-permute-done | bytes 196640 | tf_op jit(solution)/shard_map/ppermute | solution.py:227
  30.0 0.0 copy-start.6
  30.0 3.1 %collective-permute-start.6 = (bf16[3,128,768]{2,1,0:T(8,128)(2,1)S(1)}, bf16[3,128,768]{2,1,0:T(8,128)(2,1)S(1)}, u32[]{:S(2)}, u32[]{:S(2)}) collective-permute-start(bf16[3,128,768]{2,1,0:T(8,128)(2,1)S(1)} %dynamic-slice_bitcast_fusion), channel_id=1, source_target_pairs={{0,4},{4,0},{1,5},{5,1},{2,6},{6,2},{3,7},{7,3},{8,12},{12,8},{9,1... | collective-permute-start | bytes 1769480 | tf_op jit(solution)/shard_map/ppermute | solution.py:227
  33.2 1.4 %collective-permute-start.4 = (bf16[4,32,768]{2,1,0:T(8,128)(2,1)S(1)}, bf16[4,32,768]{2,1,0:T(8,128)(2,1)S(1)}, u32[]{:S(2)}, u32[]{:S(2)}) collective-permute-start(bf16[4,32,768]{2,1,0:T(8,128)(2,1)S(1)} %broadcast_select_fusion.1), channel_id=1, source_target_pairs={{0,16},{4,20},{16,32},{20,36},{24,8},{28,12},{32,48},{36,52},{40,2... | collective-permute-start | bytes 589832 | tf_op jit(solution)/shard_map/ppermute | solution.py:290
  34.6 1.3 collective-permute-start.5
  35.9 0.9 dynamic-slice_bitcast_fusion.1
  36.8 2.2 %collective-permute-start.2 = (bf16[3,128,768]{2,1,0:T(8,128)(2,1)}, bf16[3,128,768]{2,1,0:T(8,128)(2,1)}, u32[]{:S(2)}, u32[]{:S(2)}) collective-permute-start(bf16[3,128,768]{2,1,0:T(8,128)(2,1)} %dynamic-slice_bitcast_fusion.1), channel_id=1, source_target_pairs={{0,4},{4,0},{1,5},{5,1},{2,6},{6,2},{3,7},{7,3},{8,12},{12,8},{9,1... | collective-permute-start | bytes 1769480 | tf_op jit(solution)/shard_map/ppermute | solution.py:227
  39.0 0.1 pad_maximum_fusion.3.scal
  39.1 0.0 collective-permute-done.3.refs_1_
  39.1 0.0 collective-permute-done.4.refs_3_
  39.1 3.6 %collective-permute-done.5.refs_4_ = bf16[4,32,768]{2,1,0:T(8,128)(2,1)S(1)} collective-permute-done((bf16[4,32,768]{2,1,0:T(8,128)(2,1)S(1)}, bf16[4,32,768]{2,1,0:T(8,128)(2,1)S(1)}, u32[]{:S(2)}, u32[]{:S(2)}) %collective-permute-start.5) | collective-permute-done | bytes 196640 | tf_op jit(solution)/shard_map/ppermute | solution.py:291
  42.7 0.2 slice_reduce_fusion
  42.9 0.0 collective-permute-done.6.other
  42.9 0.8 copy-done.2
  43.8 3.8 %collective-permute-start.8 = (bf16[2,2,32,768]{3,2,1,0:T(8,128)(2,1)S(1)}, bf16[2,2,32,768]{3,2,1,0:T(8,128)(2,1)}, u32[]{:S(2)}, u32[]{:S(2)}) collective-permute-start(bf16[2,2,32,768]{3,2,1,0:T(8,128)(2,1)S(1)} %collective-permute-done.1.refs_1_), channel_id=1, source_target_pairs={{0,16},{4,20},{16,32},{20,36},{24,8},{28,12},{32,48},{36,52},{40,2... | collective-permute-start | bytes 589832 | tf_op jit(solution)/shard_map/ppermute | solution.py:298
  47.6 2.8 %collective-permute-start.7 = (bf16[2,2,32,768]{3,2,1,0:T(8,128)(2,1)S(1)}, bf16[2,2,32,768]{3,2,1,0:T(8,128)(2,1)}, u32[]{:S(2)}, u32[]{:S(2)}) collective-permute-start(bf16[2,2,32,768]{3,2,1,0:T(8,128)(2,1)S(1)} %collective-permute-done.3.refs_1_), channel_id=1, source_target_pairs={{0,16},{4,20},{16,32},{20,36},{24,8},{28,12},{32,48},{36,52},{40,2... | collective-permute-start | bytes 589832 | tf_op jit(solution)/shard_map/ppermute | solution.py:298
  50.4 0.1 and_select_fusion
  50.5 0.1 select_n.79.bias
  50.6 1.1 copy-done.3
  51.6 3.3 %teacher.1.refs_5_ = f32[6,128,256]{2,1,0:T(8,128)S(1)} custom-call(s32[1]{0:T(128)} %bitcast.core, f32[16]{0:T(128)S(1)} %select_n.79.bias, f32[8]{0:T(128)S(1)} %pad_maximum_fusion.3.scal, bf16[1,3,128,1536]{3,2,1,0:T(8,128)(2,1)S(1)} %copy-done, bf16[3,128,768]{2,1,0:T(8,128)(2,1)S(1)} %copy-done.3, ...), custom_call_target="tpu_custom_call" | custom-call | flops 600000000 | bytes 4000000 | tf_op jit(solution)/shard_map/teacher/pallas_call | solution.py:164
  54.9 0.0 collective-permute-done.2.other
  54.9 0.0 collective-permute-done.7.refs_2_
  54.9 7.3 %student.1 = (bf16[1,3,128,1536]{3,2,1,0:T(8,128)(2,1)}, bf16[3,128,768]{2,1,0:T(8,128)(2,1)}, f32[2,2,32,768]{3,2,1,0:T(8,128)S(1)}, f32[2,2,32,768]{3,2,1,0:T(...) custom-call(s32[1]{0:T(128)} %bitcast.core, ...), custom_call_target="tpu_custom_call" | custom-call | flops 900000000 | bytes 8000000 | tf_op jit(solution)/shard_map/student/pallas_call | solution.py:208
  62.2 4.6 %collective-permute-start.11 = (bf16[3,128,768]{2,1,0:T(8,128)(2,1)}, bf16[3,128,768]{2,1,0:T(8,128)(2,1)S(1)}, u32[]{:S(2)}, u32[]{:S(2)}) collective-permute-start(bf16[3,128,768]{2,1,0:T(8,128)(2,1)} %get-tuple-element.48), channel_id=1, source_target_pairs={{0,4},{4,0},{1,5},{5,1},{2,6},{6,2},{3,7},{7,3},{8,12},{12,8},{9,1... | collective-permute-start | bytes 1769480 | tf_op jit(solution)/shard_map/ppermute | solution.py:227
  66.9 1.3 collective-permute-start.9
  68.2 4.8 %collective-permute-start.10 = (bf16[2,32,768]{2,1,0:T(8,128)(2,1)S(1)}, bf16[2,32,768]{2,1,0:T(8,128)(2,1)S(1)}, u32[]{:S(2)}, u32[]{:S(2)}) collective-permute-start(bf16[2,32,768]{2,1,0:T(8,128)(2,1)S(1)} %bitcast.64), channel_id=1, source_target_pairs={{0,16},{4,20},{16,32},{20,36},{24,8},{28,12},{32,48},{36,52},{40,2... | collective-permute-start | bytes 294920 | tf_op jit(solution)/shard_map/ppermute | solution.py:344
  73.0 0.1 reduce_sum.37
  73.1 0.2 dynamic_update_slice.8
  73.4 0.1 broadcast_select_fusion.2
  73.5 1.8 %collective-permute-done.10 = bf16[2,32,768]{2,1,0:T(8,128)(2,1)S(1)} collective-permute-done((bf16[2,32,768]{2,1,0:T(8,128)(2,1)S(1)}, bf16[2,32,768]{2,1,0:T(8,128)(2,1)S(1)}, u32[]{:S(2)}, u32[]{:S(2)}) %collective-permute-start.10) | collective-permute-done | bytes 98336 | tf_op jit(solution)/shard_map/ppermute | solution.py:344
  75.2 3.2 %collective-permute-done.9 = bf16[3,2,32,768]{3,2,1,0:T(8,128)(2,1)S(1)} collective-permute-done((bf16[3,2,32,768]{3,2,1,0:T(8,128)(2,1)S(1)}, bf16[3,2,32,768]{3,2,1,0:T(8,128)(2,1)S(1)}, u32[]{:S(2)}, u32[]{:S(2)}) %collective-permute-start.9) | collective-permute-done | bytes 294944 | tf_op jit(solution)/shard_map/ppermute | solution.py:343
  78.5 6.9 %collective-permute-start.12 = (bf16[2,2,32,768]{3,2,1,0:T(8,128)(2,1)S(1)}, bf16[2,2,32,768]{3,2,1,0:T(8,128)(2,1)S(1)}, u32[]{:S(2)}, u32[]{:S(2)}) collective-permute-start(bf16[2,2,32,768]{3,2,1,0:T(8,128)(2,1)S(1)} %fusion), channel_id=1, source_target_pairs={{0,8},{8,0},{1,9},{9,1},{2,10},{10,2},{3,11},{11,3},{4,12},{12,4},... | collective-permute-start | bytes 589832 | tf_op jit(solution)/shard_map/ppermute | solution.py:227
  85.5 0.6 broadcast_in_dim.72
  86.1 7.7 %all-to-all-start = ((f32[16,8,12]{2,1,0:T(8,128)}), f32[16,8,12]{2,1,0:T(8,128)S(1)}, u32[]{:S(2)}, u32[]{:S(2)}) async-start(f32[16,8,12]{2,1,0:T(8,128)} %broadcast_in_dim.72), calls=%async_computation | async-start | bytes 131072 | tf_op jit(solution)/shard_map/all_to_all | solution.py:233
  93.8 0.9 bitcast_dynamic-update-slice_fusion
  94.7 6.7 %all-to-all-done = f32[16,8,12]{2,1,0:T(8,128)S(1)} async-done(((f32[16,8,12]{2,1,0:T(8,128)}), f32[16,8,12]{2,1,0:T(8,128)S(1)}, u32[]{:S(2)}, u32[]{:S(2)}) %all-to-all-start) | async-done | bytes 6176 | tf_op jit(solution)/shard_map/all_to_all | solution.py:233
  101.4 0.1 copy.22
  101.5 0.0 collective-permute-done.12
  101.6 2.3 %collective-permute-start.13 = (bf16[2,32,768]{2,1,0:T(8,128)(2,1)S(1)}, bf16[2,32,768]{2,1,0:T(8,128)(2,1)S(1)}, u32[]{:S(2)}, u32[]{:S(2)}) collective-permute-start(bf16[2,32,768]{2,1,0:T(8,128)(2,1)S(1)} %get-tuple-element.79), channel_id=1, source_target_pairs={{0,4},{4,0},{1,5},{5,1},{2,6},{6,2},{3,7},{7,3},{8,12},{12,8},{9,1... | collective-permute-start | bytes 294920 | tf_op jit(solution)/shard_map/ppermute | solution.py:227
  103.9 0.1 copy.19
  104.0 0.7 broadcast_in_dim.74
  104.6 16.7 %all-to-all-start.1 = ((f32[32,8,12]{2,1,0:T(8,128)}), f32[32,8,12]{2,1,0:T(8,128)S(1)}, u32[]{:S(2)}, u32[]{:S(2)}) async-start(f32[32,8,12]{2,1,0:T(8,128)} %broadcast_in_dim.74), calls=%async_computation.1 | async-start | bytes 262144 | tf_op jit(solution)/shard_map/all_to_all | solution.py:233
  121.3 9.8 %all-to-all-done.1 = f32[32,8,12]{2,1,0:T(8,128)S(1)} async-done(((f32[32,8,12]{2,1,0:T(8,128)}), f32[32,8,12]{2,1,0:T(8,128)S(1)}, u32[]{:S(2)}, u32[]{:S(2)}) %all-to-all-start.1) | async-done | bytes 12320 | tf_op jit(solution)/shard_map/all_to_all | solution.py:233
  131.2 0.1 copy.23
  131.3 0.0 collective-permute-done.13
  131.3 0.7 copy.21
  132.0 0.7 maximum_select_fusion
  (30 shorter events, 0.5 us)
Async XLA Ops:
  0.6 14.8 %copy-start.4 = (bf16[1,2,32,1536]{3,2,1,0:T(8,128)(2,1)S(1)}, bf16[1,2,32,1536]{3,2,1,0:T(8,128)(2,1)}, u32[]{:S(2)}) copy-start(bf16[1,2,32,1536]{3,2,1,0:T(8,128)(2,1)} %param.11) | copy-start | bytes 589828
  0.6 14.8 %copy-start.5 = (bf16[1,2,32,1536]{3,2,1,0:T(8,128)(2,1)S(1)}, bf16[1,2,32,1536]{3,2,1,0:T(8,128)(2,1)}, u32[]{:S(2)}) copy-start(bf16[1,2,32,1536]{3,2,1,0:T(8,128)(2,1)} %param.12) | copy-start | bytes 589828
  0.7 14.5 %copy-start.7 = (f32[8,12]{1,0:T(8,128)S(1)}, f32[8,12]{1,0:T(8,128)}, u32[]{:S(2)}) copy-start(f32[8,12]{1,0:T(8,128)} %param.17) | copy-start | bytes 1156
  4.4 11.1 %collective-permute-start = (bf16[5,32,768]{2,1,0:T(8,128)(2,1)S(1)}, bf16[5,32,768]{2,1,0:T(8,128)(2,1)S(1)}, u32[]{:S(2)}, u32[]{:S(2)}) collective-permute-start(bf16[5,32,768]{2,1,0:T(8,128)(2,1)S(1)} %pad_maximum_fusion), channel_id=1, source_target_pairs={{0,4},{4,0},{1,5},{5,1},{2,6},{6,2},{3,7},{7,3},{8,12},{12,8},{9,1... | collective-permute-start | bytes 737288 | tf_op jit(solution)/shard_map/ppermute | solution.py:227
  15.4 14.5 %copy-start = (bf16[1,3,128,1536]{3,2,1,0:T(8,128)(2,1)S(1)}, bf16[1,3,128,1536]{3,2,1,0:T(8,128)(2,1)}, u32[]{:S(2)}) copy-start(bf16[1,3,128,1536]{3,2,1,0:T(8,128)(2,1)} %mine) | copy-start | bytes 3538948
  15.6 20.3 %copy-start.1 = (bf16[1,3,128,1536]{3,2,1,0:T(8,128)(2,1)S(1)}, bf16[1,3,128,1536]{3,2,1,0:T(8,128)(2,1)}, u32[]{:S(2)}) copy-start(bf16[1,3,128,1536]{3,2,1,0:T(8,128)(2,1)} %mine.1) | copy-start | bytes 3538948
  15.6 14.4 %collective-permute-start.1 = (bf16[2,2,32,768]{3,2,1,0:T(8,128)(2,1)S(1)}, bf16[2,2,32,768]{3,2,1,0:T(8,128)(2,1)S(1)}, u32[]{:S(2)}, u32[]{:S(2)}) collective-permute-start(bf16[2,2,32,768]{3,2,1,0:T(8,128)(2,1)S(1)} %pad_maximum_fusion.1.refs_0_), channel_id=1, source_target_pairs={{0,8},{8,0},{1,9},{9,1},{2,10},{10,2},{3,11},{11,3},{4,12},{12,4},... | collective-permute-start | bytes 589832 | tf_op jit(solution)/shard_map/ppermute | solution.py:227
  21.0 18.0 %collective-permute-start.3 = (bf16[2,2,32,768]{3,2,1,0:T(8,128)(2,1)S(1)}, bf16[2,2,32,768]{3,2,1,0:T(8,128)(2,1)S(1)}, u32[]{:S(2)}, u32[]{:S(2)}) collective-permute-start(bf16[2,2,32,768]{3,2,1,0:T(8,128)(2,1)S(1)} %pad_maximum_fusion.2.refs_0_), channel_id=1, source_target_pairs={{0,8},{8,0},{1,9},{9,1},{2,10},{10,2},{3,11},{11,3},{4,12},{12,4},... | collective-permute-start | bytes 589832 | tf_op jit(solution)/shard_map/ppermute | solution.py:227
  30.0 12.7 %copy-start.6 = (s32[1,1,2]{2,1,0:T(1,128)S(1)}, s32[1,1,2]{2,1,0:T(1,128)}, u32[]{:S(2)}) copy-start(s32[1,1,2]{2,1,0:T(1,128)} %param.13) | copy-start | bytes 28
  30.0 12.9 %collective-permute-start.6 = (bf16[3,128,768]{2,1,0:T(8,128)(2,1)S(1)}, bf16[3,128,768]{2,1,0:T(8,128)(2,1)S(1)}, u32[]{:S(2)}, u32[]{:S(2)}) collective-permute-start(bf16[3,128,768]{2,1,0:T(8,128)(2,1)S(1)} %dynamic-slice_bitcast_fusion), channel_id=1, source_target_pairs={{0,4},{4,0},{1,5},{5,1},{2,6},{6,2},{3,7},{7,3},{8,12},{12,8},{9,1... | collective-permute-start | bytes 1769480 | tf_op jit(solution)/shard_map/ppermute | solution.py:227
  33.2 5.9 %collective-permute-start.4 = (bf16[4,32,768]{2,1,0:T(8,128)(2,1)S(1)}, bf16[4,32,768]{2,1,0:T(8,128)(2,1)S(1)}, u32[]{:S(2)}, u32[]{:S(2)}) collective-permute-start(bf16[4,32,768]{2,1,0:T(8,128)(2,1)S(1)} %broadcast_select_fusion.1), channel_id=1, source_target_pairs={{0,16},{4,20},{16,32},{20,36},{24,8},{28,12},{32,48},{36,52},{40,2... | collective-permute-start | bytes 589832 | tf_op jit(solution)/shard_map/ppermute | solution.py:290
  34.6 8.1 %collective-permute-start.5 = (bf16[4,32,768]{2,1,0:T(8,128)(2,1)S(1)}, bf16[4,32,768]{2,1,0:T(8,128)(2,1)S(1)}, u32[]{:S(2)}, u32[]{:S(2)}) collective-permute-start(bf16[4,32,768]{2,1,0:T(8,128)(2,1)S(1)} %get-tuple-element.74), channel_id=1, source_target_pairs={{16,0},{20,4},{32,16},{36,20},{8,24},{12,28},{48,32},{52,36},{24,4... | collective-permute-start | bytes 589832 | tf_op jit(solution)/shard_map/ppermute | solution.py:291
  36.8 18.1 %collective-permute-start.2 = (bf16[3,128,768]{2,1,0:T(8,128)(2,1)}, bf16[3,128,768]{2,1,0:T(8,128)(2,1)}, u32[]{:S(2)}, u32[]{:S(2)}) collective-permute-start(bf16[3,128,768]{2,1,0:T(8,128)(2,1)} %dynamic-slice_bitcast_fusion.1), channel_id=1, source_target_pairs={{0,4},{4,0},{1,5},{5,1},{2,6},{6,2},{3,7},{7,3},{8,12},{12,8},{9,1... | collective-permute-start | bytes 1769480 | tf_op jit(solution)/shard_map/ppermute | solution.py:227
  42.9 0.8 copy-start.2
  43.8 6.8 %collective-permute-start.8 = (bf16[2,2,32,768]{3,2,1,0:T(8,128)(2,1)S(1)}, bf16[2,2,32,768]{3,2,1,0:T(8,128)(2,1)}, u32[]{:S(2)}, u32[]{:S(2)}) collective-permute-start(bf16[2,2,32,768]{3,2,1,0:T(8,128)(2,1)S(1)} %collective-permute-done.1.refs_1_), channel_id=1, source_target_pairs={{0,16},{4,20},{16,32},{20,36},{24,8},{28,12},{32,48},{36,52},{40,2... | collective-permute-start | bytes 589832 | tf_op jit(solution)/shard_map/ppermute | solution.py:298
  47.6 7.4 %collective-permute-start.7 = (bf16[2,2,32,768]{3,2,1,0:T(8,128)(2,1)S(1)}, bf16[2,2,32,768]{3,2,1,0:T(8,128)(2,1)}, u32[]{:S(2)}, u32[]{:S(2)}) collective-permute-start(bf16[2,2,32,768]{3,2,1,0:T(8,128)(2,1)S(1)} %collective-permute-done.3.refs_1_), channel_id=1, source_target_pairs={{0,16},{4,20},{16,32},{20,36},{24,8},{28,12},{32,48},{36,52},{40,2... | collective-permute-start | bytes 589832 | tf_op jit(solution)/shard_map/ppermute | solution.py:298
  50.5 1.1 copy-start.3
  62.2 16.2 %collective-permute-start.11 = (bf16[3,128,768]{2,1,0:T(8,128)(2,1)}, bf16[3,128,768]{2,1,0:T(8,128)(2,1)S(1)}, u32[]{:S(2)}, u32[]{:S(2)}) collective-permute-start(bf16[3,128,768]{2,1,0:T(8,128)(2,1)} %get-tuple-element.48), channel_id=1, source_target_pairs={{0,4},{4,0},{1,5},{5,1},{2,6},{6,2},{3,7},{7,3},{8,12},{12,8},{9,1... | collective-permute-start | bytes 1769480 | tf_op jit(solution)/shard_map/ppermute | solution.py:227
  66.9 11.6 %collective-permute-start.9 = (bf16[3,2,32,768]{3,2,1,0:T(8,128)(2,1)S(1)}, bf16[3,2,32,768]{3,2,1,0:T(8,128)(2,1)S(1)}, u32[]{:S(2)}, u32[]{:S(2)}) collective-permute-start(bf16[3,2,32,768]{3,2,1,0:T(8,128)(2,1)S(1)} %get-tuple-element.46), channel_id=1, source_target_pairs={{16,0},{20,4},{32,16},{36,20},{8,24},{12,28},{48,32},{52,36},{24,4... | collective-permute-start | bytes 884744 | tf_op jit(solution)/shard_map/ppermute | solution.py:343
  68.2 7.0 %collective-permute-start.10 = (bf16[2,32,768]{2,1,0:T(8,128)(2,1)S(1)}, bf16[2,32,768]{2,1,0:T(8,128)(2,1)S(1)}, u32[]{:S(2)}, u32[]{:S(2)}) collective-permute-start(bf16[2,32,768]{2,1,0:T(8,128)(2,1)S(1)} %bitcast.64), channel_id=1, source_target_pairs={{0,16},{4,20},{16,32},{20,36},{24,8},{28,12},{32,48},{36,52},{40,2... | collective-permute-start | bytes 294920 | tf_op jit(solution)/shard_map/ppermute | solution.py:344
  78.5 22.9 %collective-permute-start.12 = (bf16[2,2,32,768]{3,2,1,0:T(8,128)(2,1)S(1)}, bf16[2,2,32,768]{3,2,1,0:T(8,128)(2,1)S(1)}, u32[]{:S(2)}, u32[]{:S(2)}) collective-permute-start(bf16[2,2,32,768]{3,2,1,0:T(8,128)(2,1)S(1)} %fusion), channel_id=1, source_target_pairs={{0,8},{8,0},{1,9},{9,1},{2,10},{10,2},{3,11},{11,3},{4,12},{12,4},... | collective-permute-start | bytes 589832 | tf_op jit(solution)/shard_map/ppermute | solution.py:227
  86.1 15.3 %all-to-all-start = ((f32[16,8,12]{2,1,0:T(8,128)}), f32[16,8,12]{2,1,0:T(8,128)S(1)}, u32[]{:S(2)}, u32[]{:S(2)}) async-start(f32[16,8,12]{2,1,0:T(8,128)} %broadcast_in_dim.72), calls=%async_computation | async-start | bytes 131072 | tf_op jit(solution)/shard_map/all_to_all | solution.py:233
  101.6 29.7 %collective-permute-start.13 = (bf16[2,32,768]{2,1,0:T(8,128)(2,1)S(1)}, bf16[2,32,768]{2,1,0:T(8,128)(2,1)S(1)}, u32[]{:S(2)}, u32[]{:S(2)}) collective-permute-start(bf16[2,32,768]{2,1,0:T(8,128)(2,1)S(1)} %get-tuple-element.79), channel_id=1, source_target_pairs={{0,4},{4,0},{1,5},{5,1},{2,6},{6,2},{3,7},{7,3},{8,12},{12,8},{9,1... | collective-permute-start | bytes 294920 | tf_op jit(solution)/shard_map/ppermute | solution.py:227
  104.6 26.5 %all-to-all-start.1 = ((f32[32,8,12]{2,1,0:T(8,128)}), f32[32,8,12]{2,1,0:T(8,128)S(1)}, u32[]{:S(2)}, u32[]{:S(2)}) async-start(f32[32,8,12]{2,1,0:T(8,128)} %broadcast_in_dim.74), calls=%async_computation.1 | async-start | bytes 262144 | tf_op jit(solution)/shard_map/all_to_all | solution.py:233

commit v5 on v4

--- a/solution.py
+++ b/solution.py
@@ -14,8 +14,8 @@
 HALF = "seq_2"
 CORE = "seq_3"
 SLOTS = 8
-STEP_HEADS = 6
-VMEM = 36 * 1024 * 1024
+STEP_HEADS = 3
+VMEM = 28 * 1024 * 1024
 
 
 def dot(a, b, contract_a, contract_b):
@@ -192,10 +192,7 @@
 
     outs = [
         (jax.ShapeDtypeStruct(mine.shape, jnp.bfloat16), in_specs[2]),
-        (
-            jax.ShapeDtypeStruct((3, vb, half_width), jnp.bfloat16),
-            pl.BlockSpec((3, vb, width), lambda h, c: (0, 0, h)),
-        ),
+        (jax.ShapeDtypeStruct(other.shape, jnp.bfloat16), in_specs[3]),
         blocks(2, jnp.float32),
         blocks(2, jnp.float32),
         blocks(3, jnp.bfloat16),
@@ -268,34 +265,23 @@
     def part(x, which):
         return lax.dynamic_slice_in_dim(x, which * half_width, half_width, x.ndim - 1)
 
-    span = alignment[0, 0]
-    rows = teacher_audio.shape[2]
-    upper = lax.broadcasted_iota(jnp.int32, (1, rows, half_width), 1) < rows // 2
-    slab = jnp.where(upper, span[0], span[1]).astype(jnp.bfloat16)
     audio = jnp.concatenate([teacher_audio[0], student_audio[0]], axis=0)
     kept = part(audio, core)
-    received = swap(jnp.concatenate([part(audio, 1 - core), slab], axis=0), CORE)
-    got = received[:4]
-    span_other = jnp.stack([received[4, 0, 0], received[4, rows // 2, 0]]).astype(jnp.int32)
+    got = swap(part(audio, 1 - core), CORE)
     inner = core == half
     pairs = [jnp.stack([kept[i : i + 2], got[i : i + 2]]) for i in (0, 2)]
     zeds = [swap(pair, HALF) for pair in pairs]
-    zeds[0], teacher_video, student_video, guidance_index, step_index, span_other = (
+    zeds[0], teacher_video, student_video, alignment, guidance_index, step_index = (
         lax.optimization_barrier(
-            (zeds[0], teacher_video, student_video, guidance_index, step_index, span_other)
+            (zeds[0], teacher_video, student_video, alignment, guidance_index, step_index)
         )
     )
+    same = lax.ppermute(jnp.where(inner, got, kept), SEQ, far_out)
+    opposite = lax.ppermute(jnp.where(inner, kept, got), SEQ, far_back)
+    fars = [lax.ppermute(zed, SEQ, far_out) for zed in zeds]
     teach_other = swap(part(teacher_video[0], 1 - core), CORE)
     pupil_other = swap(part(student_video[0], 1 - core), CORE)
-    same = lax.ppermute(jnp.where(inner, got, kept), SEQ, far_out)
-    opposite = lax.ppermute(jnp.where(inner, kept, got), SEQ, far_back)
-    zeds[1], same, opposite = lax.optimization_barrier(
-        (zeds[1], same, opposite)
-    )
-    zeds, teach_other = lax.optimization_barrier(
-        (zeds, teach_other)
-    )
-    fars = [lax.ppermute(zed, SEQ, far_out) for zed in zeds]
+    spans = lax.all_gather(alignment[0, 0], CORE)
 
     side = 2 - 4 * half
     near = 7 * half
@@ -311,8 +297,8 @@
             base + 4 - near,
         ]
     )
-    spans = jnp.stack([span, span_other])
-    first, length = spans[None, :, 0], spans[None, :, 1]
+    span = jnp.where(core == 0, spans, spans[::-1])
+    first, length = span[None, :, 0], span[None, :, 1]
     used = (owners[:, None] >= first) & (owners[:, None] < first + length) & (null_flag[0] == 0)
     bias = jnp.where(used, 0.0, -jnp.inf).astype(jnp.float32).reshape(2 * SLOTS)
 
@@ -341,31 +327,26 @@
         levels[:, None] == level_index, head_totals[None, :], jnp.zeros_like(gamma)
     )
     far_in = lax.ppermute(far, SEQ, far_back)
-    opposite_in = lax.ppermute(opposite[0], SEQ, far_out)
-    other_in = swap(grad_other, CORE)
-    far_in, opposite_in, other_in, contribution = lax.optimization_barrier(
-        (far_in, opposite_in, other_in, contribution)
-    )
-    grad_video = lax.dynamic_update_slice_in_dim(
-        grad_video, other_in[None], (1 - core) * half_width, 3
-    )
+    far_in, contribution = lax.optimization_barrier((far_in, everywhere(contribution, COLUMN)))
     far_in = far_in.astype(jnp.float32)
+    opposite_in = lax.ppermute(opposite[0], SEQ, far_out).astype(jnp.float32)
     zed_in = swap((zed + far_in[:2]).astype(jnp.bfloat16), HALF)
-    near_in = (far_in[2], opposite_in.astype(jnp.float32))
+    zed_in, gamma_grad = lax.optimization_barrier((zed_in, everywhere(contribution, PLANE)))
+    zed_in = zed_in.astype(jnp.float32)
+    near_in = (far_in[2], opposite_in)
     keep = own[0] + jnp.where(inner, near_in[1], near_in[0])
     leave = own[1] + jnp.where(inner, near_in[0], near_in[1])
-    zed_in, contribution, keep, leave, grad_video = lax.optimization_barrier(
-        (zed_in, everywhere(contribution, COLUMN), keep, leave, grad_video)
-    )
-    zed_in = zed_in.astype(jnp.float32)
     keep = (keep + zed_in[0]).astype(jnp.bfloat16)
     arrived = swap((leave + zed_in[1]).astype(jnp.bfloat16), CORE)
-    gamma_grad, arrived = lax.optimization_barrier((everywhere(contribution, PLANE), arrived))
     grad_audio = jnp.where(
         core == 0,
         jnp.concatenate([keep, arrived], axis=-1),
         jnp.concatenate([arrived, keep], axis=-1),
     )[None]
+    grad_video = lax.dynamic_update_slice_in_dim(
+        grad_video, swap(grad_other, CORE)[None], (1 - core) * half_width, 3
+    )
+
     gamma_grad = gamma_grad / (tokens * count * head_dim)
     return (grad_video, grad_audio, gamma_grad)
 

time: 133 us -> 116 us (0.87)
  blocking collectives: 0 us -> 24.9 us
  waiting for transfers between devices: 28.3 us -> 6.89 us
  starting transfers between devices: 77.1 us -> 57 us
  local copies, waits for them, and re-layouts: 8.5 us -> 6.28 us
    all_to_all x0 -> x1, blocking collectives: none -> 23.1 us  [everywhere(): return jnp.sum(lax.all_to_all(copies, axes, 0, 0), axis=0)]
    all_to_all x2 -> x1, starting transfers between devices: 24.3 us -> 8.52 us  [everywhere(): return jnp.sum(lax.all_to_all(copies, axes, 0, 0), axis=0)]
    all_to_all x2 -> x1, waiting for transfers between devices: 16.5 us -> 5.9 us  [everywhere(): return jnp.sum(lax.all_to_all(copies, axes, 0, 0), axis=0)]
    ppermute x1, waiting for transfers between devices: 3.64 us -> 0.01 us  [body(): opposite = lax.ppermute(jnp.where(inner, kept, got), SEQ, far_back)]
    ppermute x1, waiting for transfers between devices: 3.23 us -> 0.01 us  [body(): far_in = lax.ppermute(far, SEQ, far_back)]
    ppermute x8, waiting for transfers between devices: 3.13 us -> 0.26 us  [swap(): return lax.ppermute(x, axis, [(0, 1), (1, 0)])]
    ppermute x8, starting transfers between devices: 37.3 us -> 34.6 us  [swap(): return lax.ppermute(x, axis, [(0, 1), (1, 0)])]
    convert_element_type x2 -> x0, other arithmetic: 2.66 us -> none  [the longest x1 1.37 us: body(): jnp.stack([received[4, 0, 0], received[4, rows // 2, 0]]).astype(jnp.int32)]
  transfers between devices with their start and end apart: 16 -> 15, of which waited for: 6 -> 4; matrix products, arithmetic and copies ran while one was open for 5% -> 7% of each run, Pallas kernels for 2% -> 3%
where the time goes in v5:
time: 116 us; the launch traced here: 115 us
  starting transfers between devices  57 us (49%)
  blocking collectives  24.9 us (21%)
  Pallas kernels  10.9 us (9%)
  waiting for transfers between devices  6.89 us (6%)
  local copies, waits for them, and re-layouts  6.28 us (5%)
  other arithmetic  6.1 us (5%)
  between operations  2.93 us (3%)
    ppermute x8, starting transfers between devices, swap(): return lax.ppermute(x, axis, [(0, 1), (1, 0)])  34.6 us
    all_to_all x1, blocking collectives, everywhere(): return jnp.sum(lax.all_to_all(copies, axes, 0, 0), axis=0)  23.1 us
    all_to_all x1, starting transfers between devices, everywhere(): return jnp.sum(lax.all_to_all(copies, axes, 0, 0), axis=0)  8.52 us
    pallas_call x1, Pallas kernels, student_call(): pl.pallas_call(functools.partial(student_kernel, head_dim), grid_spec=plt...  7.26 us
    all_to_all x1, waiting for transfers between devices, everywhere(): return jnp.sum(lax.all_to_all(copies, axes, 0, 0), axis=0)  5.9 us
    ppermute x2, starting transfers between devices, body(): fars = [lax.ppermute(zed, SEQ, far_out) for zed in zeds]  4.64 us
    pallas_call x1, Pallas kernels, teacher_call(): pl.pallas_call(functools.partial(teacher_kernel, head_dim), grid_spec=plt...  3.67 us
    ppermute x1, starting transfers between devices, body(): opposite_in = lax.ppermute(opposite[0], SEQ, far_out).astype(jnp.float32)  3.56 us
  transfers between devices with their start and end apart: 15, of which 4 were waited for; matrix products, arithmetic and copies ran while one was open for 7% of the time, Pallas kernels for 3%

profile of v5, /device:TPU:1, one launch (start us, length us, event | category | flops | bytes accessed | tf_op | source)
XLA Modules:
  0.0 115.0 jit_solution(1797554448435883968)
XLA Ops:
  0.6 1.0 fusion.7
  1.6 8.8 %collective-permute-start = (bf16[4,32,768]{2,1,0:T(8,128)(2,1)S(1)}, bf16[4,32,768]{2,1,0:T(8,128)(2,1)S(1)}, u32[]{:S(2)}, u32[]{:S(2)}) collective-permute-start(bf16[4,32,768]{2,1,0:T(8,128)(2,1)S(1)} %fusion.7), channel_id=1, source_target_pairs={{0,4},{4,0},{1,5},{5,1},{2,6},{6,2},{3,7},{7,3},{8,12},{12,8},{9,1... | collective-permute-start | bytes 589832 | tf_op jit(solution)/shard_map/ppermute | solution.py:224
  12.4 0.8 select_reduce_fusion
  13.2 0.1 dynamic_slice.21
  13.3 0.6 stack.57
  13.9 0.1 pad_maximum_fusion.2.scal
  14.0 0.0 collective-permute-done
  14.0 1.7 %broadcast_select_fusion = (bf16[4,32,768]{2,1,0:T(8,128)(2,1)}, bf16[4,32,768]{2,1,0:T(8,128)(2,1)S(1)}) fusion(bf16[4,32,768]{2,1,0:T(8,128)(2,1)S(1)} %collective-permute-done, pred[]{:T(512)S(6)} %eq.31, s32[]{:T(128)S(6)} %select_n.81, bf16[2,32,1536]{2,1,0:T(8,128)(2,1)} %bitcast.63, bf16[2,32,1536]{2,1,0:T(8,128)(2,1)} %bitcast.61), kind=kLoop, calls=%fused_computation.25 | loop fusion | flops 491520 | bytes 983045 | tf_op jit(solution)/shard_map/jit(_where)/select_n | solution.py:280
  15.7 0.0 copy-start.1
  15.7 5.4 %collective-permute-start.1 = (bf16[2,2,32,768]{3,2,1,0:T(8,128)(2,1)S(1)}, bf16[2,2,32,768]{3,2,1,0:T(8,128)(2,1)S(1)}, u32[]{:S(2)}, u32[]{:S(2)}) collective-permute-start(bf16[2,2,32,768]{3,2,1,0:T(8,128)(2,1)S(1)} %pad_maximum_fusion.refs_0_), channel_id=1, source_target_pairs={{0,8},{8,0},{1,9},{9,1},{2,10},{10,2},{3,11},{11,3},{4,12},{12,4},... | collective-permute-start | bytes 589832 | tf_op jit(solution)/shard_map/ppermute | solution.py:224
  21.1 0.7 broadcast_select_fusion.1
  21.8 3.1 %collective-permute-start.5 = (bf16[4,32,768]{2,1,0:T(8,128)(2,1)}, bf16[4,32,768]{2,1,0:T(8,128)(2,1)S(1)}, u32[]{:S(2)}, u32[]{:S(2)}) collective-permute-start(bf16[4,32,768]{2,1,0:T(8,128)(2,1)} %broadcast_select_fusion.1), channel_id=1, source_target_pairs={{0,16},{4,20},{16,32},{20,36},{24,8},{28,12},{32,48},{36,52},{40,2... | collective-permute-start | bytes 589832 | tf_op jit(solution)/shard_map/ppermute | solution.py:279
  25.0 1.3 %collective-permute-start.6 = (bf16[4,32,768]{2,1,0:T(8,128)(2,1)}, bf16[4,32,768]{2,1,0:T(8,128)(2,1)S(1)}, u32[]{:S(2)}, u32[]{:S(2)}) collective-permute-start(bf16[4,32,768]{2,1,0:T(8,128)(2,1)} %get-tuple-element.48), channel_id=1, source_target_pairs={{16,0},{20,4},{32,16},{36,20},{8,24},{12,28},{48,32},{52,36},{24,4... | collective-permute-start | bytes 589832 | tf_op jit(solution)/shard_map/ppermute | solution.py:280
  26.3 0.0 copy-start.4
  26.3 4.8 %collective-permute-start.3 = (bf16[2,2,32,768]{3,2,1,0:T(8,128)(2,1)S(1)}, bf16[2,2,32,768]{3,2,1,0:T(8,128)(2,1)S(1)}, u32[]{:S(2)}, u32[]{:S(2)}) collective-permute-start(bf16[2,2,32,768]{3,2,1,0:T(8,128)(2,1)S(1)} %pad_maximum_fusion.1.refs_0_), channel_id=1, source_target_pairs={{0,8},{8,0},{1,9},{9,1},{2,10},{10,2},{3,11},{11,3},{4,12},{12,4},... | collective-permute-start | bytes 589832 | tf_op jit(solution)/shard_map/ppermute | solution.py:224
  31.1 0.0 collective-permute-done.1.refs_1_
  31.1 0.0 copy-done
  31.1 0.9 dynamic-slice_bitcast_fusion
  32.0 3.0 %collective-permute-start.7 = (bf16[3,128,768]{2,1,0:T(8,128)(2,1)}, bf16[3,128,768]{2,1,0:T(8,128)(2,1)}, u32[]{:S(2)}, u32[]{:S(2)}) collective-permute-start(bf16[3,128,768]{2,1,0:T(8,128)(2,1)} %dynamic-slice_bitcast_fusion), channel_id=1, source_target_pairs={{0,4},{4,0},{1,5},{5,1},{2,6},{6,2},{3,7},{7,3},{8,12},{12,8},{9,1... | collective-permute-start | bytes 1769480 | tf_op jit(solution)/shard_map/ppermute | solution.py:224
  35.0 0.0 copy-done.1
  35.0 0.9 dynamic-slice_bitcast_fusion.1
  35.9 0.0 copy-done.4
  35.9 1.8 %all-gather = s32[2,1,2]{2,1,0:T(1,128)S(1)} all-gather(s32[1,1,2]{2,1,0:T(1,128)S(1)} %copy-done.4), channel_id=2, replica_groups=mesh['seq_0'=8,'seq_1'=4,'seq_2'=2,'seq_3'=2,'dp'=4] {'seq_3'}, dimensions={0}, use_global_device_ids=true | all-gather | bytes 24 | tf_op jit(solution)/shard_map/all_gather | solution.py:284
  37.7 2.1 %collective-permute-start.2 = (bf16[3,128,768]{2,1,0:T(8,128)(2,1)}, bf16[3,128,768]{2,1,0:T(8,128)(2,1)}, u32[]{:S(2)}, u32[]{:S(2)}) collective-permute-start(bf16[3,128,768]{2,1,0:T(8,128)(2,1)} %dynamic-slice_bitcast_fusion.1), channel_id=1, source_target_pairs={{0,4},{4,0},{1,5},{5,1},{2,6},{6,2},{3,7},{7,3},{8,12},{12,8},{9,1... | collective-permute-start | bytes 1769480 | tf_op jit(solution)/shard_map/ppermute | solution.py:224
  39.8 0.2 slice_reduce_fusion
  40.0 0.0 collective-permute-done.5.refs_3_
  40.0 2.3 %collective-permute-start.8 = (bf16[2,2,32,768]{3,2,1,0:T(8,128)(2,1)S(1)}, bf16[2,2,32,768]{3,2,1,0:T(8,128)(2,1)}, u32[]{:S(2)}, u32[]{:S(2)}) collective-permute-start(bf16[2,2,32,768]{3,2,1,0:T(8,128)(2,1)S(1)} %collective-permute-done.1.refs_1_), channel_id=1, source_target_pairs={{0,16},{4,20},{16,32},{20,36},{24,8},{28,12},{32,48},{36,52},{40,2... | collective-permute-start | bytes 589832 | tf_op jit(solution)/shard_map/ppermute | solution.py:281
  42.4 0.0 collective-permute-done.3.refs_1_
  42.4 2.3 %collective-permute-start.4 = (bf16[2,2,32,768]{3,2,1,0:T(8,128)(2,1)S(1)}, bf16[2,2,32,768]{3,2,1,0:T(8,128)(2,1)}, u32[]{:S(2)}, u32[]{:S(2)}) collective-permute-start(bf16[2,2,32,768]{3,2,1,0:T(8,128)(2,1)S(1)} %collective-permute-done.3.refs_1_), channel_id=1, source_target_pairs={{0,16},{4,20},{16,32},{20,36},{24,8},{28,12},{32,48},{36,52},{40,2... | collective-permute-start | bytes 589832 | tf_op jit(solution)/shard_map/ppermute | solution.py:281
  44.7 0.7 and_select_fusion
  45.4 0.1 select_n.85.bias
  45.4 0.0 collective-permute-done.6.refs_4_
  45.4 0.2 collective-permute-done.8.refs_2_
  45.6 0.0 collective-permute-done.7.other
  45.6 3.7 %teacher.1.refs_5_ = f32[6,128,256]{2,1,0:T(8,128)S(1)} custom-call(s32[1]{0:T(128)} %bitcast.core, f32[16]{0:T(128)S(1)} %select_n.85.bias, f32[8]{0:T(128)S(1)} %pad_maximum_fusion.2.scal, bf16[1,3,128,1536]{3,2,1,0:T(8,128)(2,1)S(1)} %copy-done, bf16[3,128,768]{2,1,0:T(8,128)(2,1)} %collective-permute-done.7.other, ...), custom_call_target="tpu_custom_call" | custom-call | flops 600000000 | bytes 4000000 | tf_op jit(solution)/shard_map/teacher/pallas_call | solution.py:164
  49.3 0.5 collective-permute-done.4.refs_2_
  49.8 0.0 collective-permute-done.2.other
  49.8 7.3 %student.1 = (bf16[1,3,128,1536]{3,2,1,0:T(8,128)(2,1)}, bf16[3,128,768]{2,1,0:T(8,128)(2,1)S(1)}, f32[2,2,32,768]{3,2,1,0:T(8,128)S(1)}, f32[2,2,32,768]{3,2,1,...) custom-call(s32[1]{0:T(128)} %bitcast.core, ...), custom_call_target="tpu_custom_call" | custom-call | flops 900000000 | bytes 8000000 | tf_op jit(solution)/shard_map/student/pallas_call | solution.py:205
  57.1 0.8 copy-done.2
  57.9 1.3 %collective-permute-start.11 = (bf16[3,2,32,768]{3,2,1,0:T(8,128)(2,1)}, bf16[3,2,32,768]{3,2,1,0:T(8,128)(2,1)S(1)}, u32[]{:S(2)}, u32[]{:S(2)}) collective-permute-start(bf16[3,2,32,768]{3,2,1,0:T(8,128)(2,1)} %get-tuple-element.30), channel_id=1, source_target_pairs={{16,0},{20,4},{32,16},{36,20},{8,24},{12,28},{48,32},{52,36},{24,4... | collective-permute-start | bytes 884744 | tf_op jit(solution)/shard_map/ppermute | solution.py:329
  59.2 0.1 reduce_sum.37
  59.3 0.2 dynamic_update_slice.18
  59.6 0.1 broadcast_select_fusion.2
  59.7 23.1 %all_to_all.10 = f32[16,8,12]{2,1,0:T(8,128)S(1)} all-to-all(f32[16,8,12]{2,1,0:T(8,128)S(1)} %broadcast_in_dim.60), channel_id=1, replica_groups=mesh['seq_0'=8,'seq_1'=4,'seq_2'=2,'seq_3'=2,'dp'=4] {'seq_2','seq_3','dp'}, dimensions={0} | all-to-all | bytes 12288 | tf_op jit(solution)/shard_map/all_to_all | solution.py:230
  82.8 0.1 copy.22
  82.9 0.0 collective-permute-done.11
  83.0 2.5 %collective-permute-start.12 = (bf16[2,2,32,768]{3,2,1,0:T(8,128)(2,1)S(1)}, bf16[2,2,32,768]{3,2,1,0:T(8,128)(2,1)S(1)}, u32[]{:S(2)}, u32[]{:S(2)}) collective-permute-start(bf16[2,2,32,768]{3,2,1,0:T(8,128)(2,1)S(1)} %fusion), channel_id=1, source_target_pairs={{0,8},{8,0},{1,9},{9,1},{2,10},{10,2},{3,11},{11,3},{4,12},{12,4},... | collective-permute-start | bytes 589832 | tf_op jit(solution)/shard_map/ppermute | solution.py:224
  85.5 3.6 %collective-permute-start.10 = (bf16[2,32,768]{2,1,0:T(8,128)(2,1)S(1)}, bf16[2,32,768]{2,1,0:T(8,128)(2,1)S(1)}, u32[]{:S(2)}, u32[]{:S(2)}) collective-permute-start(bf16[2,32,768]{2,1,0:T(8,128)(2,1)S(1)} %bitcast.59), channel_id=1, source_target_pairs={{0,16},{4,20},{16,32},{20,36},{24,8},{28,12},{32,48},{36,52},{40,2... | collective-permute-start | bytes 294920 | tf_op jit(solution)/shard_map/ppermute | solution.py:332
  89.0 0.1 copy.19
  89.1 0.7 broadcast_in_dim.61
  89.8 8.5 %all-to-all-start.1 = ((f32[32,8,12]{2,1,0:T(8,128)}), f32[32,8,12]{2,1,0:T(8,128)S(1)}, u32[]{:S(2)}, u32[]{:S(2)}) async-start(f32[32,8,12]{2,1,0:T(8,128)} %broadcast_in_dim.61), calls=%async_computation.1 | async-start | bytes 262144 | tf_op jit(solution)/shard_map/all_to_all | solution.py:230
  98.3 0.0 copy-done.3
  98.3 3.4 %collective-permute-start.9 = (bf16[3,128,768]{2,1,0:T(8,128)(2,1)S(1)}, bf16[3,128,768]{2,1,0:T(8,128)(2,1)S(1)}, u32[]{:S(2)}, u32[]{:S(2)}) collective-permute-start(bf16[3,128,768]{2,1,0:T(8,128)(2,1)S(1)} %copy-done.3), channel_id=1, source_target_pairs={{0,4},{4,0},{1,5},{5,1},{2,6},{6,2},{3,7},{7,3},{8,12},{12,8},{9,1... | collective-permute-start | bytes 1769480 | tf_op jit(solution)/shard_map/ppermute | solution.py:224
  101.8 5.9 %all-to-all-done.1 = f32[32,8,12]{2,1,0:T(8,128)S(1)} async-done(((f32[32,8,12]{2,1,0:T(8,128)}), f32[32,8,12]{2,1,0:T(8,128)S(1)}, u32[]{:S(2)}, u32[]{:S(2)}) %all-to-all-start.1) | async-done | bytes 12320 | tf_op jit(solution)/shard_map/all_to_all | solution.py:230
  107.7 0.1 copy.23
  107.8 0.0 collective-permute-done.12
  107.8 0.0 collective-permute-done.10
  107.8 0.1 fusion.9
  107.9 4.6 %collective-permute-start.13 = (bf16[2,32,768]{2,1,0:T(8,128)(2,1)S(1)}, bf16[2,32,768]{2,1,0:T(8,128)(2,1)S(1)}, u32[]{:S(2)}, u32[]{:S(2)}) collective-permute-start(bf16[2,32,768]{2,1,0:T(8,128)(2,1)S(1)} %get-tuple-element.51), channel_id=1, source_target_pairs={{0,4},{4,0},{1,5},{5,1},{2,6},{6,2},{3,7},{7,3},{8,12},{12,8},{9,1... | collective-permute-start | bytes 294920 | tf_op jit(solution)/shard_map/ppermute | solution.py:224
  112.5 0.7 copy.21
  113.2 0.2 collective-permute-done.13
  113.5 0.7 maximum_select_fusion
  114.2 0.0 collective-permute-done.9
  114.2 0.9 bitcast_dynamic-update-slice_fusion
  (18 shorter events, 0.3 us)
Async XLA Ops:
  1.6 12.4 %collective-permute-start = (bf16[4,32,768]{2,1,0:T(8,128)(2,1)S(1)}, bf16[4,32,768]{2,1,0:T(8,128)(2,1)S(1)}, u32[]{:S(2)}, u32[]{:S(2)}) collective-permute-start(bf16[4,32,768]{2,1,0:T(8,128)(2,1)S(1)} %fusion.7), channel_id=1, source_target_pairs={{0,4},{4,0},{1,5},{5,1},{2,6},{6,2},{3,7},{7,3},{8,12},{12,8},{9,1... | collective-permute-start | bytes 589832 | tf_op jit(solution)/shard_map/ppermute | solution.py:224
  15.7 15.5 %copy-start = (bf16[1,3,128,1536]{3,2,1,0:T(8,128)(2,1)S(1)}, bf16[1,3,128,1536]{3,2,1,0:T(8,128)(2,1)}, u32[]{:S(2)}) copy-start(bf16[1,3,128,1536]{3,2,1,0:T(8,128)(2,1)} %mine) | copy-start | bytes 3538948
  15.7 19.3 %copy-start.1 = (bf16[1,3,128,1536]{3,2,1,0:T(8,128)(2,1)S(1)}, bf16[1,3,128,1536]{3,2,1,0:T(8,128)(2,1)}, u32[]{:S(2)}) copy-start(bf16[1,3,128,1536]{3,2,1,0:T(8,128)(2,1)} %mine.1) | copy-start | bytes 3538948
  15.7 15.4 %collective-permute-start.1 = (bf16[2,2,32,768]{3,2,1,0:T(8,128)(2,1)S(1)}, bf16[2,2,32,768]{3,2,1,0:T(8,128)(2,1)S(1)}, u32[]{:S(2)}, u32[]{:S(2)}) collective-permute-start(bf16[2,2,32,768]{3,2,1,0:T(8,128)(2,1)S(1)} %pad_maximum_fusion.refs_0_), channel_id=1, source_target_pairs={{0,8},{8,0},{1,9},{9,1},{2,10},{10,2},{3,11},{11,3},{4,12},{12,4},... | collective-permute-start | bytes 589832 | tf_op jit(solution)/shard_map/ppermute | solution.py:224
  21.8 18.2 %collective-permute-start.5 = (bf16[4,32,768]{2,1,0:T(8,128)(2,1)}, bf16[4,32,768]{2,1,0:T(8,128)(2,1)S(1)}, u32[]{:S(2)}, u32[]{:S(2)}) collective-permute-start(bf16[4,32,768]{2,1,0:T(8,128)(2,1)} %broadcast_select_fusion.1), channel_id=1, source_target_pairs={{0,16},{4,20},{16,32},{20,36},{24,8},{28,12},{32,48},{36,52},{40,2... | collective-permute-start | bytes 589832 | tf_op jit(solution)/shard_map/ppermute | solution.py:279
  25.0 20.5 %collective-permute-start.6 = (bf16[4,32,768]{2,1,0:T(8,128)(2,1)}, bf16[4,32,768]{2,1,0:T(8,128)(2,1)S(1)}, u32[]{:S(2)}, u32[]{:S(2)}) collective-permute-start(bf16[4,32,768]{2,1,0:T(8,128)(2,1)} %get-tuple-element.48), channel_id=1, source_target_pairs={{16,0},{20,4},{32,16},{36,20},{8,24},{12,28},{48,32},{52,36},{24,4... | collective-permute-start | bytes 589832 | tf_op jit(solution)/shard_map/ppermute | solution.py:280
  26.3 9.6 %copy-start.4 = (s32[1,1,2]{2,1,0:T(1,128)S(1)}, s32[1,1,2]{2,1,0:T(1,128)}, u32[]{:S(2)}) copy-start(s32[1,1,2]{2,1,0:T(1,128)} %param.13) | copy-start | bytes 28
  26.3 16.1 %collective-permute-start.3 = (bf16[2,2,32,768]{3,2,1,0:T(8,128)(2,1)S(1)}, bf16[2,2,32,768]{3,2,1,0:T(8,128)(2,1)S(1)}, u32[]{:S(2)}, u32[]{:S(2)}) collective-permute-start(bf16[2,2,32,768]{3,2,1,0:T(8,128)(2,1)S(1)} %pad_maximum_fusion.1.refs_0_), channel_id=1, source_target_pairs={{0,8},{8,0},{1,9},{9,1},{2,10},{10,2},{3,11},{11,3},{4,12},{12,4},... | collective-permute-start | bytes 589832 | tf_op jit(solution)/shard_map/ppermute | solution.py:224
  32.0 13.6 %collective-permute-start.7 = (bf16[3,128,768]{2,1,0:T(8,128)(2,1)}, bf16[3,128,768]{2,1,0:T(8,128)(2,1)}, u32[]{:S(2)}, u32[]{:S(2)}) collective-permute-start(bf16[3,128,768]{2,1,0:T(8,128)(2,1)} %dynamic-slice_bitcast_fusion), channel_id=1, source_target_pairs={{0,4},{4,0},{1,5},{5,1},{2,6},{6,2},{3,7},{7,3},{8,12},{12,8},{9,1... | collective-permute-start | bytes 1769480 | tf_op jit(solution)/shard_map/ppermute | solution.py:224
  37.7 12.1 %collective-permute-start.2 = (bf16[3,128,768]{2,1,0:T(8,128)(2,1)}, bf16[3,128,768]{2,1,0:T(8,128)(2,1)}, u32[]{:S(2)}, u32[]{:S(2)}) collective-permute-start(bf16[3,128,768]{2,1,0:T(8,128)(2,1)} %dynamic-slice_bitcast_fusion.1), channel_id=1, source_target_pairs={{0,4},{4,0},{1,5},{5,1},{2,6},{6,2},{3,7},{7,3},{8,12},{12,8},{9,1... | collective-permute-start | bytes 1769480 | tf_op jit(solution)/shard_map/ppermute | solution.py:224
  40.0 5.6 %collective-permute-start.8 = (bf16[2,2,32,768]{3,2,1,0:T(8,128)(2,1)S(1)}, bf16[2,2,32,768]{3,2,1,0:T(8,128)(2,1)}, u32[]{:S(2)}, u32[]{:S(2)}) collective-permute-start(bf16[2,2,32,768]{3,2,1,0:T(8,128)(2,1)S(1)} %collective-permute-done.1.refs_1_), channel_id=1, source_target_pairs={{0,16},{4,20},{16,32},{20,36},{24,8},{28,12},{32,48},{36,52},{40,2... | collective-permute-start | bytes 589832 | tf_op jit(solution)/shard_map/ppermute | solution.py:281
  42.4 7.5 %collective-permute-start.4 = (bf16[2,2,32,768]{3,2,1,0:T(8,128)(2,1)S(1)}, bf16[2,2,32,768]{3,2,1,0:T(8,128)(2,1)}, u32[]{:S(2)}, u32[]{:S(2)}) collective-permute-start(bf16[2,2,32,768]{3,2,1,0:T(8,128)(2,1)S(1)} %collective-permute-done.3.refs_1_), channel_id=1, source_target_pairs={{0,16},{4,20},{16,32},{20,36},{24,8},{28,12},{32,48},{36,52},{40,2... | collective-permute-start | bytes 589832 | tf_op jit(solution)/shard_map/ppermute | solution.py:281
  57.1 0.8 copy-start.2
  57.9 25.0 %collective-permute-start.11 = (bf16[3,2,32,768]{3,2,1,0:T(8,128)(2,1)}, bf16[3,2,32,768]{3,2,1,0:T(8,128)(2,1)S(1)}, u32[]{:S(2)}, u32[]{:S(2)}) collective-permute-start(bf16[3,2,32,768]{3,2,1,0:T(8,128)(2,1)} %get-tuple-element.30), channel_id=1, source_target_pairs={{16,0},{20,4},{32,16},{36,20},{8,24},{12,28},{48,32},{52,36},{24,4... | collective-permute-start | bytes 884744 | tf_op jit(solution)/shard_map/ppermute | solution.py:329
  82.8 15.5 %copy-start.3 = (bf16[3,128,768]{2,1,0:T(8,128)(2,1)S(1)}, bf16[3,128,768]{2,1,0:T(8,128)(2,1)}, u32[]{:S(2)}) copy-start(bf16[3,128,768]{2,1,0:T(8,128)(2,1)} %copy-done.2) | copy-start | bytes 1769476
  83.0 24.8 %collective-permute-start.12 = (bf16[2,2,32,768]{3,2,1,0:T(8,128)(2,1)S(1)}, bf16[2,2,32,768]{3,2,1,0:T(8,128)(2,1)S(1)}, u32[]{:S(2)}, u32[]{:S(2)}) collective-permute-start(bf16[2,2,32,768]{3,2,1,0:T(8,128)(2,1)S(1)} %fusion), channel_id=1, source_target_pairs={{0,8},{8,0},{1,9},{9,1},{2,10},{10,2},{3,11},{11,3},{4,12},{12,4},... | collective-permute-start | bytes 589832 | tf_op jit(solution)/shard_map/ppermute | solution.py:224
  85.5 22.4 %collective-permute-start.10 = (bf16[2,32,768]{2,1,0:T(8,128)(2,1)S(1)}, bf16[2,32,768]{2,1,0:T(8,128)(2,1)S(1)}, u32[]{:S(2)}, u32[]{:S(2)}) collective-permute-start(bf16[2,32,768]{2,1,0:T(8,128)(2,1)S(1)} %bitcast.59), channel_id=1, source_target_pairs={{0,16},{4,20},{16,32},{20,36},{24,8},{28,12},{32,48},{36,52},{40,2... | collective-permute-start | bytes 294920 | tf_op jit(solution)/shard_map/ppermute | solution.py:332
  89.8 17.9 %all-to-all-start.1 = ((f32[32,8,12]{2,1,0:T(8,128)}), f32[32,8,12]{2,1,0:T(8,128)S(1)}, u32[]{:S(2)}, u32[]{:S(2)}) async-start(f32[32,8,12]{2,1,0:T(8,128)} %broadcast_in_dim.61), calls=%async_computation.1 | async-start | bytes 262144 | tf_op jit(solution)/shard_map/all_to_all | solution.py:230
  98.3 15.9 %collective-permute-start.9 = (bf16[3,128,768]{2,1,0:T(8,128)(2,1)S(1)}, bf16[3,128,768]{2,1,0:T(8,128)(2,1)S(1)}, u32[]{:S(2)}, u32[]{:S(2)}) collective-permute-start(bf16[3,128,768]{2,1,0:T(8,128)(2,1)S(1)} %copy-done.3), channel_id=1, source_target_pairs={{0,4},{4,0},{1,5},{5,1},{2,6},{6,2},{3,7},{7,3},{8,12},{12,8},{9,1... | collective-permute-start | bytes 1769480 | tf_op jit(solution)/shard_map/ppermute | solution.py:224
  107.9 5.5 %collective-permute-start.13 = (bf16[2,32,768]{2,1,0:T(8,128)(2,1)S(1)}, bf16[2,32,768]{2,1,0:T(8,128)(2,1)S(1)}, u32[]{:S(2)}, u32[]{:S(2)}) collective-permute-start(bf16[2,32,768]{2,1,0:T(8,128)(2,1)S(1)} %get-tuple-element.51), channel_id=1, source_target_pairs={{0,4},{4,0},{1,5},{5,1},{2,6},{6,2},{3,7},{7,3},{8,12},{12,8},{9,1... | collective-permute-start | bytes 294920 | tf_op jit(solution)/shard_map/ppermute | solution.py:224

commit v6 on v5

--- a/solution.py
+++ b/solution.py
@@ -271,13 +271,14 @@
     inner = core == half
     pairs = [jnp.stack([kept[i : i + 2], got[i : i + 2]]) for i in (0, 2)]
     zeds = [swap(pair, HALF) for pair in pairs]
-    zeds[0], teacher_video, student_video, alignment, guidance_index, step_index = (
-        lax.optimization_barrier(
-            (zeds[0], teacher_video, student_video, alignment, guidance_index, step_index)
-        )
+    zeds[0], guidance_index, step_index = lax.optimization_barrier(
+        (zeds[0], guidance_index, step_index)
     )
     same = lax.ppermute(jnp.where(inner, got, kept), SEQ, far_out)
     opposite = lax.ppermute(jnp.where(inner, kept, got), SEQ, far_back)
+    same, teacher_video, student_video, alignment = lax.optimization_barrier(
+        (same, teacher_video, student_video, alignment)
+    )
     fars = [lax.ppermute(zed, SEQ, far_out) for zed in zeds]
     teach_other = swap(part(teacher_video[0], 1 - core), CORE)
     pupil_other = swap(part(student_video[0], 1 - core), CORE)

time: 116 us -> 115 us (level)
  starting transfers between devices: 57 us -> 59.5 us
  blocking collectives: 24.9 us -> 23.6 us
  other arithmetic: 6.1 us -> 4.83 us
    all_to_all x1, starting transfers between devices: 8.52 us -> 10.6 us  [everywhere(): return jnp.sum(lax.all_to_all(copies, axes, 0, 0), axis=0)]
    all_to_all x1, blocking collectives: 23.1 us -> 21.9 us  [everywhere(): return jnp.sum(lax.all_to_all(copies, axes, 0, 0), axis=0)]
  transfers between devices with their start and end apart: 15 -> 15, of which waited for: 4 -> 2; matrix products, arithmetic and copies ran while one was open for 7% -> 5% of each run, Pallas kernels for 3% -> 3%
where the time goes in v6:
time: 115 us; the launch traced here: 114 us
  starting transfers between devices  59.5 us (52%)
  blocking collectives  23.6 us (21%)
  Pallas kernels  11 us (10%)
  waiting for transfers between devices  6.52 us (6%)
  local copies, waits for them, and re-layouts  5.73 us (5%)
  other arithmetic  4.83 us (4%)
  between operations  2.99 us (3%)
    ppermute x8, starting transfers between devices, swap(): return lax.ppermute(x, axis, [(0, 1), (1, 0)])  34.3 us
    all_to_all x1, blocking collectives, everywhere(): return jnp.sum(lax.all_to_all(copies, axes, 0, 0), axis=0)  21.9 us
    all_to_all x1, starting transfers between devices, everywhere(): return jnp.sum(lax.all_to_all(copies, axes, 0, 0), axis=0)  10.6 us
    pallas_call x1, Pallas kernels, student_call(): pl.pallas_call(functools.partial(student_kernel, head_dim), grid_spec=plt...  7.26 us
    all_to_all x1, waiting for transfers between devices, everywhere(): return jnp.sum(lax.all_to_all(copies, axes, 0, 0), axis=0)  6.24 us
    ppermute x2, starting transfers between devices, body(): fars = [lax.ppermute(zed, SEQ, far_out) for zed in zeds]  5.63 us
    pallas_call x1, Pallas kernels, teacher_call(): pl.pallas_call(functools.partial(teacher_kernel, head_dim), grid_spec=plt...  3.69 us
    ppermute x1, starting transfers between devices, body(): opposite_in = lax.ppermute(opposite[0], SEQ, far_out).astype(jnp.float32)  3.35 us
  transfers between devices with their start and end apart: 15, of which 2 were waited for; matrix products, arithmetic and copies ran while one was open for 5% of the time, Pallas kernels for 3%

profile of v6, /device:TPU:1, one launch (start us, length us, event | category | flops | bytes accessed | tf_op | source)
XLA Modules:
  0.0 114.2 jit_solution(6165399630685843072)
XLA Ops:
  0.6 1.0 fusion.8
  1.6 8.8 %collective-permute-start = (bf16[4,32,768]{2,1,0:T(8,128)(2,1)S(1)}, bf16[4,32,768]{2,1,0:T(8,128)(2,1)S(1)}, u32[]{:S(2)}, u32[]{:S(2)}) collective-permute-start(bf16[4,32,768]{2,1,0:T(8,128)(2,1)S(1)} %fusion.8), channel_id=1, source_target_pairs={{0,4},{4,0},{1,5},{5,1},{2,6},{6,2},{3,7},{7,3},{8,12},{12,8},{9,1... | collective-permute-start | bytes 589832 | tf_op jit(solution)/shard_map/ppermute | solution.py:224
  12.4 0.0 copy-start.4
  12.4 0.8 select_reduce_fusion
  13.2 0.1 dynamic_slice.21
  13.3 0.1 stack.57
  13.4 0.0 collective-permute-done
  13.4 0.0 copy-done.4
  13.4 1.7 %broadcast_select_fusion = (bf16[4,32,768]{2,1,0:T(8,128)(2,1)}, bf16[4,32,768]{2,1,0:T(8,128)(2,1)S(1)}) fusion(bf16[4,32,768]{2,1,0:T(8,128)(2,1)S(1)} %collective-permute-done, pred[]{:T(512)S(6)} %eq.27, s32[]{:T(128)S(6)} %select_n.83, bf16[2,32,1536]{2,1,0:T(8,128)(2,1)} %bitcast.63, bf16[2,32,1536]{2,1,0:T(8,128)(2,1)} %bitcast.61), kind=kLoop, calls=%fused_computation.25 | loop fusion | flops 491520 | bytes 983045 | tf_op jit(solution)/shard_map/jit(_where)/select_n | solution.py:278
  15.1 0.0 copy-start.6
  15.1 0.0 copy-start.1
  15.2 5.4 %collective-permute-start.2 = (bf16[2,2,32,768]{3,2,1,0:T(8,128)(2,1)S(1)}, bf16[2,2,32,768]{3,2,1,0:T(8,128)(2,1)S(1)}, u32[]{:S(2)}, u32[]{:S(2)}) collective-permute-start(bf16[2,2,32,768]{3,2,1,0:T(8,128)(2,1)S(1)} %pad_maximum_fusion.refs_0_), channel_id=1, source_target_pairs={{0,8},{8,0},{1,9},{9,1},{2,10},{10,2},{3,11},{11,3},{4,12},{12,4},... | collective-permute-start | bytes 589832 | tf_op jit(solution)/shard_map/ppermute | solution.py:224
  20.6 3.1 %collective-permute-start.1 = (bf16[4,32,768]{2,1,0:T(8,128)(2,1)S(1)}, bf16[4,32,768]{2,1,0:T(8,128)(2,1)S(1)}, u32[]{:S(2)}, u32[]{:S(2)}) collective-permute-start(bf16[4,32,768]{2,1,0:T(8,128)(2,1)S(1)} %broadcast_select_fusion.1), channel_id=1, source_target_pairs={{0,16},{4,20},{16,32},{20,36},{24,8},{28,12},{32,48},{36,52},{40,2... | collective-permute-start | bytes 589832 | tf_op jit(solution)/shard_map/ppermute | solution.py:277
  23.7 0.1 pad_maximum_fusion.2.scal
  23.8 1.3 %collective-permute-start.6 = (bf16[4,32,768]{2,1,0:T(8,128)(2,1)}, bf16[4,32,768]{2,1,0:T(8,128)(2,1)S(1)}, u32[]{:S(2)}, u32[]{:S(2)}) collective-permute-start(bf16[4,32,768]{2,1,0:T(8,128)(2,1)} %get-tuple-element.50), channel_id=1, source_target_pairs={{16,0},{20,4},{32,16},{36,20},{8,24},{12,28},{48,32},{52,36},{24,4... | collective-permute-start | bytes 589832 | tf_op jit(solution)/shard_map/ppermute | solution.py:278
  25.1 4.8 %collective-permute-start.4 = (bf16[2,2,32,768]{3,2,1,0:T(8,128)(2,1)S(1)}, bf16[2,2,32,768]{3,2,1,0:T(8,128)(2,1)S(1)}, u32[]{:S(2)}, u32[]{:S(2)}) collective-permute-start(bf16[2,2,32,768]{3,2,1,0:T(8,128)(2,1)S(1)} %pad_maximum_fusion.1.refs_0_), channel_id=1, source_target_pairs={{0,8},{8,0},{1,9},{9,1},{2,10},{10,2},{3,11},{11,3},{4,12},{12,4},... | collective-permute-start | bytes 589832 | tf_op jit(solution)/shard_map/ppermute | solution.py:224
  29.9 0.0 collective-permute-done.2.refs_1_
  29.9 0.0 collective-permute-done.1.refs_3_
  29.9 0.0 copy-done
  30.0 0.9 dynamic-slice_bitcast_fusion
  30.8 3.0 %collective-permute-start.7 = (bf16[3,128,768]{2,1,0:T(8,128)(2,1)}, bf16[3,128,768]{2,1,0:T(8,128)(2,1)}, u32[]{:S(2)}, u32[]{:S(2)}) collective-permute-start(bf16[3,128,768]{2,1,0:T(8,128)(2,1)} %dynamic-slice_bitcast_fusion), channel_id=1, source_target_pairs={{0,4},{4,0},{1,5},{5,1},{2,6},{6,2},{3,7},{7,3},{8,12},{12,8},{9,1... | collective-permute-start | bytes 1769480 | tf_op jit(solution)/shard_map/ppermute | solution.py:224
  33.9 0.0 copy-done.6
  33.9 1.8 %all-gather = s32[2,1,2]{2,1,0:T(1,128)S(1)} all-gather(s32[1,1,2]{2,1,0:T(1,128)S(1)} %copy-done.6), channel_id=2, replica_groups=mesh['seq_0'=8,'seq_1'=4,'seq_2'=2,'seq_3'=2,'dp'=4] {'seq_3'}, dimensions={0}, use_global_device_ids=true | all-gather | bytes 24 | tf_op jit(solution)/shard_map/all_gather | solution.py:285
  35.7 2.5 %collective-permute-start.8 = (bf16[2,2,32,768]{3,2,1,0:T(8,128)(2,1)S(1)}, bf16[2,2,32,768]{3,2,1,0:T(8,128)(2,1)}, u32[]{:S(2)}, u32[]{:S(2)}) collective-permute-start(bf16[2,2,32,768]{3,2,1,0:T(8,128)(2,1)S(1)} %collective-permute-done.2.refs_1_), channel_id=1, source_target_pairs={{0,16},{4,20},{16,32},{20,36},{24,8},{28,12},{32,48},{36,52},{40,2... | collective-permute-start | bytes 589832 | tf_op jit(solution)/shard_map/ppermute | solution.py:282
  38.2 0.9 dynamic-slice_bitcast_fusion.1
  39.0 2.4 %collective-permute-start.3 = (bf16[3,128,768]{2,1,0:T(8,128)(2,1)}, bf16[3,128,768]{2,1,0:T(8,128)(2,1)}, u32[]{:S(2)}, u32[]{:S(2)}) collective-permute-start(bf16[3,128,768]{2,1,0:T(8,128)(2,1)} %dynamic-slice_bitcast_fusion.1), channel_id=1, source_target_pairs={{0,4},{4,0},{1,5},{5,1},{2,6},{6,2},{3,7},{7,3},{8,12},{12,8},{9,1... | collective-permute-start | bytes 1769480 | tf_op jit(solution)/shard_map/ppermute | solution.py:224
  41.4 0.2 slice_reduce_fusion
  41.6 0.0 collective-permute-done.4.refs_1_
  41.6 3.1 %collective-permute-start.5 = (bf16[2,2,32,768]{3,2,1,0:T(8,128)(2,1)S(1)}, bf16[2,2,32,768]{3,2,1,0:T(8,128)(2,1)}, u32[]{:S(2)}, u32[]{:S(2)}) collective-permute-start(bf16[2,2,32,768]{3,2,1,0:T(8,128)(2,1)S(1)} %collective-permute-done.4.refs_1_), channel_id=1, source_target_pairs={{0,16},{4,20},{16,32},{20,36},{24,8},{28,12},{32,48},{36,52},{40,2... | collective-permute-start | bytes 589832 | tf_op jit(solution)/shard_map/ppermute | solution.py:282
  44.8 0.1 and_select_fusion
  44.8 0.1 select_n.87.bias
  44.9 0.0 collective-permute-done.6.refs_4_
  44.9 0.0 collective-permute-done.8.refs_2_
  44.9 0.0 collective-permute-done.7.other
  44.9 3.7 %teacher.1.refs_5_ = f32[6,128,256]{2,1,0:T(8,128)S(1)} custom-call(s32[1]{0:T(128)} %bitcast.core, f32[16]{0:T(128)S(1)} %select_n.87.bias, f32[8]{0:T(128)S(1)} %pad_maximum_fusion.2.scal, bf16[1,3,128,1536]{3,2,1,0:T(8,128)(2,1)S(1)} %copy-done, bf16[3,128,768]{2,1,0:T(8,128)(2,1)} %collective-permute-done.7.other, ...), custom_call_target="tpu_custom_call" | custom-call | flops 600000000 | bytes 4000000 | tf_op jit(solution)/shard_map/teacher/pallas_call | solution.py:164
  48.6 0.0 collective-permute-done.5.refs_2_
  48.7 0.0 collective-permute-done.3.other
  48.7 7.3 %student.1 = (bf16[1,3,128,1536]{3,2,1,0:T(8,128)(2,1)}, bf16[3,128,768]{2,1,0:T(8,128)(2,1)S(1)}, f32[2,2,32,768]{3,2,1,0:T(8,128)S(1)}, f32[2,2,32,768]{3,2,1,...) custom-call(s32[1]{0:T(128)} %bitcast.core, ...), custom_call_target="tpu_custom_call" | custom-call | flops 900000000 | bytes 8000000 | tf_op jit(solution)/shard_map/student/pallas_call | solution.py:205
  55.9 0.8 copy-done.2
  56.7 1.3 %collective-permute-start.11 = (bf16[3,2,32,768]{3,2,1,0:T(8,128)(2,1)}, bf16[3,2,32,768]{3,2,1,0:T(8,128)(2,1)S(1)}, u32[]{:S(2)}, u32[]{:S(2)}) collective-permute-start(bf16[3,2,32,768]{3,2,1,0:T(8,128)(2,1)} %get-tuple-element.32), channel_id=1, source_target_pairs={{16,0},{20,4},{32,16},{36,20},{8,24},{12,28},{48,32},{52,36},{24,4... | collective-permute-start | bytes 884744 | tf_op jit(solution)/shard_map/ppermute | solution.py:330
  58.0 0.1 reduce_sum.37
  58.2 0.2 dynamic_update_slice.18
  58.4 0.0 copy-done.5
  58.4 0.1 broadcast_select_fusion.2
  58.5 21.9 %all_to_all.10 = f32[16,8,12]{2,1,0:T(8,128)S(1)} all-to-all(f32[16,8,12]{2,1,0:T(8,128)S(1)} %broadcast_in_dim.60), channel_id=1, replica_groups=mesh['seq_0'=8,'seq_1'=4,'seq_2'=2,'seq_3'=2,'dp'=4] {'seq_2','seq_3','dp'}, dimensions={0} | all-to-all | bytes 12288 | tf_op jit(solution)/shard_map/all_to_all | solution.py:230
  80.4 0.1 copy.22
  80.5 0.0 collective-permute-done.11
  80.6 2.5 %collective-permute-start.12 = (bf16[2,2,32,768]{3,2,1,0:T(8,128)(2,1)S(1)}, bf16[2,2,32,768]{3,2,1,0:T(8,128)(2,1)S(1)}, u32[]{:S(2)}, u32[]{:S(2)}) collective-permute-start(bf16[2,2,32,768]{3,2,1,0:T(8,128)(2,1)S(1)} %fusion), channel_id=1, source_target_pairs={{0,8},{8,0},{1,9},{9,1},{2,10},{10,2},{3,11},{11,3},{4,12},{12,4},... | collective-permute-start | bytes 589832 | tf_op jit(solution)/shard_map/ppermute | solution.py:224
  83.0 3.3 %collective-permute-start.10 = (bf16[2,32,768]{2,1,0:T(8,128)(2,1)S(1)}, bf16[2,32,768]{2,1,0:T(8,128)(2,1)S(1)}, u32[]{:S(2)}, u32[]{:S(2)}) collective-permute-start(bf16[2,32,768]{2,1,0:T(8,128)(2,1)S(1)} %bitcast.59), channel_id=1, source_target_pairs={{0,16},{4,20},{16,32},{20,36},{24,8},{28,12},{32,48},{36,52},{40,2... | collective-permute-start | bytes 294920 | tf_op jit(solution)/shard_map/ppermute | solution.py:333
  86.4 0.1 copy.19
  86.5 0.7 broadcast_in_dim.61
  87.1 10.6 %all-to-all-start.1 = ((f32[32,8,12]{2,1,0:T(8,128)}), f32[32,8,12]{2,1,0:T(8,128)S(1)}, u32[]{:S(2)}, u32[]{:S(2)}) async-start(f32[32,8,12]{2,1,0:T(8,128)} %broadcast_in_dim.61), calls=%async_computation.1 | async-start | bytes 262144 | tf_op jit(solution)/shard_map/all_to_all | solution.py:230
  97.7 3.1 %collective-permute-start.9 = (bf16[3,128,768]{2,1,0:T(8,128)(2,1)S(1)}, bf16[3,128,768]{2,1,0:T(8,128)(2,1)S(1)}, u32[]{:S(2)}, u32[]{:S(2)}) collective-permute-start(bf16[3,128,768]{2,1,0:T(8,128)(2,1)S(1)} %copy-done.3), channel_id=1, source_target_pairs={{0,4},{4,0},{1,5},{5,1},{2,6},{6,2},{3,7},{7,3},{8,12},{12,8},{9,1... | collective-permute-start | bytes 1769480 | tf_op jit(solution)/shard_map/ppermute | solution.py:224
  100.9 6.2 %all-to-all-done.1 = f32[32,8,12]{2,1,0:T(8,128)S(1)} async-done(((f32[32,8,12]{2,1,0:T(8,128)}), f32[32,8,12]{2,1,0:T(8,128)S(1)}, u32[]{:S(2)}, u32[]{:S(2)}) %all-to-all-start.1) | async-done | bytes 12320 | tf_op jit(solution)/shard_map/all_to_all | solution.py:230
  107.2 0.1 copy.23
  107.3 0.0 collective-permute-done.12
  107.3 0.0 collective-permute-done.10
  107.3 0.1 fusion.9
  107.4 4.3 %collective-permute-start.13 = (bf16[2,32,768]{2,1,0:T(8,128)(2,1)S(1)}, bf16[2,32,768]{2,1,0:T(8,128)(2,1)S(1)}, u32[]{:S(2)}, u32[]{:S(2)}) collective-permute-start(bf16[2,32,768]{2,1,0:T(8,128)(2,1)S(1)} %get-tuple-element.53), channel_id=1, source_target_pairs={{0,4},{4,0},{1,5},{5,1},{2,6},{6,2},{3,7},{7,3},{8,12},{12,8},{9,1... | collective-permute-start | bytes 294920 | tf_op jit(solution)/shard_map/ppermute | solution.py:224
  111.7 0.7 copy.21
  112.4 0.2 collective-permute-done.13
  112.6 0.7 maximum_select_fusion
  113.3 0.0 collective-permute-done.9
  113.3 0.9 bitcast_dynamic-update-slice_fusion
  (22 shorter events, 0.3 us)
Async XLA Ops:
  1.6 11.8 %collective-permute-start = (bf16[4,32,768]{2,1,0:T(8,128)(2,1)S(1)}, bf16[4,32,768]{2,1,0:T(8,128)(2,1)S(1)}, u32[]{:S(2)}, u32[]{:S(2)}) collective-permute-start(bf16[4,32,768]{2,1,0:T(8,128)(2,1)S(1)} %fusion.8), channel_id=1, source_target_pairs={{0,4},{4,0},{1,5},{5,1},{2,6},{6,2},{3,7},{7,3},{8,12},{12,8},{9,1... | collective-permute-start | bytes 589832 | tf_op jit(solution)/shard_map/ppermute | solution.py:224
  12.4 1.0 copy-start.4
  15.1 14.9 %copy-start = (bf16[1,3,128,1536]{3,2,1,0:T(8,128)(2,1)S(1)}, bf16[1,3,128,1536]{3,2,1,0:T(8,128)(2,1)}, u32[]{:S(2)}) copy-start(bf16[1,3,128,1536]{3,2,1,0:T(8,128)(2,1)} %mine) | copy-start | bytes 3538948
  15.1 18.7 %copy-start.6 = (s32[1,1,2]{2,1,0:T(1,128)S(1)}, s32[1,1,2]{2,1,0:T(1,128)}, u32[]{:S(2)}) copy-start(s32[1,1,2]{2,1,0:T(1,128)} %param.13) | copy-start | bytes 28
  15.1 23.0 %copy-start.1 = (bf16[1,3,128,1536]{3,2,1,0:T(8,128)(2,1)S(1)}, bf16[1,3,128,1536]{3,2,1,0:T(8,128)(2,1)}, u32[]{:S(2)}) copy-start(bf16[1,3,128,1536]{3,2,1,0:T(8,128)(2,1)} %mine.1) | copy-start | bytes 3538948
  15.2 14.8 %collective-permute-start.2 = (bf16[2,2,32,768]{3,2,1,0:T(8,128)(2,1)S(1)}, bf16[2,2,32,768]{3,2,1,0:T(8,128)(2,1)S(1)}, u32[]{:S(2)}, u32[]{:S(2)}) collective-permute-start(bf16[2,2,32,768]{3,2,1,0:T(8,128)(2,1)S(1)} %pad_maximum_fusion.refs_0_), channel_id=1, source_target_pairs={{0,8},{8,0},{1,9},{9,1},{2,10},{10,2},{3,11},{11,3},{4,12},{12,4},... | collective-permute-start | bytes 589832 | tf_op jit(solution)/shard_map/ppermute | solution.py:224
  20.6 9.4 %collective-permute-start.1 = (bf16[4,32,768]{2,1,0:T(8,128)(2,1)S(1)}, bf16[4,32,768]{2,1,0:T(8,128)(2,1)S(1)}, u32[]{:S(2)}, u32[]{:S(2)}) collective-permute-start(bf16[4,32,768]{2,1,0:T(8,128)(2,1)S(1)} %broadcast_select_fusion.1), channel_id=1, source_target_pairs={{0,16},{4,20},{16,32},{20,36},{24,8},{28,12},{32,48},{36,52},{40,2... | collective-permute-start | bytes 589832 | tf_op jit(solution)/shard_map/ppermute | solution.py:277
  23.8 21.1 %collective-permute-start.6 = (bf16[4,32,768]{2,1,0:T(8,128)(2,1)}, bf16[4,32,768]{2,1,0:T(8,128)(2,1)S(1)}, u32[]{:S(2)}, u32[]{:S(2)}) collective-permute-start(bf16[4,32,768]{2,1,0:T(8,128)(2,1)} %get-tuple-element.50), channel_id=1, source_target_pairs={{16,0},{20,4},{32,16},{36,20},{8,24},{12,28},{48,32},{52,36},{24,4... | collective-permute-start | bytes 589832 | tf_op jit(solution)/shard_map/ppermute | solution.py:278
  25.1 16.5 %collective-permute-start.4 = (bf16[2,2,32,768]{3,2,1,0:T(8,128)(2,1)S(1)}, bf16[2,2,32,768]{3,2,1,0:T(8,128)(2,1)S(1)}, u32[]{:S(2)}, u32[]{:S(2)}) collective-permute-start(bf16[2,2,32,768]{3,2,1,0:T(8,128)(2,1)S(1)} %pad_maximum_fusion.1.refs_0_), channel_id=1, source_target_pairs={{0,8},{8,0},{1,9},{9,1},{2,10},{10,2},{3,11},{11,3},{4,12},{12,4},... | collective-permute-start | bytes 589832 | tf_op jit(solution)/shard_map/ppermute | solution.py:224
  30.8 14.1 %collective-permute-start.7 = (bf16[3,128,768]{2,1,0:T(8,128)(2,1)}, bf16[3,128,768]{2,1,0:T(8,128)(2,1)}, u32[]{:S(2)}, u32[]{:S(2)}) collective-permute-start(bf16[3,128,768]{2,1,0:T(8,128)(2,1)} %dynamic-slice_bitcast_fusion), channel_id=1, source_target_pairs={{0,4},{4,0},{1,5},{5,1},{2,6},{6,2},{3,7},{7,3},{8,12},{12,8},{9,1... | collective-permute-start | bytes 1769480 | tf_op jit(solution)/shard_map/ppermute | solution.py:224
  35.7 9.3 %collective-permute-start.8 = (bf16[2,2,32,768]{3,2,1,0:T(8,128)(2,1)S(1)}, bf16[2,2,32,768]{3,2,1,0:T(8,128)(2,1)}, u32[]{:S(2)}, u32[]{:S(2)}) collective-permute-start(bf16[2,2,32,768]{3,2,1,0:T(8,128)(2,1)S(1)} %collective-permute-done.2.refs_1_), channel_id=1, source_target_pairs={{0,16},{4,20},{16,32},{20,36},{24,8},{28,12},{32,48},{36,52},{40,2... | collective-permute-start | bytes 589832 | tf_op jit(solution)/shard_map/ppermute | solution.py:282
  39.0 9.6 %collective-permute-start.3 = (bf16[3,128,768]{2,1,0:T(8,128)(2,1)}, bf16[3,128,768]{2,1,0:T(8,128)(2,1)}, u32[]{:S(2)}, u32[]{:S(2)}) collective-permute-start(bf16[3,128,768]{2,1,0:T(8,128)(2,1)} %dynamic-slice_bitcast_fusion.1), channel_id=1, source_target_pairs={{0,4},{4,0},{1,5},{5,1},{2,6},{6,2},{3,7},{7,3},{8,12},{12,8},{9,1... | collective-permute-start | bytes 1769480 | tf_op jit(solution)/shard_map/ppermute | solution.py:224
  41.6 7.0 %collective-permute-start.5 = (bf16[2,2,32,768]{3,2,1,0:T(8,128)(2,1)S(1)}, bf16[2,2,32,768]{3,2,1,0:T(8,128)(2,1)}, u32[]{:S(2)}, u32[]{:S(2)}) collective-permute-start(bf16[2,2,32,768]{3,2,1,0:T(8,128)(2,1)S(1)} %collective-permute-done.4.refs_1_), channel_id=1, source_target_pairs={{0,16},{4,20},{16,32},{20,36},{24,8},{28,12},{32,48},{36,52},{40,2... | collective-permute-start | bytes 589832 | tf_op jit(solution)/shard_map/ppermute | solution.py:282
  48.6 9.8 %copy-start.5 = (pred[8]{0:T(512)(128)(4,1)S(1)}, pred[8]{0:T(512)(128)(4,1)}, u32[]{:S(2)}) copy-start(pred[8]{0:T(512)(128)(4,1)} %copy-done.4) | copy-start | bytes 28
  55.9 0.8 copy-start.2
  56.7 23.7 %collective-permute-start.11 = (bf16[3,2,32,768]{3,2,1,0:T(8,128)(2,1)}, bf16[3,2,32,768]{3,2,1,0:T(8,128)(2,1)S(1)}, u32[]{:S(2)}, u32[]{:S(2)}) collective-permute-start(bf16[3,2,32,768]{3,2,1,0:T(8,128)(2,1)} %get-tuple-element.32), channel_id=1, source_target_pairs={{16,0},{20,4},{32,16},{36,20},{8,24},{12,28},{48,32},{52,36},{24,4... | collective-permute-start | bytes 884744 | tf_op jit(solution)/shard_map/ppermute | solution.py:330
  80.4 17.4 %copy-start.3 = (bf16[3,128,768]{2,1,0:T(8,128)(2,1)S(1)}, bf16[3,128,768]{2,1,0:T(8,128)(2,1)}, u32[]{:S(2)}) copy-start(bf16[3,128,768]{2,1,0:T(8,128)(2,1)} %copy-done.2) | copy-start | bytes 1769476
  80.6 26.7 %collective-permute-start.12 = (bf16[2,2,32,768]{3,2,1,0:T(8,128)(2,1)S(1)}, bf16[2,2,32,768]{3,2,1,0:T(8,128)(2,1)S(1)}, u32[]{:S(2)}, u32[]{:S(2)}) collective-permute-start(bf16[2,2,32,768]{3,2,1,0:T(8,128)(2,1)S(1)} %fusion), channel_id=1, source_target_pairs={{0,8},{8,0},{1,9},{9,1},{2,10},{10,2},{3,11},{11,3},{4,12},{12,4},... | collective-permute-start | bytes 589832 | tf_op jit(solution)/shard_map/ppermute | solution.py:224
  83.0 24.3 %collective-permute-start.10 = (bf16[2,32,768]{2,1,0:T(8,128)(2,1)S(1)}, bf16[2,32,768]{2,1,0:T(8,128)(2,1)S(1)}, u32[]{:S(2)}, u32[]{:S(2)}) collective-permute-start(bf16[2,32,768]{2,1,0:T(8,128)(2,1)S(1)} %bitcast.59), channel_id=1, source_target_pairs={{0,16},{4,20},{16,32},{20,36},{24,8},{28,12},{32,48},{36,52},{40,2... | collective-permute-start | bytes 294920 | tf_op jit(solution)/shard_map/ppermute | solution.py:333
  87.1 20.0 %all-to-all-start.1 = ((f32[32,8,12]{2,1,0:T(8,128)}), f32[32,8,12]{2,1,0:T(8,128)S(1)}, u32[]{:S(2)}, u32[]{:S(2)}) async-start(f32[32,8,12]{2,1,0:T(8,128)} %broadcast_in_dim.61), calls=%async_computation.1 | async-start | bytes 262144 | tf_op jit(solution)/shard_map/all_to_all | solution.py:230
  97.7 15.6 %collective-permute-start.9 = (bf16[3,128,768]{2,1,0:T(8,128)(2,1)S(1)}, bf16[3,128,768]{2,1,0:T(8,128)(2,1)S(1)}, u32[]{:S(2)}, u32[]{:S(2)}) collective-permute-start(bf16[3,128,768]{2,1,0:T(8,128)(2,1)S(1)} %copy-done.3), channel_id=1, source_target_pairs={{0,4},{4,0},{1,5},{5,1},{2,6},{6,2},{3,7},{7,3},{8,12},{12,8},{9,1... | collective-permute-start | bytes 1769480 | tf_op jit(solution)/shard_map/ppermute | solution.py:224
  107.4 5.2 %collective-permute-start.13 = (bf16[2,32,768]{2,1,0:T(8,128)(2,1)S(1)}, bf16[2,32,768]{2,1,0:T(8,128)(2,1)S(1)}, u32[]{:S(2)}, u32[]{:S(2)}) collective-permute-start(bf16[2,32,768]{2,1,0:T(8,128)(2,1)S(1)} %get-tuple-element.53), channel_id=1, source_target_pairs={{0,4},{4,0},{1,5},{5,1},{2,6},{6,2},{3,7},{7,3},{8,12},{12,8},{9,1... | collective-permute-start | bytes 294920 | tf_op jit(solution)/shard_map/ppermute | solution.py:224
